TPU v7x, 512 devices: a whole 4x8x8 slice. The times are simulated.
512 devices in a mesh: corpus: 64 (over z, y_lo, core), tensor: 8 (over y_hi, x).
Axes of the slice: x: 4, y: 8 (y_hi: 2, y_lo: 4; y = y_hi * 4 + y_lo), z: 8, core: 2. Of those that a mesh axis runs over, the one named last changes fastest.
Arguments:
- query_rows: bfloat16 [64, 8, 4096], P('corpus', None, 'tensor'), may hold values from -6 to 6
- corpus_rows: bfloat16 [512, 24, 4096], P('corpus', None, 'tensor'), may hold values from -6 to 6
- passage_length: int32 [512], replicated, may hold values from 1 to 24, 6144 in all
- candidate_owner: int32 [64, 8], P('corpus'), may hold values from 0 to 63, all different within a row
- candidate_slot: int32 [64, 8], P('corpus'), may hold values from 0 to 7
- norm_gain: bfloat16 [4096], P('tensor'), may hold values from 0.099609375 to 1.8984375
- project_weight: bfloat16 [4096, 3, 2048], P('corpus', None, 'tensor'), may hold values from -3 to 3
- output_weight: bfloat16 [2048, 4096], P('tensor', 'corpus'), may hold values from -0.375 to 0.375
Outputs:
- layer_output: bfloat16 [16384, 4096], P('corpus', 'tensor')
Inputs may be any that keep to these rules, and one draw needn't show every extreme that they name: `candidate_owner`: the 8 candidates of a group lie on 8 different owner shards.
All inputs are finite; a program needn't handle non-finite values.
Results may differ from a plain program's by a relative error of at most 0.018.
The roundings to bfloat16 on the way count: a program that leaves them out, or rounds other values in their place, can miss the bound.
Values may be sent and summed in bfloat16 or wider, within the bound.
No kernel may reach another device: no remote copies, remote signals or barrier semaphores. Data moves between devices by JAX's collectives and lax.ppermute only.
A program may use at most 64 MiB of HBM per device.

v0:
```python
import jax
import jax.numpy as jnp
from jax import lax
from jax.sharding import PartitionSpec as P

HEAD_DIM = 128


def rotate_pairs(inputs, seq_len):
    half_size = inputs.shape[-1] // 2
    frequency = jnp.power(
        10000.0, -2.0 * jnp.arange(half_size, dtype=jnp.float32) / inputs.shape[-1]
    )
    position = (jnp.arange(inputs.shape[0], dtype=jnp.int32) % seq_len).astype(jnp.float32)
    angles = position[:, None] * frequency[None, :]
    cosine_table = jnp.cos(angles)[:, None, :]
    sine_table = jnp.sin(angles)[:, None, :]
    first_part = inputs[..., :half_size]
    second_part = inputs[..., half_size:]
    return jnp.concatenate(
        [
            first_part * cosine_table - second_part * sine_table,
            second_part * cosine_table + first_part * sine_table,
        ],
        axis=-1,
    )


def attend(queries, keys, values, pair_count, seq_len, query_len):
    pair_total = pair_count.shape[0]
    head_count = queries.shape[1]
    head_dim = queries.shape[2]
    shape_four = (pair_total, seq_len, head_count, head_dim)
    scores = jnp.einsum(
        "pqhd,pkhd->phqk",
        queries.reshape(shape_four),
        keys.reshape(shape_four),
        preferred_element_type=jnp.float32,
    ) * (1.0 / float(head_dim) ** 0.5)
    slots = jnp.arange(seq_len, dtype=jnp.int32)
    allowed = (slots[None, :] <= slots[:, None])[None, None] & (
        slots[None, None, None, :] < query_len + pair_count[:, None, None, None]
    )
    scores = jnp.where(allowed, scores, -1e30)
    row_max = jnp.max(scores, axis=-1, keepdims=True)
    exponent = jnp.exp(scores - row_max)
    row_total = jnp.sum(exponent, axis=-1, keepdims=True)
    attention_weights = (exponent / row_total).astype(jnp.bfloat16)
    attended = jnp.einsum(
        "phqk,pkhd->pqhd",
        attention_weights,
        values.reshape(shape_four),
        preferred_element_type=jnp.float32,
    )
    return attended.astype(jnp.bfloat16).reshape(pair_total * seq_len, head_count * head_dim)


def on_device(
    query_rows,
    corpus_rows,
    passage_length,
    candidate_owner,
    candidate_slot,
    norm_gain,
    project_weight,
    output_weight,
):
    owner_index = lax.axis_index("corpus")
    stored = corpus_rows.shape[0]
    passage_rows = corpus_rows.shape[1]
    features = corpus_rows.shape[2]
    tensor_count = lax.axis_size("tensor")
    every_owner, every_slot = (
        lax.all_gather(candidate_owner, "corpus", axis=0, tiled=True),
        lax.all_gather(candidate_slot, "corpus", axis=0, tiled=True),
    )
    asked_here = every_owner == owner_index
    wanted = jnp.sum(jnp.where(asked_here, every_slot, 0), axis=1)
    present = jnp.any(asked_here, axis=1)
    chosen = jnp.take(corpus_rows, wanted, axis=0)
    counts = jnp.take(passage_length, owner_index * stored + wanted, axis=0)
    live_rows = (jnp.arange(passage_rows, dtype=jnp.int32)[None, :] < counts[:, None]) & present[
        :, None
    ]
    outgoing = jnp.where(live_rows[:, :, None], chosen, jnp.zeros((), chosen.dtype))
    arrived = lax.all_to_all(outgoing, "corpus", split_axis=0, concat_axis=0, tiled=True)
    own_owner = candidate_owner[0]
    pair_total = own_owner.shape[0]
    passages = jnp.take(arrived, own_owner, axis=0)
    query_len = query_rows.shape[1]
    seq_len = query_len + passage_rows
    row_count = pair_total * seq_len
    query_copy = jnp.broadcast_to(query_rows[0][None], (pair_total, query_len, features))
    packed = jnp.concatenate([query_copy, passages], axis=1).reshape(row_count, features)
    pair_count = jnp.take(passage_length, own_owner * stored + candidate_slot[0], axis=0)
    widened = packed.astype(jnp.float32)
    squares = lax.psum(jnp.sum(widened * widened, axis=1), "tensor")
    inverse_rms = lax.rsqrt(squares / (features * tensor_count) + 1e-05)
    local_normed = (widened * inverse_rms[:, None] * norm_gain.astype(jnp.float32)[None, :]).astype(
        jnp.bfloat16
    )
    normed = lax.all_gather(local_normed, "tensor", axis=1, tiled=True)
    local_width = project_weight.shape[2]
    heads_here = local_width // HEAD_DIM
    piece = lax.all_gather(project_weight, "corpus", axis=0, tiled=True)
    flat_piece = piece.reshape(piece.shape[0], 3 * local_width)
    projected = jnp.dot(normed, flat_piece, preferred_element_type=jnp.float32)
    projected = projected.reshape(row_count, 3, heads_here, HEAD_DIM)
    queries = rotate_pairs(projected[:, 0], seq_len).astype(jnp.bfloat16)
    keys = rotate_pairs(projected[:, 1], seq_len).astype(jnp.bfloat16)
    values = projected[:, 2].astype(jnp.bfloat16)
    attended = attend(queries, keys, values, pair_count, seq_len, query_len)
    partial_value = jnp.dot(
        attended,
        lax.all_gather(output_weight, "corpus", axis=1, tiled=True),
        preferred_element_type=jnp.float32,
    )
    own_share = lax.psum_scatter(
        partial_value.astype(jnp.bfloat16), "tensor", scatter_dimension=1, tiled=True
    ).astype(jnp.float32)
    return (widened + own_share).astype(jnp.bfloat16)


def solution(mesh):
    placed = (
        P("corpus", None, "tensor"),
        P("corpus", None, "tensor"),
        P(),
        P("corpus", None),
        P("corpus", None),
        P("tensor"),
        P("corpus", None, "tensor"),
        P("tensor", "corpus"),
    )
    return jax.shard_map(
        on_device, mesh=mesh, in_specs=placed, out_specs=P("corpus", "tensor"), check_vma=False
    )
```

profile of v0, /device:TPU:1, one launch (start us, length us, event | category | flops | bytes accessed | tf_op | source)
XLA Modules:
  0.0 548.8 jit_solution(13920632422575181263)
XLA Ops:
  6.5 0.7 all-gather.8.cloned.1.call-update
  7.3 86.9 %all-gather = s32[64,1,8]{2,1,0:T(1,128)S(1)} all-gather(s32[1,1,8]{2,1,0:T(1,128)} %bitcast.86), channel_id=1, replica_groups=mesh['corpus'=64,'tensor'=8] {'corpus'}, dimensions={0}, use_global_device_ids=true | all-gather | bytes 2080 | tf_op jit(solution)/shard_map/all_gather | solution.py:74
  94.1 73.7 %all-gather.1 = s32[64,1,8]{2,1,0:T(1,128)S(1)} all-gather(s32[1,1,8]{2,1,0:T(1,128)} %bitcast.85), channel_id=1, replica_groups=mesh['corpus'=64,'tensor'=8] {'corpus'}, dimensions={0}, use_global_device_ids=true | all-gather | bytes 2080 | tf_op jit(solution)/shard_map/all_gather | solution.py:75
  167.8 1.3 fusion.17
  169.1 1.5 gather_fusion
  170.6 0.7 gather_fusion.1
  171.3 1.2 compare_reduce_fusion
  172.6 1.4 select_select_fusion
  174.0 4.5 all-to-all-start
  178.6 38.8 %all-to-all-done = bf16[64,24,512]{2,1,0:T(8,128)(2,1)S(1)} async-done(((bf16[64,24,512]{2,1,0:T(8,128)(2,1)}), bf16[64,24,512]{2,1,0:T(8,128)(2,1)S(1)}, u32[]{:S(2)}, u32[]{:S(2)}) %all-to-all-start) | async-done | bytes 1572896 | tf_op jit(solution)/shard_map/all_to_all | solution.py:86
  217.4 0.6 gather_fusion.2
  218.3 25.3 %psum.7 = f32[256]{0:T(256)S(1)} all-reduce(f32[256]{0:T(256)S(1)} %reduce_sum.34), channel_id=1, replica_groups=mesh['corpus'=64,'tensor'=8] {'tensor'}, use_global_device_ids=true, to_apply=%region_3.4 | all-reduce | flops 256 | bytes 2048 | tf_op jit(solution)/shard_map/psum | solution.py:97
  243.7 0.8 fusion.9
  244.6 0.7 all-gather.10.cloned.1.call-update
  245.3 0.6 gather_fusion.3
  246.2 0.3 multiply_cosine_fusion
  246.5 8.7 %copy.28 = bf16[4096,3,256]{0,2,1:T(8,128)(2,1)} copy(bf16[4096,3,256]{2,0,1:T(8,128)(2,1)} %all-gather.8.cloned.1.call-done) | data formatting | bytes 12582912 | tf_op jit(solution)/shard_map/all_gather | solution.py:105
  255.3 66.1 %all-gather.6.cloned.1.call-done = bf16[256,4096]{1,0:T(8,128)(2,1)} async-done(((bf16[256,512]{1,0:T(8,128)(2,1)}), bf16[256,4096]{1,0:T(8,128)(2,1)}) %all-gather.6.cloned.1.call-update) | async-done | bytes 2097168 | tf_op jit(solution)/shard_map/all_gather | solution.py:102
  321.4 5.2 fusion.1
  327.4 0.3 fusion.4
  328.1 112.1 %all-gather.10.cloned.1.call-done = bf16[256,4096]{0,1:T(8,128)(2,1)} async-done(((bf16[256,64]{0,1:T(8,128)(2,1)}), bf16[256,4096]{0,1:T(8,128)(2,1)}) %all-gather.10.cloned.1.call-update) | async-done | bytes 2097168 | tf_op jit(solution)/shard_map/all_gather | solution.py:115
  440.3 3.7 convolution_convert_fusion
  444.0 96.6 %reduce-scatter.2.cloned.1.call-done = bf16[256,512]{1,0:T(8,128)(2,1)} async-done(((bf16[256,4096]{1,0:T(8,128)(2,1)}), bf16[256,512]{1,0:T(8,128)(2,1)}) %reduce-scatter.2.cloned.1.call-update) | async-done | bytes 262160 | tf_op jit(solution)/shard_map/reduce_scatter | solution.py:118
  540.6 1.7 fusion.10
  (51 shorter events, 2.1 us)
Async XLA Ops:
  6.5 164.1 %copy-start = (bf16[8,24,512]{2,1,0:T(8,128)(2,1)S(1)}, bf16[8,24,512]{2,1,0:T(8,128)(2,1)}, u32[]{:S(2)}) copy-start(bf16[8,24,512]{2,1,0:T(8,128)(2,1)} %param.9) | copy-start | bytes 589828
  6.5 240.0 %all-gather.8.cloned.1.call-start = ((), (), s32[]{:S(2)}) async-start(), calls=%async_computation.3 | async-start | bytes 6389760 | tf_op jit(solution)/shard_map/all_gather | solution.py:105
  174.0 4.5 copy-start.5
  174.0 4.6 copy-start.3
  174.0 4.6 copy-start.4
  174.0 44.0 %copy-start.2 = (bf16[1,8,512]{2,1,0:T(8,128)(2,1)S(1)}, bf16[1,8,512]{2,1,0:T(8,128)(2,1)}, u32[]{:S(2)}) copy-start(bf16[1,8,512]{2,1,0:T(8,128)(2,1)} %param.8) | copy-start | bytes 24580
  174.0 71.3 %copy-start.1 = (s32[512]{0:T(512)S(1)}, s32[512]{0:T(512)}, u32[]{:S(2)}) copy-start(s32[512]{0:T(512)} %param.10) | copy-start | bytes 6148
  174.0 43.4 %all-to-all-start = ((bf16[64,24,512]{2,1,0:T(8,128)(2,1)}), bf16[64,24,512]{2,1,0:T(8,128)(2,1)S(1)}, u32[]{:S(2)}, u32[]{:S(2)}) async-start(bf16[64,24,512]{2,1,0:T(8,128)(2,1)} %select_select_fusion), calls=%async_computation | async-start | bytes 3145728 | tf_op jit(solution)/shard_map/all_to_all | solution.py:86
  178.5 142.9 %all-gather.6.cloned.1.call-start = ((), (), s32[]{:S(2)}) async-start(), calls=%async_computation.2 | async-start | bytes 2359296 | tf_op jit(solution)/shard_map/all_gather | solution.py:102
  244.5 195.7 %all-gather.10.cloned.1.call-start = ((), (), s32[]{:S(2)}) async-start(), calls=%async_computation.4 | async-start | bytes 2129920 | tf_op jit(solution)/shard_map/all_gather | solution.py:115
  245.3 295.3 %reduce-scatter.2.cloned.1.call-start = ((), (), s32[]{:S(2)}) async-start(), calls=%async_computation.5 | async-start | bytes 2359296 | tf_op jit(solution)/shard_map/reduce_scatter | solution.py:118
Sparse Core Ops, SparseCore 0:
  9.5 127.3 all-gather.7
  244.6 76.6 all-gather.5
  323.5 116.6 all-gather.9
  444.8 95.7 reduce-scatter.1
where the time goes:
time: 550 us; the launch traced here: 549 us
  waiting for transfers between devices  315 us (57%)
  blocking collectives  186 us (34%)
  between operations  13.4 us (2%)
  local copies, waits for them, and re-layouts  12.9 us (2%)
  matrix products  9.45 us (2%)
  other arithmetic  7.48 us (1%)
    all_gather x1, waiting for transfers between devices, on_device(): lax.all_gather(output_weight, 'corpus', axis=1, tiled=True)  112 us
    reduce_scatter x1, waiting for transfers between devices, on_device(): lax.psum_scatter(partial_value.astype(jnp.bfloat16), 'tensor', scatter_di...  96.6 us
    all_gather x1, blocking collectives, on_device(): lax.all_gather(candidate_owner, 'corpus', axis=0, tiled=True)  86.9 us
    all_gather x1, blocking collectives, on_device(): lax.all_gather(candidate_slot, 'corpus', axis=0, tiled=True)  73.7 us
    all_gather x1, waiting for transfers between devices, on_device(): normed = lax.all_gather(local_normed, 'tensor', axis=1, tiled=True)  66.1 us
    all_to_all x1, waiting for transfers between devices, on_device(): lax.all_to_all(outgoing, 'corpus', split_axis=0, concat_axis=0, tiled=True)  38.8 us
    psum x1, blocking collectives, on_device(): squares = lax.psum(jnp.sum(widened * widened, axis=1), 'tensor')  25.3 us
  transfers between devices with their start and end apart: 5, of which 4 were waited for; matrix products, arithmetic and copies ran while one was open for 4% of the time, Pallas kernels for 0%

commit v1 on v0

v1 whole, which is shorter than its diff:
```python
import jax
import jax.numpy as jnp
from jax import lax
from jax.sharding import Mesh, PartitionSpec as P

HEAD_DIM = 128
SPLIT = (("z", 8), ("y", 4), ("c", 2), ("h", 2), ("x", 4))
AXES = tuple(name for name, _ in SPLIT)
CORPUS = ("z", "y", "c")
TENSOR = ("h", "x")


def rotation_tables(position):
    half = HEAD_DIM // 2
    frequency = jnp.power(10000.0, -2.0 * jnp.arange(half, dtype=jnp.float32) / HEAD_DIM)
    angles = position.astype(jnp.float32)[:, None] * frequency[None, :]
    return jnp.cos(angles), jnp.sin(angles)


def rotate(inputs, cosine, sine):
    half = HEAD_DIM // 2
    first, second = inputs[:, :half], inputs[:, half:]
    return jnp.concatenate(
        [first * cosine - second * sine, second * cosine + first * sine], axis=-1
    ).astype(jnp.bfloat16)


def on_device(
    query_rows,
    corpus_rows,
    passage_length,
    candidate_owner,
    candidate_slot,
    norm_gain,
    project_weight,
    output_weight,
):
    bf16, f32, i32 = jnp.bfloat16, jnp.float32, jnp.int32
    sizes = dict(SPLIT)
    shards = sizes["z"] * sizes["y"] * sizes["c"]
    plane = sizes["y"] * sizes["c"]
    tensors = sizes["h"] * sizes["x"]
    core = lax.axis_index("c")
    stored, passage_rows, features = corpus_rows.shape
    query_len = query_rows.shape[1]
    pairs = candidate_owner.shape[1]
    rows = query_len + pairs * passage_rows
    depth = project_weight.shape[0]

    own_owner, own_slot = candidate_owner[0], candidate_slot[0]
    asks = jnp.arange(shards, dtype=i32)[:, None] == own_owner[None, :]
    request = jnp.sum(jnp.where(asks, own_slot[None, :] + 1, 0), axis=1)
    request = jnp.broadcast_to(request[:, None], (shards, 128))
    asked = lax.all_to_all(request, CORPUS, split_axis=0, concat_axis=0, tiled=True)
    wanted = jnp.clip(asked[:, 0] - 1, 0, stored - 1)

    wide = project_weight.reshape(depth, 3, 2, HEAD_DIM).transpose(2, 0, 1, 3)
    wide = wide.reshape(2, depth, 3 * HEAD_DIM)
    wide = jnp.broadcast_to(wide[None], (sizes["y"], 2, depth, 3 * HEAD_DIM))
    wide = wide.reshape(plane, depth, 3 * HEAD_DIM)
    wide = lax.all_to_all(wide, ("y", "c"), split_axis=0, concat_axis=0, tiled=True)
    wide = wide.reshape(plane * depth, 3 * HEAD_DIM)
    wide_own = lax.all_gather(wide, "z", axis=0, tiled=True)
    swap_core = [(0, 1), (1, 0)]
    wide_other = lax.ppermute(wide_own, "c", swap_core)

    cells = [(z, q, t) for z in range(sizes["z"]) for q in range(plane) for t in range(tensors)]
    number = {cell: i for i, cell in enumerate(cells)}
    turn = [(number[(z, q, t)], number[(t, q, z)]) for z, q, t in cells]
    narrow = lax.ppermute(output_weight.T, AXES, turn)
    narrow = narrow.reshape(depth, 2, HEAD_DIM).transpose(1, 0, 2)
    narrow = jnp.broadcast_to(narrow[None], (sizes["y"], 2, depth, HEAD_DIM))
    narrow = narrow.reshape(plane, depth, HEAD_DIM)
    narrow = lax.all_to_all(narrow, ("y", "c"), split_axis=0, concat_axis=0, tiled=True)
    narrow = narrow.reshape(1, plane * depth, HEAD_DIM)
    narrow_own = lax.all_gather(narrow, "z", axis=0, tiled=True)
    narrow_other = lax.ppermute(narrow_own, "c", swap_core)

    outgoing = jnp.take(corpus_rows, wanted, axis=0, mode="clip")
    arrived = lax.all_to_all(outgoing, CORPUS, split_axis=0, concat_axis=0, tiled=True)
    counts = jnp.take(passage_length, own_owner * stored + own_slot, axis=0, mode="clip")
    passages = jnp.take(arrived, own_owner, axis=0, mode="clip")
    inside = jnp.arange(passage_rows, dtype=i32)[None, :] < counts[:, None]
    passages = jnp.where(inside[:, :, None], passages, jnp.zeros((), bf16))
    packed = jnp.concatenate([query_rows[0], passages.reshape(-1, features)], axis=0)

    far = lax.ppermute(packed, "h", [(0, 1), (1, 0)])
    low = lax.axis_index("h") == 0
    both = jnp.stack([jnp.where(low, packed, far), jnp.where(low, far, packed)])
    spread = jnp.broadcast_to(both[None], (sizes["x"],) + both.shape)
    full = lax.all_to_all(spread, "x", split_axis=0, concat_axis=0, tiled=True)
    full = full.transpose(2, 1, 0, 3).reshape(rows, tensors * features)
    gain = lax.all_gather(norm_gain, TENSOR, axis=0, tiled=True)
    widened = full.astype(f32)
    mean = jnp.mean(widened * widened, axis=1, keepdims=True)
    normed = (widened * lax.rsqrt(mean + 1e-05) * gain.astype(f32)[None, :]).astype(bf16)

    row = jnp.arange(rows, dtype=i32)
    is_query = row < query_len
    place = (row - query_len) % passage_rows
    slot = jnp.where(is_query, row, query_len + place)
    pair = jnp.where(is_query, -1, (row - query_len) // passage_rows)
    count_of = jnp.concatenate(
        [jnp.full((query_len,), passage_rows, i32), jnp.repeat(counts, passage_rows)]
    )
    allowed = (slot[None, :] <= slot[:, None]) & (
        is_query[None, :]
        | ((pair[None, :] == pair[:, None]) & (slot < query_len + count_of)[None, :])
    )
    cosine, sine = rotation_tables(slot)

    def head(weight):
        projected = jnp.dot(normed, weight, preferred_element_type=f32)
        queries = rotate(projected[:, :HEAD_DIM], cosine, sine)
        keys = rotate(projected[:, HEAD_DIM : 2 * HEAD_DIM], cosine, sine)
        values = projected[:, 2 * HEAD_DIM :].astype(bf16)
        scores = lax.dot_general(
            queries, keys, (((1,), (1,)), ((), ())), preferred_element_type=f32
        ) * (1.0 / float(HEAD_DIM) ** 0.5)
        scores = jnp.where(allowed, scores, -1e30)
        exponent = jnp.exp(scores - jnp.max(scores, axis=-1, keepdims=True))
        weights = (exponent / jnp.sum(exponent, axis=-1, keepdims=True)).astype(bf16)
        return jnp.dot(weights, values, preferred_element_type=f32).astype(bf16)

    mine, theirs = head(wide_own), head(wide_other)
    first = core == 0
    attended = jnp.concatenate(
        [jnp.where(first, mine, theirs), jnp.where(first, theirs, mine)], axis=1
    )
    spread = jnp.broadcast_to(attended[None], (tensors,) + attended.shape)
    heads = lax.all_to_all(spread, TENSOR, split_axis=0, concat_axis=0, tiled=True)
    low_head, high_head = heads[:, :, :HEAD_DIM], heads[:, :, HEAD_DIM:]
    near_head = jnp.where(first, low_head, high_head)
    far_head = jnp.where(first, high_head, low_head)
    numbers = (((2,), (2,)), ((0,), (0,)))
    partial_value = lax.dot_general(
        near_head, narrow_own, numbers, preferred_element_type=f32
    ) + lax.dot_general(far_head, narrow_other, numbers, preferred_element_type=f32)
    summed = jnp.sum(partial_value.astype(bf16).astype(f32), axis=0)
    final = (packed.astype(f32) + summed).astype(bf16)
    query_out = jnp.broadcast_to(final[None, :query_len], (pairs, query_len, features))
    passage_out = final[query_len:].reshape(pairs, passage_rows, features)
    return jnp.concatenate([query_out, passage_out], axis=1).reshape(-1, features)


def solution(mesh):
    fine = Mesh(mesh.devices.reshape([size for _, size in SPLIT]), AXES)
    placed = (
        P(CORPUS, None, TENSOR),
        P(CORPUS, None, TENSOR),
        P(),
        P(CORPUS, None),
        P(CORPUS, None),
        P(TENSOR),
        P(CORPUS, None, TENSOR),
        P(TENSOR, CORPUS),
    )
    return jax.shard_map(
        on_device, mesh=fine, in_specs=placed, out_specs=P(CORPUS, TENSOR), check_vma=False
    )
```

time: 550 us -> 246 us (0.45)
  the two profiles are of different devices: /device:TPU:1 before, /device:TPU:8 now
where the time goes in v1:
time: 246 us; the launch traced here: 245 us
  blocking collectives  89.9 us (37%)
  waiting for transfers between devices  66.7 us (27%)
  starting transfers between devices  39.6 us (16%)
  local copies, waits for them, and re-layouts  16.6 us (7%)
  between operations  13.8 us (6%)
  matrix products  9.98 us (4%)
  other arithmetic  8.08 us (3%)
    all_gather x1, blocking collectives, on_device(): gain = lax.all_gather(norm_gain, TENSOR, axis=0, tiled=True)  51.9 us
    all_to_all x1, waiting for transfers between devices, on_device(): lax.all_to_all(outgoing, CORPUS, split_axis=0, concat_axis=0, tiled=True)  43.7 us
    all_to_all x1, blocking collectives, on_device(): lax.all_to_all(wide, ('y', 'c'), split_axis=0, concat_axis=0, tiled=True)  19.6 us
    all_to_all x1, blocking collectives, on_device(): lax.all_to_all(request, CORPUS, split_axis=0, concat_axis=0, tiled=True)  18.4 us
    all_to_all x1, starting transfers between devices, on_device(): full = lax.all_to_all(spread, 'x', split_axis=0, concat_axis=0, tiled=True)  11.3 us
    all_gather x1, waiting for transfers between devices, on_device(): narrow_own = lax.all_gather(narrow, 'z', axis=0, tiled=True)  9.42 us
    all_to_all x1, waiting for transfers between devices, on_device(): lax.all_to_all(spread, TENSOR, split_axis=0, concat_axis=0, tiled=True)  8.6 us
    convert_element_type x2, local copies, waits for them, and re-layouts, on_device(): widened = full.astype(f32)  7.85 us
  transfers between devices with their start and end apart: 10, of which 5 were waited for; matrix products, arithmetic and copies ran while one was open for 13% of the time, Pallas kernels for 0%

profile of v1, /device:TPU:8, one launch (start us, length us, event | category | flops | bytes accessed | tf_op | source)
XLA Modules:
  0.0 244.7 jit_solution(5958399169833023144)
XLA Ops:
  7.7 19.6 %all_to_all.34 = bf16[8,64,384]{2,1,0:T(8,128)(2,1)} all-to-all(bf16[8,64,384]{2,1,0:T(8,128)(2,1)S(1)} %bitcast.34), channel_id=1, replica_groups=mesh['z'=8,'y'=4,'c'=2,'h'=2,'x'=4] {'y','c'}, dimensions={0} | all-to-all | bytes 786432 | tf_op jit(solution)/shard_map/all_to_all | solution.py:61
  29.0 18.4 %all_to_all.35 = s32[64,1,128]{2,1,0:T(1,128)S(1)} all-to-all(s32[64,1,128]{2,1,0:T(1,128)S(1)} %broadcast_in_dim.59), channel_id=1, replica_groups=mesh['z'=8,'y'=4,'c'=2,'h'=2,'x'=4] {'z','y','c'}, dimensions={0} | all-to-all | bytes 65536 | tf_op jit(solution)/shard_map/all_to_all | solution.py:54
  47.5 1.8 gather_fusion.1
  49.3 5.5 %all-to-all-start.1 = ((bf16[64,24,512]{2,1,0:T(8,128)(2,1)}), bf16[64,24,512]{2,1,0:T(8,128)(2,1)S(1)}, u32[]{:S(2)}, u32[]{:S(2)}) async-start(bf16[64,24,512]{2,1,0:T(8,128)(2,1)} %gather_fusion.1), calls=%async_computation.1 | async-start | bytes 3145728 | tf_op jit(solution)/shard_map/all_to_all | solution.py:80
  55.8 43.7 %all-to-all-done.1 = bf16[64,24,512]{2,1,0:T(8,128)(2,1)S(1)} async-done(((bf16[64,24,512]{2,1,0:T(8,128)(2,1)}), bf16[64,24,512]{2,1,0:T(8,128)(2,1)S(1)}, u32[]{:S(2)}, u32[]{:S(2)}) %all-to-all-start.1) | async-done | bytes 1572896 | tf_op jit(solution)/shard_map/all_to_all | solution.py:80
  100.2 6.0 %collective-permute-start = (bf16[200,512]{1,0:T(8,128)(2,1)S(1)}, bf16[200,512]{1,0:T(8,128)(2,1)S(1)}, u32[]{:S(2)}, u32[]{:S(2)}) collective-permute-start(bf16[200,512]{1,0:T(8,128)(2,1)S(1)} %pad_maximum_fusion.2), channel_id=1, source_target_pairs={{0,4},{4,0},{1,5},{5,1},{2,6},{6,2},{3,7},{7,3},{8,12},{12,8},{9,1... | collective-permute-start | bytes 614408 | tf_op jit(solution)/shard_map/ppermute | solution.py:87
  107.7 5.0 %all-to-all-start.5 = ((bf16[8,64,128]{2,1,0:T(8,128)(2,1)}), bf16[8,64,128]{2,1,0:T(8,128)(2,1)S(1)}, u32[]{:S(2)}, u32[]{:S(2)}) async-start(bf16[8,64,128]{2,1,0:T(8,128)(2,1)} %bitcast.15), calls=%async_computation.5 | async-start | bytes 262144 | tf_op jit(solution)/shard_map/all_to_all | solution.py:74
  112.7 2.0 collective-permute-start.1
  115.3 4.8 %all-to-all-done.5 = bf16[8,64,128]{2,1,0:T(8,128)(2,1)S(1)} async-done(((bf16[8,64,128]{2,1,0:T(8,128)(2,1)}), bf16[8,64,128]{2,1,0:T(8,128)(2,1)S(1)}, u32[]{:S(2)}, u32[]{:S(2)}) %all-to-all-start.5) | async-done | bytes 131104 | tf_op jit(solution)/shard_map/all_to_all | solution.py:74
  120.2 2.0 broadcast_in_dim.62
  122.2 11.3 %all-to-all-start.2 = ((bf16[4,2,200,512]{3,1,2,0:T(2,128)(2,1)}), bf16[4,2,200,512]{3,1,2,0:T(2,128)(2,1)S(1)}, u32[]{:S(2)}, u32[]{:S(2)}) async-start(bf16[4,2,200,512]{3,1,2,0:T(2,128)(2,1)} %broadcast_in_dim.62), calls=%async_computation.2 | async-start | bytes 3276800 | tf_op jit(solution)/shard_map/all_to_all | solution.py:91
  133.5 51.9 %all-gather = bf16[8,1,512]{2,1,0:T(2,128)(2,1)S(1)} all-gather(bf16[1,1,512]{2,1,0:T(2,128)(2,1)S(1)} %reshape.192), channel_id=1, replica_groups=mesh['z'=8,'y'=4,'c'=2,'h'=2,'x'=4] {'h','x'}, dimensions={0}, use_global_device_ids=true | all-gather | bytes 9216 | tf_op jit(solution)/shard_map/all_gather | solution.py:93
  185.6 1.1 convert_bitcast_fusion
  186.8 3.8 %copy.22 = f32[200,2,4,512]{3,2,1,0:T(4,128)} copy(f32[200,2,4,512]{3,1,0,2:T(2,128)S(1)} %convert_bitcast_fusion) | data formatting | bytes 6553600 | tf_op jit(solution)/shard_map/convert_element_type | solution.py:94
  190.6 4.0 %reshape.162 = f32[200,4096]{1,0:T(8,128)S(1)} reshape(f32[200,2,4,512]{3,2,1,0:T(4,128)} %copy.22) | data formatting | bytes 6553600 | tf_op jit(solution)/shard_map/convert_element_type | solution.py:94
  194.6 3.6 %fusion = f32[200]{0:T(256)S(1)} fusion(bf16[4,2,200,512]{3,1,2,0:T(2,128)(2,1)} %copy-done.2), kind=kLoop, calls=%fused_computation.5 | loop fusion | flops 2457400 | bytes 1639200 | tf_op jit(solution)/shard_map/reduce_sum | solution.py:95
  198.2 3.0 %fusion.70 = f32[200,384]{1,0:T(8,128)S(1)} fusion(bf16[4096,384]{1,0:T(8,128)(2,1)} %all-gather.4.cloned.1.call-done, f32[200,4096]{1,0:T(8,128)S(1)} %reshape.162, f32[4096]{0:T(1024)S(1)} %bitcast.38, f32[200]{0:T(256)S(1)} %add_rsqrt_fusion), kind=kOutput, calls=%fused_computation.118 | convolution fusion | flops 631603200 | bytes 6746912 | tf_op jit(solution)/shard_map/dot_general | solution.py:113
  201.2 3.0 %fusion.69 = f32[200,384]{1,0:T(8,128)S(1)} fusion(bf16[4096,384]{1,0:T(8,128)(2,1)} %collective-permute-done.1, f32[200,4096]{1,0:T(8,128)S(1)} %reshape.162, f32[4096]{0:T(1024)S(1)} %bitcast.39, f32[200]{0:T(256)S(1)} %add_rsqrt_fusion), kind=kOutput, calls=%fused_computation.117 | convolution fusion | flops 631603200 | bytes 6746912 | tf_op jit(solution)/shard_map/dot_general | solution.py:113
  206.0 1.0 broadcast_in_dim.66
  207.0 7.2 %all-to-all-start.4 = ((bf16[8,200,256]{2,1,0:T(8,128)(2,1)}), bf16[8,200,256]{2,1,0:T(8,128)(2,1)S(1)}, u32[]{:S(2)}, u32[]{:S(2)}) async-start(bf16[8,200,256]{2,1,0:T(8,128)(2,1)} %broadcast_in_dim.66), calls=%async_computation.4 | async-start | bytes 1638400 | tf_op jit(solution)/shard_map/all_to_all | solution.py:131
  214.2 9.4 %all-gather.6.cloned.1.call-done = bf16[8,512,128]{2,1,0:T(8,128)(2,1)} async-done(((bf16[1,512,128]{2,1,0:T(8,128)(2,1)}), bf16[8,512,128]{2,1,0:T(8,128)(2,1)}) %all-gather.6.cloned.1.call-update) | async-done | bytes 1048592 | tf_op jit(solution)/shard_map/all_gather | solution.py:76
  223.6 1.9 collective-permute-start.3
  225.5 8.6 %all-to-all-done.4 = bf16[8,200,256]{2,1,0:T(8,128)(2,1)S(1)} async-done(((bf16[8,200,256]{2,1,0:T(8,128)(2,1)}), bf16[8,200,256]{2,1,0:T(8,128)(2,1)S(1)}, u32[]{:S(2)}, u32[]{:S(2)}) %all-to-all-start.4) | async-done | bytes 819232 | tf_op jit(solution)/shard_map/all_to_all | solution.py:131
  234.1 2.1 fusion.4
  (78 shorter events, 10.0 us)
Async XLA Ops:
  6.5 40.9 %copy-start = (bf16[8,24,512]{2,1,0:T(8,128)(2,1)S(1)}, bf16[8,24,512]{2,1,0:T(8,128)(2,1)}, u32[]{:S(2)}) copy-start(bf16[8,24,512]{2,1,0:T(8,128)(2,1)} %param.9) | copy-start | bytes 589828
  6.5 106.2 %all-gather.4.cloned.1.call-start = ((), (), s32[]{:S(2)}) async-start(), calls=%async_computation.6 | async-start | bytes 3538944 | tf_op jit(solution)/shard_map/all_gather | solution.py:63
  27.4 27.5 %copy-start.1 = (s32[512]{0:T(512)S(1)}, s32[512]{0:T(512)}, u32[]{:S(2)}) copy-start(s32[512]{0:T(512)} %param.10) | copy-start | bytes 6148
  47.5 8.3 %copy-start.7 = (s32[1,8]{1,0:T(1,128)S(1)}, s32[1,8]{1,0:T(1,128)}, u32[]{:S(2)}) copy-start(s32[1,8]{1,0:T(1,128)} %param.11) | copy-start | bytes 100
  47.5 52.7 %copy-start.6 = (bf16[1,8,512]{2,1,0:T(8,128)(2,1)S(1)}, bf16[1,8,512]{2,1,0:T(8,128)(2,1)}, u32[]{:S(2)}) copy-start(bf16[1,8,512]{2,1,0:T(8,128)(2,1)} %param.8) | copy-start | bytes 24580
  47.5 58.8 %copy-start.9 = (bf16[256,64]{0,1:T(8,128)(2,1)S(1)}, bf16[256,64]{0,1:T(8,128)(2,1)}, u32[]{:S(2)}) copy-start(bf16[256,64]{0,1:T(8,128)(2,1)} %param.15) | copy-start | bytes 98308
  49.3 50.2 %all-to-all-start.1 = ((bf16[64,24,512]{2,1,0:T(8,128)(2,1)}), bf16[64,24,512]{2,1,0:T(8,128)(2,1)S(1)}, u32[]{:S(2)}, u32[]{:S(2)}) async-start(bf16[64,24,512]{2,1,0:T(8,128)(2,1)} %gather_fusion.1), calls=%async_computation.1 | async-start | bytes 3145728 | tf_op jit(solution)/shard_map/all_to_all | solution.py:80
  100.2 22.0 %copy-start.3 = (bf16[192,512]{1,0:T(8,128)(2,1)}, bf16[192,512]{1,0:T(8,128)(2,1)S(1)}, u32[]{:S(2)}) copy-start(bf16[192,512]{1,0:T(8,128)(2,1)S(1)} %bitcast_select_fusion) | copy-start | bytes 589828
  100.2 14.6 %collective-permute-start = (bf16[200,512]{1,0:T(8,128)(2,1)S(1)}, bf16[200,512]{1,0:T(8,128)(2,1)S(1)}, u32[]{:S(2)}, u32[]{:S(2)}) collective-permute-start(bf16[200,512]{1,0:T(8,128)(2,1)S(1)} %pad_maximum_fusion.2), channel_id=1, source_target_pairs={{0,4},{4,0},{1,5},{5,1},{2,6},{6,2},{3,7},{7,3},{8,12},{12,8},{9,1... | collective-permute-start | bytes 614408 | tf_op jit(solution)/shard_map/ppermute | solution.py:87
  106.3 0.7 collective-permute-start.2
  107.7 12.5 %all-to-all-start.5 = ((bf16[8,64,128]{2,1,0:T(8,128)(2,1)}), bf16[8,64,128]{2,1,0:T(8,128)(2,1)S(1)}, u32[]{:S(2)}, u32[]{:S(2)}) async-start(bf16[8,64,128]{2,1,0:T(8,128)(2,1)} %bitcast.15), calls=%async_computation.5 | async-start | bytes 262144 | tf_op jit(solution)/shard_map/all_to_all | solution.py:74
  112.7 88.5 %collective-permute-start.1 = (bf16[4096,384]{1,0:T(8,128)(2,1)}, bf16[4096,384]{1,0:T(8,128)(2,1)}, u32[]{:S(2)}, u32[]{:S(2)}) collective-permute-start(bf16[4096,384]{1,0:T(8,128)(2,1)} %all-gather.4.cloned.1.call-done), channel_id=1, source_target_pairs={{0,8},{8,0},{1,9},{9,1},{2,10},{10,2},{3,11},{11,3},{4,12},{12,4},... | collective-permute-start | bytes 9437192 | tf_op jit(solution)/shard_map/ppermute | solution.py:65
  115.0 18.5 %copy-start.8 = (bf16[512]{0:T(512)(128)(2,1)S(1)}, bf16[512]{0:T(512)(128)(2,1)}, u32[]{:S(2)}) copy-start(bf16[512]{0:T(512)(128)(2,1)} %param.13) | copy-start | bytes 3076
  120.2 65.4 %copy-start.5 = (bf16[8,64,128]{2,1,0:T(8,128)(2,1)}, bf16[8,64,128]{2,1,0:T(8,128)(2,1)S(1)}, u32[]{:S(2)}) copy-start(bf16[8,64,128]{2,1,0:T(8,128)(2,1)S(1)} %all-to-all-done.5) | copy-start | bytes 393220
  122.2 63.4 %all-to-all-start.2 = ((bf16[4,2,200,512]{3,1,2,0:T(2,128)(2,1)}), bf16[4,2,200,512]{3,1,2,0:T(2,128)(2,1)S(1)}, u32[]{:S(2)}, u32[]{:S(2)}) async-start(bf16[4,2,200,512]{3,1,2,0:T(2,128)(2,1)} %broadcast_in_dim.62), calls=%async_computation.2 | async-start | bytes 3276800 | tf_op jit(solution)/shard_map/all_to_all | solution.py:91
  133.5 90.1 %all-gather.6.cloned.1.call-start = ((), (), s32[]{:S(2)}) async-start(), calls=%async_computation.7 | async-start | bytes 1179648 | tf_op jit(solution)/shard_map/all_gather | solution.py:76
  185.6 1.2 copy-start.2
  207.0 27.1 %all-to-all-start.4 = ((bf16[8,200,256]{2,1,0:T(8,128)(2,1)}), bf16[8,200,256]{2,1,0:T(8,128)(2,1)S(1)}, u32[]{:S(2)}, u32[]{:S(2)}) async-start(bf16[8,200,256]{2,1,0:T(8,128)(2,1)} %broadcast_in_dim.66), calls=%async_computation.4 | async-start | bytes 1638400 | tf_op jit(solution)/shard_map/all_to_all | solution.py:131
  223.6 12.6 %collective-permute-start.3 = (bf16[8,512,128]{2,1,0:T(8,128)(2,1)}, bf16[8,512,128]{2,1,0:T(8,128)(2,1)S(1)}, u32[]{:S(2)}, u32[]{:S(2)}) collective-permute-start(bf16[8,512,128]{2,1,0:T(8,128)(2,1)} %all-gather.6.cloned.1.call-done), channel_id=1, source_target_pairs={{0,8},{8,0},{1,9},{9,1},{2,10},{10,2},{3,11},{11,3},{4,12},{12,4},... | collective-permute-start | bytes 3145736 | tf_op jit(solution)/shard_map/ppermute | solution.py:77
  236.1 0.9 copy-start.4
Sparse Core Ops, SparseCore 0:
  27.5 82.8 all-gather.3
  185.7 37.8 all-gather.5

commit v2 on v1

v2 whole, which is shorter than its diff:
```python
import functools

import jax
import jax.numpy as jnp
from jax import lax
from jax.experimental import pallas as pl
from jax.experimental.pallas import tpu as pltpu
from jax.sharding import Mesh, PartitionSpec as P

HEAD_DIM = 128
ROW_TILE = 16
SPLIT = (("z", 8), ("y", 4), ("c", 2), ("h", 2), ("x", 4))
SIZE = dict(SPLIT)
AXES = tuple(name for name, _ in SPLIT)
CORPUS = ("z", "y", "c")
TENSOR = ("h", "x")
SWAP = [(0, 1), (1, 0)]
VMEM = pl.BlockSpec(memory_space=pltpu.VMEM)


def attention_kernel(full_ref, own_ref, other_ref, cos_ref, sin_ref, mask_ref, out_ref, normed_ref, *, gain_row):
    bf16, f32 = jnp.bfloat16, jnp.float32
    spread, highs, rows, features = full_ref.shape
    width = spread * highs * features
    total = jnp.zeros((rows, HEAD_DIM), f32)
    for x in range(spread):
        for h in range(highs):
            chunk = full_ref[x, h].astype(f32)
            square = chunk * chunk
            for lane in range(0, features, HEAD_DIM):
                total = total + square[:, lane : lane + HEAD_DIM]
    inverse = lax.rsqrt(jnp.sum(total, axis=1, keepdims=True) / width + 1e-05)
    for x in range(spread):
        for h in range(highs):
            chunk = full_ref[x, h].astype(f32)
            gain = chunk[gain_row : gain_row + 1, :]
            begin = (h * spread + x) * features
            normed_ref[:, begin : begin + features] = (chunk * inverse * gain).astype(bf16)

    def rotate(inputs):
        return (
            inputs * cos_ref[...] + pltpu.roll(inputs, HEAD_DIM // 2, 1) * sin_ref[...]
        ).astype(bf16)

    def head(weight_ref):
        projected = jnp.dot(normed_ref[...], weight_ref[...], preferred_element_type=f32)
        queries = rotate(projected[:, :HEAD_DIM])
        keys = rotate(projected[:, HEAD_DIM : 2 * HEAD_DIM])
        values = projected[:, 2 * HEAD_DIM :].astype(bf16)
        scores = lax.dot_general(
            queries, keys, (((1,), (1,)), ((), ())), preferred_element_type=f32
        ) * (1.0 / float(HEAD_DIM) ** 0.5)
        scores = jnp.where(mask_ref[...] > 0, scores, -1e30)
        exponent = jnp.exp(scores - jnp.max(scores, axis=-1, keepdims=True))
        weights = (exponent / jnp.sum(exponent, axis=-1, keepdims=True)).astype(bf16)
        return jnp.dot(weights, values, preferred_element_type=f32).astype(bf16)

    mine, theirs = head(own_ref), head(other_ref)
    first = lax.axis_index("c") == 0
    out_ref[:, :HEAD_DIM] = jnp.where(first, mine, theirs)
    out_ref[:, HEAD_DIM:] = jnp.where(first, theirs, mine)


def output_kernel(heads_ref, own_ref, other_ref, packed_ref, out_ref, *, query_len, pairs, passage_rows):
    bf16, f32 = jnp.bfloat16, jnp.float32
    first = lax.axis_index("c") == 0
    numbers = (((1,), (1,)), ((), ()))
    summed = jnp.zeros(packed_ref.shape, f32)
    for t in range(heads_ref.shape[0]):
        low, high = heads_ref[t, :, :HEAD_DIM], heads_ref[t, :, HEAD_DIM:]
        near, far = jnp.where(first, low, high), jnp.where(first, high, low)
        partial_value = lax.dot_general(
            near, own_ref[t], numbers, preferred_element_type=f32
        ) + lax.dot_general(far, other_ref[t], numbers, preferred_element_type=f32)
        summed = summed + partial_value.astype(bf16).astype(f32)
    final = packed_ref[...].astype(f32) + summed
    blocks = []
    for pair in range(pairs):
        begin = query_len + pair * passage_rows
        blocks += [final[:query_len], final[begin : begin + passage_rows]]
    out_ref[...] = jnp.concatenate(blocks, axis=0).astype(bf16)


def shift(value, axis, step):
    count = SIZE[axis]
    return lax.ppermute(value, axis, [(i, (i + step) % count) for i in range(count)])


def gather_plane(blocks):
    first = lax.axis_index("c") == 0
    mine = jnp.where(first, blocks[0], blocks[1])
    got = lax.ppermute(jnp.where(first, blocks[1], blocks[0]), "c", SWAP)
    pair = jnp.concatenate([jnp.where(first, mine, got), jnp.where(first, got, mine)], axis=0)
    pieces = jnp.stack([pair] + [shift(pair, "y", step) for step in range(1, SIZE["y"])])
    order = (lax.axis_index("y") - jnp.arange(SIZE["y"], dtype=jnp.int32)) % SIZE["y"]
    pieces = jnp.take(pieces, order, axis=0, mode="clip")
    return pieces.reshape(-1, pieces.shape[2])


def on_device(
    query_rows,
    corpus_rows,
    passage_length,
    candidate_owner,
    candidate_slot,
    norm_gain,
    project_weight,
    output_weight,
):
    bf16, f32, i32 = jnp.bfloat16, jnp.float32, jnp.int32
    shards = SIZE["z"] * SIZE["y"] * SIZE["c"]
    plane = SIZE["y"] * SIZE["c"]
    tensors = SIZE["h"] * SIZE["x"]
    stored, passage_rows, features = corpus_rows.shape
    query_len = query_rows.shape[1]
    pairs = candidate_owner.shape[1]
    live = query_len + pairs * passage_rows
    rows = (live // ROW_TILE + 1) * ROW_TILE
    depth = project_weight.shape[0]

    wide = project_weight.reshape(depth, 3, 2, HEAD_DIM).transpose(2, 0, 1, 3)
    wide = gather_plane(wide.reshape(2, depth, 3 * HEAD_DIM))

    own_owner, own_slot = candidate_owner[0], candidate_slot[0]
    asks = jnp.arange(shards, dtype=i32)[:, None] == own_owner[None, :]
    request = jnp.sum(jnp.where(asks, own_slot[None, :] + 1, 0), axis=1)
    request = jnp.broadcast_to(request[:, None], (shards, 128))
    asked = lax.all_to_all(request, CORPUS, split_axis=0, concat_axis=0, tiled=True)
    wanted = jnp.clip(asked[:, 0] - 1, 0, stored - 1)

    wide_own = lax.all_gather(wide, "z", axis=0, tiled=True)
    wide_other = lax.ppermute(wide_own, "c", SWAP)
    cells = [(z, q, t) for z in range(SIZE["z"]) for q in range(plane) for t in range(tensors)]
    number = {cell: i for i, cell in enumerate(cells)}
    turn = [(number[(z, q, t)], number[(t, q, z)]) for z, q, t in cells]
    narrow = lax.ppermute(output_weight.T, AXES, turn)
    narrow, wanted = lax.optimization_barrier((narrow, wanted))
    narrow = gather_plane(narrow.reshape(depth, 2, HEAD_DIM).transpose(1, 0, 2))
    narrow_own = lax.all_gather(narrow[None], "z", axis=0, tiled=True)
    narrow_other = lax.ppermute(narrow_own, "c", SWAP)

    outgoing = jnp.take(corpus_rows, wanted, axis=0, mode="clip")
    arrived = lax.all_to_all(outgoing, CORPUS, split_axis=0, concat_axis=0, tiled=True)
    counts = jnp.take(passage_length, own_owner * stored + own_slot, axis=0, mode="clip")
    passages = jnp.take(arrived, own_owner, axis=0, mode="clip")
    inside = jnp.arange(passage_rows, dtype=i32)[None, :] < counts[:, None]
    passages = jnp.where(inside[:, :, None], passages, jnp.zeros((), bf16))
    packed = jnp.concatenate(
        [
            query_rows[0],
            passages.reshape(-1, features),
            norm_gain[None],
            jnp.zeros((rows - live - 1, features), bf16),
        ],
        axis=0,
    )

    far = lax.ppermute(packed, "h", SWAP)
    low = lax.axis_index("h") == 0
    both = jnp.stack([jnp.where(low, packed, far), jnp.where(low, far, packed)])
    spread = jnp.broadcast_to(both[None], (SIZE["x"],) + both.shape)
    full = lax.all_to_all(spread, "x", split_axis=0, concat_axis=0, tiled=True)

    row = jnp.arange(rows, dtype=i32)
    is_query = row < query_len
    slot = jnp.where(is_query, row, query_len + (row - query_len) % passage_rows)
    pair = jnp.where(is_query, -1, (row - query_len) // passage_rows)
    count_of = jnp.concatenate(
        [
            jnp.full((query_len,), passage_rows, i32),
            jnp.repeat(counts, passage_rows),
            jnp.zeros((rows - live,), i32),
        ]
    )
    allowed = (slot[None, :] <= slot[:, None]) & (
        is_query[None, :]
        | ((pair[None, :] == pair[:, None]) & (slot < query_len + count_of)[None, :])
    )
    half = HEAD_DIM // 2
    frequency = jnp.power(10000.0, -2.0 * jnp.arange(half, dtype=f32) / HEAD_DIM)
    angles = slot.astype(f32)[:, None] * frequency[None, :]
    cosine, sine = jnp.cos(angles), jnp.sin(angles)

    attended = pl.pallas_call(
        functools.partial(attention_kernel, gain_row=live),
        out_shape=jax.ShapeDtypeStruct((rows, 2 * HEAD_DIM), bf16),
        in_specs=[VMEM] * 6,
        out_specs=VMEM,
        scratch_shapes=[pltpu.VMEM((rows, tensors * features), bf16)],
        compiler_params=pltpu.CompilerParams(vmem_limit_bytes=32 * 1024 * 1024),
        cost_estimate=pl.CostEstimate(
            flops=2 * rows * tensors * features * 6 * HEAD_DIM,
            bytes_accessed=8 * 1024 * 1024,
            transcendentals=2 * rows * rows,
        ),
        name="attention",
    )(
        full,
        wide_own,
        wide_other,
        jnp.concatenate([cosine, cosine], axis=1),
        jnp.concatenate([-sine, sine], axis=1),
        allowed.astype(f32),
    )

    spread = jnp.broadcast_to(attended[None], (tensors,) + attended.shape)
    heads = lax.all_to_all(spread, TENSOR, split_axis=0, concat_axis=0, tiled=True)
    return pl.pallas_call(
        functools.partial(
            output_kernel, query_len=query_len, pairs=pairs, passage_rows=passage_rows
        ),
        out_shape=jax.ShapeDtypeStruct((pairs * (query_len + passage_rows), features), bf16),
        in_specs=[VMEM] * 4,
        out_specs=VMEM,
        compiler_params=pltpu.CompilerParams(vmem_limit_bytes=32 * 1024 * 1024),
        cost_estimate=pl.CostEstimate(
            flops=2 * rows * tensors * 2 * HEAD_DIM * features,
            bytes_accessed=3 * 1024 * 1024,
            transcendentals=0,
        ),
        name="output",
    )(heads, narrow_own, narrow_other, packed)


def solution(mesh):
    fine = Mesh(mesh.devices.reshape([size for _, size in SPLIT]), AXES)
    placed = (
        P(CORPUS, None, TENSOR),
        P(CORPUS, None, TENSOR),
        P(),
        P(CORPUS, None),
        P(CORPUS, None),
        P(TENSOR),
        P(CORPUS, None, TENSOR),
        P(TENSOR, CORPUS),
    )
    return jax.shard_map(
        on_device, mesh=fine, in_specs=placed, out_specs=P(CORPUS, TENSOR), check_vma=False
    )
```

time: 246 us -> 215 us (0.87)
  blocking collectives: 89.9 us -> 0 us
  starting transfers between devices: 39.6 us -> 81.2 us
  waiting for transfers between devices: 66.7 us -> 97.6 us
  matrix products: 9.98 us -> 0 us
  Pallas kernels: 0 us -> 6.81 us
  other arithmetic: 8.08 us -> 1.75 us
  local copies, waits for them, and re-layouts: 16.6 us -> 13.3 us
    all_gather x1 -> x0, blocking collectives: 51.9 us -> none  [on_device(): gain = lax.all_gather(norm_gain, TENSOR, axis=0, tiled=True)]
    all_to_all x1, waiting for transfers between devices: 43.7 us -> 0.01 us  [on_device(): lax.all_to_all(outgoing, CORPUS, split_axis=0, concat_axis=0, tiled=True)]
    all_gather x1, waiting for transfers between devices: 0.01 us -> 43.3 us  [on_device(): wide_own = lax.all_gather(wide, 'z', axis=0, tiled=True)]
    all_to_all x2 -> x0, blocking collectives: 38 us -> none  [the longest x1 19.6 us: on_device(): lax.all_to_all(wide, ('y', 'c'), split_axis=0, concat_axis=0, tiled=True)]
    ppermute x3 -> x11, starting transfers between devices: 9.98 us -> 39.6 us  [the longest x6 22.3 us: shift(): lax.ppermute(value, axis, [(i, (i + step) % count) for i in range(count)])]
    all_to_all x1, waiting for transfers between devices: 0.01 us -> 19.1 us  [on_device(): full = lax.all_to_all(spread, 'x', split_axis=0, concat_axis=0, tiled=True)]
    all_to_all x1, starting transfers between devices: 5.51 us -> 17.4 us  [on_device(): lax.all_to_all(outgoing, CORPUS, split_axis=0, concat_axis=0, tiled=True)]
    dot_general x8 -> x0, matrix products: 9.98 us -> none  [the longest x2 6.01 us: head(): projected = jnp.dot(normed, weight, preferred_element_type=f32)]
  transfers between devices with their start and end apart: 10 -> 18, of which waited for: 5 -> 10; matrix products, arithmetic and copies ran while one was open for 13% -> 4% of each run, Pallas kernels for 0% -> 2%
where the time goes in v2:
time: 215 us
  waiting for transfers between devices  97.6 us (45%)
  starting transfers between devices  81.2 us (38%)
  between operations  13.9 us (6%)
  local copies, waits for them, and re-layouts  13.3 us (6%)
  Pallas kernels  6.81 us (3%)
    all_gather x1, waiting for transfers between devices, on_device(): wide_own = lax.all_gather(wide, 'z', axis=0, tiled=True)  43.3 us
    ppermute x6, starting transfers between devices, shift(): lax.ppermute(value, axis, [(i, (i + step) % count) for i in range(count)])  22.3 us
    all_to_all x1, waiting for transfers between devices, on_device(): full = lax.all_to_all(spread, 'x', split_axis=0, concat_axis=0, tiled=True)  19.1 us
    all_to_all x1, starting transfers between devices, on_device(): lax.all_to_all(outgoing, CORPUS, split_axis=0, concat_axis=0, tiled=True)  17.4 us
    all_to_all x1, starting transfers between devices, on_device(): lax.all_to_all(request, CORPUS, split_axis=0, concat_axis=0, tiled=True)  12.9 us
    all_to_all x1, waiting for transfers between devices, on_device(): lax.all_to_all(spread, TENSOR, split_axis=0, concat_axis=0, tiled=True)  10.8 us
    ppermute x1, starting transfers between devices, on_device(): far = lax.ppermute(packed, 'h', SWAP)  9.15 us
    all_to_all x1, waiting for transfers between devices, on_device(): lax.all_to_all(request, CORPUS, split_axis=0, concat_axis=0, tiled=True)  8.12 us
  transfers between devices with their start and end apart: 18, of which 10 were waited for; matrix products, arithmetic and copies ran while one was open for 4% of the time, Pallas kernels for 2%

profile of v2, /device:TPU:8, one launch (start us, length us, event | category | flops | bytes accessed | tf_op | source)
XLA Modules:
  0.0 214.5 jit_solution(15004643967490618533)
XLA Ops:
  7.7 1.9 collective-permute-start.2
  10.9 7.7 %collective-permute-start.5 = (bf16[128,384]{1,0:T(8,128)(2,1)S(1)}, bf16[128,384]{1,0:T(8,128)(2,1)S(1)}, u32[]{:S(2)}, u32[]{:S(2)}) collective-permute-start(bf16[128,384]{1,0:T(8,128)(2,1)S(1)} %get-tuple-element.16), channel_id=1, source_target_pairs={{0,48},{16,0},{32,16},{48,32},{1,49},{17,1},{33,17},{49,33},{2,50}... | collective-permute-start | bytes 294920 | tf_op jit(solution)/shard_map/ppermute | solution.py:86
  18.6 1.9 collective-permute-start.4
  20.6 3.4 %collective-permute-start.3 = (bf16[128,384]{1,0:T(8,128)(2,1)S(1)}, bf16[128,384]{1,0:T(8,128)(2,1)S(1)}, u32[]{:S(2)}, u32[]{:S(2)}) collective-permute-start(bf16[128,384]{1,0:T(8,128)(2,1)S(1)} %get-tuple-element.16), channel_id=1, source_target_pairs={{0,16},{16,32},{32,48},{48,0},{1,17},{17,33},{33,49},{49,1},{2,18}... | collective-permute-start | bytes 294920 | tf_op jit(solution)/shard_map/ppermute | solution.py:86
  24.0 2.4 %collective-permute-done.4 = bf16[128,384]{1,0:T(8,128)(2,1)S(1)} collective-permute-done((bf16[128,384]{1,0:T(8,128)(2,1)S(1)}, bf16[128,384]{1,0:T(8,128)(2,1)S(1)}, u32[]{:S(2)}, u32[]{:S(2)}) %collective-permute-start.4) | collective-permute-done | bytes 98336 | tf_op jit(solution)/shard_map/ppermute | solution.py:86
  29.4 12.9 %all-to-all-start = ((s32[64,1,128]{2,1,0:T(1,128)}), s32[64,1,128]{2,1,0:T(1,128)S(1)}, u32[]{:S(2)}, u32[]{:S(2)}) async-start(s32[64,1,128]{2,1,0:T(1,128)} %broadcast_in_dim.83), calls=%async_computation | async-start | bytes 65536 | tf_op jit(solution)/shard_map/all_to_all | solution.py:128
  42.9 8.1 %all-to-all-done = s32[64,1,128]{2,1,0:T(1,128)S(1)} async-done(((s32[64,1,128]{2,1,0:T(1,128)}), s32[64,1,128]{2,1,0:T(1,128)S(1)}, u32[]{:S(2)}, u32[]{:S(2)}) %all-to-all-start) | async-done | bytes 32800 | tf_op jit(solution)/shard_map/all_to_all | solution.py:128
  53.0 17.4 %all-to-all-start.1 = ((bf16[64,24,512]{2,1,0:T(8,128)(2,1)}), bf16[64,24,512]{2,1,0:T(8,128)(2,1)S(1)}, u32[]{:S(2)}, u32[]{:S(2)}) async-start(bf16[64,24,512]{2,1,0:T(8,128)(2,1)} %gather_fusion.1), calls=%async_computation.1 | async-start | bytes 3145728 | tf_op jit(solution)/shard_map/all_to_all | solution.py:143
  70.4 43.3 %all-gather.3.cloned.1.call-done.own_ref = bf16[4096,384]{1,0:T(8,128)(2,1)} async-done(((bf16[512,384]{1,0:T(8,128)(2,1)}), bf16[4096,384]{1,0:T(8,128)(2,1)}) %all-gather.3.cloned.1.call-update) | async-done | bytes 3145744 | tf_op jit(solution)/shard_map/all_gather | solution.py:131
  113.7 1.9 collective-permute-start.6
  116.8 2.4 %collective-permute-start.7 = (bf16[64,128]{1,0:T(8,128)(2,1)S(1)}, bf16[64,128]{1,0:T(8,128)(2,1)S(1)}, u32[]{:S(2)}, u32[]{:S(2)}) collective-permute-start(bf16[64,128]{1,0:T(8,128)(2,1)S(1)} %bitcast.66), channel_id=1, source_target_pairs={{0,8},{8,0},{1,9},{9,1},{2,10},{10,2},{3,11},{11,3},{4,12},{12,4},... | collective-permute-start | bytes 49160 | tf_op jit(solution)/shard_map/ppermute | solution.py:92
  120.0 9.1 %collective-permute-start.1 = (bf16[208,512]{1,0:T(8,128)(2,1)S(1)}, bf16[208,512]{1,0:T(8,128)(2,1)S(1)}, u32[]{:S(2)}, u32[]{:S(2)}) collective-permute-start(bf16[208,512]{1,0:T(8,128)(2,1)S(1)} %maximum_maximum_fusion.packed_ref), channel_id=1, source_target_pairs={{0,4},{4,0},{1,5},{5,1},{2,6},{6,2},{3,7},{7,3},{8,12},{12,8},{9,1... | collective-permute-start | bytes 638984 | tf_op jit(solution)/shard_map/ppermute | solution.py:158
  129.2 3.3 %collective-permute-start.10 = (bf16[128,128]{1,0:T(8,128)(2,1)S(1)}, bf16[128,128]{1,0:T(8,128)(2,1)S(1)}, u32[]{:S(2)}, u32[]{:S(2)}) collective-permute-start(bf16[128,128]{1,0:T(8,128)(2,1)S(1)} %get-tuple-element.20), channel_id=1, source_target_pairs={{0,48},{16,0},{32,16},{48,32},{1,49},{17,1},{33,17},{49,33},{2,50}... | collective-permute-start | bytes 98312 | tf_op jit(solution)/shard_map/ppermute | solution.py:86
  132.6 2.5 %collective-permute-start.9 = (bf16[128,128]{1,0:T(8,128)(2,1)S(1)}, bf16[128,128]{1,0:T(8,128)(2,1)S(1)}, u32[]{:S(2)}, u32[]{:S(2)}) collective-permute-start(bf16[128,128]{1,0:T(8,128)(2,1)S(1)} %get-tuple-element.20), channel_id=1, source_target_pairs={{0,32},{16,48},{32,0},{48,16},{1,33},{17,49},{33,1},{49,17},{2,34}... | collective-permute-start | bytes 98312 | tf_op jit(solution)/shard_map/ppermute | solution.py:86
  135.1 3.4 %collective-permute-start.8 = (bf16[128,128]{1,0:T(8,128)(2,1)S(1)}, bf16[128,128]{1,0:T(8,128)(2,1)S(1)}, u32[]{:S(2)}, u32[]{:S(2)}) collective-permute-start(bf16[128,128]{1,0:T(8,128)(2,1)S(1)} %get-tuple-element.20), channel_id=1, source_target_pairs={{0,16},{16,32},{32,48},{48,0},{1,17},{17,33},{33,49},{49,1},{2,18}... | collective-permute-start | bytes 98312 | tf_op jit(solution)/shard_map/ppermute | solution.py:86
  141.8 4.0 %all-to-all-start.2 = ((bf16[4,2,208,512]{3,2,1,0:T(8,128)(2,1)}), bf16[4,2,208,512]{3,2,1,0:T(8,128)(2,1)S(1)}, u32[]{:S(2)}, u32[]{:S(2)}) async-start(bf16[4,2,208,512]{3,2,1,0:T(8,128)(2,1)} %broadcast_in_dim.88), calls=%async_computation.2 | async-start | bytes 3407872 | tf_op jit(solution)/shard_map/all_to_all | solution.py:162
  147.9 19.1 %all-to-all-done.2.full_ref = bf16[4,2,208,512]{3,2,1,0:T(8,128)(2,1)S(1)} async-done(((bf16[4,2,208,512]{3,2,1,0:T(8,128)(2,1)}), bf16[4,2,208,512]{3,2,1,0:T(8,128)(2,1)S(1)}, u32[]{:S(2)}, u32[]{:S(2)}) %all-to-all-start.2) | async-done | bytes 1703968 | tf_op jit(solution)/shard_map/all_to_all | solution.py:162
  167.1 1.9 copy-done.1
  169.0 5.0 %attention.1 = bf16[208,256]{1,0:T(8,128)(2,1)S(1)} custom-call(bf16[4,2,208,512]{3,2,1,0:T(8,128)(2,1)S(1)} %all-to-all-done.2.full_ref, bf16[4096,384]{1,0:T(8,128)(2,1)S(1)} %copy-done.1, bf16[4096,384]{1,0:T(8,128)(2,1)} %collective-permute-done.6.other_ref, f32[208,128]{1,0:T(8,128)S(1)} %get-tuple-element.28.cos_ref, ...), custom_call_target="tpu_custom_call" | custom-call | flops 1308622848 | bytes 8388608 | tf_op jit(solution)/shard_map/attention/pallas_call | solution.py:184
  175.0 6.7 %all-to-all-start.3 = ((bf16[8,208,256]{2,1,0:T(8,128)(2,1)}), bf16[8,208,256]{2,1,0:T(8,128)(2,1)S(1)}, u32[]{:S(2)}, u32[]{:S(2)}) async-start(bf16[8,208,256]{2,1,0:T(8,128)(2,1)} %broadcast_in_dim.90), calls=%async_computation.3 | async-start | bytes 1703936 | tf_op jit(solution)/shard_map/all_to_all | solution.py:207
  181.7 7.4 %all-gather.5.cloned.1.call-done.own_ref = bf16[8,512,128]{2,1,0:T(8,128)(2,1)} async-done(((bf16[1,512,128]{2,1,0:T(8,128)(2,1)}), bf16[8,512,128]{2,1,0:T(8,128)(2,1)}) %all-gather.5.cloned.1.call-update) | async-done | bytes 1048592 | tf_op jit(solution)/shard_map/all_gather | solution.py:139
  189.1 1.9 collective-permute-start.11
  191.0 2.8 %collective-permute-done.11.other_ref = bf16[8,512,128]{2,1,0:T(8,128)(2,1)S(1)} collective-permute-done((bf16[8,512,128]{2,1,0:T(8,128)(2,1)}, bf16[8,512,128]{2,1,0:T(8,128)(2,1)S(1)}, u32[]{:S(2)}, u32[]{:S(2)}) %collective-permute-start.11) | collective-permute-done | bytes 1048608 | tf_op jit(solution)/shard_map/ppermute | solution.py:140
  193.8 10.8 %all-to-all-done.3.heads_ref = bf16[8,208,256]{2,1,0:T(8,128)(2,1)S(1)} async-done(((bf16[8,208,256]{2,1,0:T(8,128)(2,1)}), bf16[8,208,256]{2,1,0:T(8,128)(2,1)S(1)}, u32[]{:S(2)}, u32[]{:S(2)}) %all-to-all-start.3) | async-done | bytes 852000 | tf_op jit(solution)/shard_map/all_to_all | solution.py:207
  (84 shorter events, 19.2 us)
Async XLA Ops:
  6.5 44.7 %copy-start = (bf16[8,24,512]{2,1,0:T(8,128)(2,1)S(1)}, bf16[8,24,512]{2,1,0:T(8,128)(2,1)}, u32[]{:S(2)}) copy-start(bf16[8,24,512]{2,1,0:T(8,128)(2,1)} %param.9) | copy-start | bytes 589828
  6.5 107.2 %all-gather.3.cloned.1.call-start = ((), (), s32[]{:S(2)}) async-start(), calls=%async_computation.4 | async-start | bytes 3538944 | tf_op jit(solution)/shard_map/all_gather | solution.py:131
  7.5 21.0 %copy-start.5 = (s32[1,8]{1,0:T(1,128)S(1)}, s32[1,8]{1,0:T(1,128)}, u32[]{:S(2)}) copy-start(s32[1,8]{1,0:T(1,128)} %param.11) | copy-start | bytes 100
  7.5 34.7 %copy-start.8 = (bf16[256,64]{0,1:T(8,128)(2,1)S(1)}, bf16[256,64]{0,1:T(8,128)(2,1)}, u32[]{:S(2)}) copy-start(bf16[256,64]{0,1:T(8,128)(2,1)} %param.15) | copy-start | bytes 98308
  7.7 3.1 %collective-permute-start.2 = (bf16[64,384]{1,0:T(8,128)(2,1)S(1)}, bf16[64,384]{1,0:T(8,128)(2,1)S(1)}, u32[]{:S(2)}, u32[]{:S(2)}) collective-permute-start(bf16[64,384]{1,0:T(8,128)(2,1)S(1)} %bitcast.60), channel_id=1, source_target_pairs={{0,8},{8,0},{1,9},{9,1},{2,10},{10,2},{3,11},{11,3},{4,12},{12,4},... | collective-permute-start | bytes 147464 | tf_op jit(solution)/shard_map/ppermute | solution.py:92
  10.9 13.1 %collective-permute-start.5 = (bf16[128,384]{1,0:T(8,128)(2,1)S(1)}, bf16[128,384]{1,0:T(8,128)(2,1)S(1)}, u32[]{:S(2)}, u32[]{:S(2)}) collective-permute-start(bf16[128,384]{1,0:T(8,128)(2,1)S(1)} %get-tuple-element.16), channel_id=1, source_target_pairs={{0,48},{16,0},{32,16},{48,32},{1,49},{17,1},{33,17},{49,33},{2,50}... | collective-permute-start | bytes 294920 | tf_op jit(solution)/shard_map/ppermute | solution.py:86
  18.6 7.7 %collective-permute-start.4 = (bf16[128,384]{1,0:T(8,128)(2,1)S(1)}, bf16[128,384]{1,0:T(8,128)(2,1)S(1)}, u32[]{:S(2)}, u32[]{:S(2)}) collective-permute-start(bf16[128,384]{1,0:T(8,128)(2,1)S(1)} %get-tuple-element.16), channel_id=1, source_target_pairs={{0,32},{16,48},{32,0},{48,16},{1,33},{17,49},{33,1},{49,17},{2,34}... | collective-permute-start | bytes 294920 | tf_op jit(solution)/shard_map/ppermute | solution.py:86
  20.6 6.5 %collective-permute-start.3 = (bf16[128,384]{1,0:T(8,128)(2,1)S(1)}, bf16[128,384]{1,0:T(8,128)(2,1)S(1)}, u32[]{:S(2)}, u32[]{:S(2)}) collective-permute-start(bf16[128,384]{1,0:T(8,128)(2,1)S(1)} %get-tuple-element.16), channel_id=1, source_target_pairs={{0,16},{16,32},{32,48},{48,0},{1,17},{17,33},{33,49},{49,1},{2,18}... | collective-permute-start | bytes 294920 | tf_op jit(solution)/shard_map/ppermute | solution.py:86
  29.4 21.7 %all-to-all-start = ((s32[64,1,128]{2,1,0:T(1,128)}), s32[64,1,128]{2,1,0:T(1,128)S(1)}, u32[]{:S(2)}, u32[]{:S(2)}) async-start(s32[64,1,128]{2,1,0:T(1,128)} %broadcast_in_dim.83), calls=%async_computation | async-start | bytes 65536 | tf_op jit(solution)/shard_map/all_to_all | solution.py:128
  42.3 8.9 %collective-permute-start = (bf16[64,256]{1,0:T(8,128)(2,1)S(1)}, bf16[64,256]{1,0:T(8,128)(2,1)S(1)}, u32[]{:S(2)}, u32[]{:S(2)}) collective-permute-start(bf16[64,256]{1,0:T(8,128)(2,1)S(1)} %bitcast.69), channel_id=1, source_target_pairs={{0,0},{1,64},{2,128},{3,192},{4,256},{5,320},{6,384},{7,448},{8,8}... | collective-permute-start | bytes 98312 | tf_op jit(solution)/shard_map/ppermute | solution.py:136
  53.0 62.6 %copy-start.6 = (bf16[512]{0:T(512)(128)(2,1)S(1)}, bf16[512]{0:T(512)(128)(2,1)}, u32[]{:S(2)}) copy-start(bf16[512]{0:T(512)(128)(2,1)} %param.13) | copy-start | bytes 3076
  53.0 62.7 %copy-start.3 = (s32[512]{0:T(512)S(1)}, s32[512]{0:T(512)}, u32[]{:S(2)}) copy-start(s32[512]{0:T(512)} %param.10) | copy-start | bytes 6148
  53.0 66.2 %all-to-all-start.1 = ((bf16[64,24,512]{2,1,0:T(8,128)(2,1)}), bf16[64,24,512]{2,1,0:T(8,128)(2,1)S(1)}, u32[]{:S(2)}, u32[]{:S(2)}) async-start(bf16[64,24,512]{2,1,0:T(8,128)(2,1)} %gather_fusion.1), calls=%async_computation.1 | async-start | bytes 3145728 | tf_op jit(solution)/shard_map/all_to_all | solution.py:143
  70.4 49.5 %copy-start.4 = (bf16[1,8,512]{2,1,0:T(8,128)(2,1)S(1)}, bf16[1,8,512]{2,1,0:T(8,128)(2,1)}, u32[]{:S(2)}) copy-start(bf16[1,8,512]{2,1,0:T(8,128)(2,1)} %param.8) | copy-start | bytes 24580
  113.7 53.3 %collective-permute-start.6 = (bf16[4096,384]{1,0:T(8,128)(2,1)}, bf16[4096,384]{1,0:T(8,128)(2,1)}, u32[]{:S(2)}, u32[]{:S(2)}) collective-permute-start(bf16[4096,384]{1,0:T(8,128)(2,1)} %all-gather.3.cloned.1.call-done.own_ref), channel_id=1, source_target_pairs={{0,8},{8,0},{1,9},{9,1},{2,10},{10,2},{3,11},{11,3},{4,12},{12,4},... | collective-permute-start | bytes 9437192 | tf_op jit(solution)/shard_map/ppermute | solution.py:132
  116.8 12.4 %collective-permute-start.7 = (bf16[64,128]{1,0:T(8,128)(2,1)S(1)}, bf16[64,128]{1,0:T(8,128)(2,1)S(1)}, u32[]{:S(2)}, u32[]{:S(2)}) collective-permute-start(bf16[64,128]{1,0:T(8,128)(2,1)S(1)} %bitcast.66), channel_id=1, source_target_pairs={{0,8},{8,0},{1,9},{9,1},{2,10},{10,2},{3,11},{11,3},{4,12},{12,4},... | collective-permute-start | bytes 49160 | tf_op jit(solution)/shard_map/ppermute | solution.py:92
  120.0 20.2 %collective-permute-start.1 = (bf16[208,512]{1,0:T(8,128)(2,1)S(1)}, bf16[208,512]{1,0:T(8,128)(2,1)S(1)}, u32[]{:S(2)}, u32[]{:S(2)}) collective-permute-start(bf16[208,512]{1,0:T(8,128)(2,1)S(1)} %maximum_maximum_fusion.packed_ref), channel_id=1, source_target_pairs={{0,4},{4,0},{1,5},{5,1},{2,6},{6,2},{3,7},{7,3},{8,12},{12,8},{9,1... | collective-permute-start | bytes 638984 | tf_op jit(solution)/shard_map/ppermute | solution.py:158
  129.2 16.6 %collective-permute-start.10 = (bf16[128,128]{1,0:T(8,128)(2,1)S(1)}, bf16[128,128]{1,0:T(8,128)(2,1)S(1)}, u32[]{:S(2)}, u32[]{:S(2)}) collective-permute-start(bf16[128,128]{1,0:T(8,128)(2,1)S(1)} %get-tuple-element.20), channel_id=1, source_target_pairs={{0,48},{16,0},{32,16},{48,32},{1,49},{17,1},{33,17},{49,33},{2,50}... | collective-permute-start | bytes 98312 | tf_op jit(solution)/shard_map/ppermute | solution.py:86
  132.6 13.2 %collective-permute-start.9 = (bf16[128,128]{1,0:T(8,128)(2,1)S(1)}, bf16[128,128]{1,0:T(8,128)(2,1)S(1)}, u32[]{:S(2)}, u32[]{:S(2)}) collective-permute-start(bf16[128,128]{1,0:T(8,128)(2,1)S(1)} %get-tuple-element.20), channel_id=1, source_target_pairs={{0,32},{16,48},{32,0},{48,16},{1,33},{17,49},{33,1},{49,17},{2,34}... | collective-permute-start | bytes 98312 | tf_op jit(solution)/shard_map/ppermute | solution.py:86
  135.1 10.7 %collective-permute-start.8 = (bf16[128,128]{1,0:T(8,128)(2,1)S(1)}, bf16[128,128]{1,0:T(8,128)(2,1)S(1)}, u32[]{:S(2)}, u32[]{:S(2)}) collective-permute-start(bf16[128,128]{1,0:T(8,128)(2,1)S(1)} %get-tuple-element.20), channel_id=1, source_target_pairs={{0,16},{16,32},{32,48},{48,0},{1,17},{17,33},{33,49},{49,1},{2,18}... | collective-permute-start | bytes 98312 | tf_op jit(solution)/shard_map/ppermute | solution.py:86
  141.8 25.2 %all-to-all-start.2 = ((bf16[4,2,208,512]{3,2,1,0:T(8,128)(2,1)}), bf16[4,2,208,512]{3,2,1,0:T(8,128)(2,1)S(1)}, u32[]{:S(2)}, u32[]{:S(2)}) async-start(bf16[4,2,208,512]{3,2,1,0:T(8,128)(2,1)} %broadcast_in_dim.88), calls=%async_computation.2 | async-start | bytes 3407872 | tf_op jit(solution)/shard_map/all_to_all | solution.py:162
  145.8 43.3 %all-gather.5.cloned.1.call-start = ((), (), s32[]{:S(2)}) async-start(), calls=%async_computation.5 | async-start | bytes 1179648 | tf_op jit(solution)/shard_map/all_gather | solution.py:139
  175.0 29.7 %all-to-all-start.3 = ((bf16[8,208,256]{2,1,0:T(8,128)(2,1)}), bf16[8,208,256]{2,1,0:T(8,128)(2,1)S(1)}, u32[]{:S(2)}, u32[]{:S(2)}) async-start(bf16[8,208,256]{2,1,0:T(8,128)(2,1)} %broadcast_in_dim.90), calls=%async_computation.3 | async-start | bytes 1703936 | tf_op jit(solution)/shard_map/all_to_all | solution.py:207
  189.1 4.8 %collective-permute-start.11 = (bf16[8,512,128]{2,1,0:T(8,128)(2,1)}, bf16[8,512,128]{2,1,0:T(8,128)(2,1)S(1)}, u32[]{:S(2)}, u32[]{:S(2)}) collective-permute-start(bf16[8,512,128]{2,1,0:T(8,128)(2,1)} %all-gather.5.cloned.1.call-done.own_ref), channel_id=1, source_target_pairs={{0,8},{8,0},{1,9},{9,1},{2,10},{10,2},{3,11},{11,3},{4,12},{12,4},... | collective-permute-start | bytes 3145736 | tf_op jit(solution)/shard_map/ppermute | solution.py:140
  (3 other events, 24.1 us)
Sparse Core Ops, SparseCore 0:
  28.6 85.0 all-gather.2
  148.7 40.3 all-gather.4

commit v3 on v2

v3 whole, which is shorter than its diff:
```python
import functools

import jax
import jax.numpy as jnp
from jax import lax
from jax.experimental import pallas as pl
from jax.experimental.pallas import tpu as pltpu
from jax.sharding import Mesh, PartitionSpec as P

HEAD_DIM = 128
ROW_TILE = 16
SPLIT = (("z", 8), ("y", 4), ("c", 2), ("h", 2), ("x", 4))
SIZE = dict(SPLIT)
AXES = tuple(name for name, _ in SPLIT)
CORPUS = ("z", "y", "c")
TENSOR = ("h", "x")
VMEM = pl.BlockSpec(memory_space=pltpu.VMEM)


def attention_kernel(near_ref, far_ref, weight_ref, cos_ref, sin_ref, mask_ref, out_ref, normed_ref, *, gain_row):
    bf16, f32 = jnp.bfloat16, jnp.float32
    spread, highs, groups, rows, part = near_ref.shape
    width = spread * highs * 2 * part
    core = lax.axis_index("c")
    for group in range(groups):
        total = jnp.zeros((rows, HEAD_DIM), f32)
        for ref in (near_ref, far_ref):
            for x in range(spread):
                for h in range(highs):
                    chunk = ref[x, h, group].astype(f32)
                    square = chunk * chunk
                    for lane in range(0, part, HEAD_DIM):
                        total = total + square[:, lane : lane + HEAD_DIM]
        inverse = lax.rsqrt(jnp.sum(total, axis=1, keepdims=True) / width + 1e-05)
        for ref, half in ((near_ref, core), (far_ref, 1 - core)):
            for x in range(spread):
                for h in range(highs):
                    chunk = ref[x, h, group].astype(f32)
                    gain = chunk[gain_row : gain_row + 1, :]
                    begin = pl.multiple_of(((h * spread + x) * 2 + half) * part, part)
                    normed_ref[group * rows : (group + 1) * rows, pl.ds(begin, part)] = (
                        chunk * inverse * gain
                    ).astype(bf16)
    projected = jnp.dot(
        normed_ref[...], weight_ref[:, : 3 * HEAD_DIM], preferred_element_type=f32
    )

    def rotate(inputs):
        return (
            inputs * cos_ref[...] + pltpu.roll(inputs, HEAD_DIM // 2, 1) * sin_ref[...]
        ).astype(bf16)

    for group in range(groups):
        mine = projected[group * rows : (group + 1) * rows]
        queries = rotate(mine[:, :HEAD_DIM])
        keys = rotate(mine[:, HEAD_DIM : 2 * HEAD_DIM])
        values = mine[:, 2 * HEAD_DIM :].astype(bf16)
        scores = lax.dot_general(
            queries, keys, (((1,), (1,)), ((), ())), preferred_element_type=f32
        ) * (1.0 / float(HEAD_DIM) ** 0.5)
        scores = jnp.where(mask_ref[group] > 0, scores, -1e30)
        exponent = jnp.exp(scores - jnp.max(scores, axis=-1, keepdims=True))
        weights = (exponent / jnp.sum(exponent, axis=-1, keepdims=True)).astype(bf16)
        out_ref[group] = jnp.dot(weights, values, preferred_element_type=f32).astype(bf16)


def output_kernel(heads_ref, own_ref, other_ref, near_ref, far_ref, out_ref, *, query_len, pairs, passage_rows):
    bf16, f32 = jnp.bfloat16, jnp.float32
    core = lax.axis_index("c")
    numbers = (((1,), (1,)), ((), ()))
    tensors = heads_ref.shape[0] // 2
    columns = own_ref.shape[0] // tensors
    near, far = near_ref[...], far_ref[...]
    first = core == 0
    final = jnp.concatenate(
        [jnp.where(first, near, far), jnp.where(first, far, near)], axis=1
    ).astype(f32)
    summed = jnp.zeros(final.shape, f32)
    for t in range(tensors):
        block = slice(t * columns, (t + 1) * columns)
        partial_value = lax.dot_general(
            heads_ref[core * tensors + t], own_ref[block], numbers, preferred_element_type=f32
        ) + lax.dot_general(
            heads_ref[(1 - core) * tensors + t], other_ref[block], numbers, preferred_element_type=f32
        )
        summed = summed + partial_value.astype(bf16).astype(f32)
    final = final + summed
    blocks = []
    for pair in range(pairs):
        begin = query_len + pair * passage_rows
        blocks += [final[:query_len], final[begin : begin + passage_rows]]
    out_ref[...] = jnp.concatenate(blocks, axis=0).astype(bf16)


def partner(value, axis, bit):
    return lax.ppermute(value, axis, [(i, i ^ bit) for i in range(SIZE[axis])])


def by_core(mine, got):
    first = lax.axis_index("c") == 0
    return jnp.stack([jnp.where(first, mine, got), jnp.where(first, got, mine)])


def halves(value, part):
    first = lax.axis_index("c") == 0
    low, high = value[..., :part], value[..., part:]
    return jnp.where(first, low, high), jnp.where(first, high, low)


def gather_plane(blocks):
    first = lax.axis_index("c") == 0
    keep = jnp.where(first, blocks[0], blocks[1])
    got = partner(jnp.where(first, blocks[1], blocks[0]), "c", 1)
    pair = by_core(keep, got)
    two = jnp.stack([pair, partner(pair, "y", 2)])
    four = jnp.concatenate([two, partner(two, "y", 1)])
    apart = jnp.arange(SIZE["y"], dtype=jnp.int32) ^ lax.axis_index("y")
    where = (apart % 2) * 2 + apart // 2
    return jnp.take(four, where, axis=0, mode="clip").reshape(-1, blocks.shape[2])


def on_device(
    query_rows,
    corpus_rows,
    passage_length,
    candidate_owner,
    candidate_slot,
    norm_gain,
    project_weight,
    output_weight,
):
    bf16, f32, i32 = jnp.bfloat16, jnp.float32, jnp.int32
    plane = SIZE["y"] * SIZE["c"]
    tensors = SIZE["h"] * SIZE["x"]
    stored, passage_rows, features = corpus_rows.shape
    part = features // 2
    query_len = query_rows.shape[1]
    pairs = candidate_owner.shape[1]
    live = query_len + pairs * passage_rows
    rows = (live // ROW_TILE + 1) * ROW_TILE
    depth = project_weight.shape[0]

    raw = jnp.concatenate([corpus_rows.reshape(-1, features), query_rows[0]], axis=0)
    keep, give = halves(raw, part)
    shared = by_core(keep, partner(give, "c", 1))
    held = shared[:, : stored * passage_rows].reshape(2 * stored, passage_rows, part)
    queries = shared[:, stored * passage_rows :]
    library = lax.all_gather(held, "z", axis=0, tiled=True)

    cells = [(z, q, t) for z in range(SIZE["z"]) for q in range(plane) for t in range(tensors)]
    number = {cell: i for i, cell in enumerate(cells)}
    turn = [(number[(z, q, t)], number[(t, q, z)]) for z, q, t in cells]
    narrow = lax.ppermute(output_weight.T, AXES, turn)
    narrow = narrow.reshape(depth, 2, HEAD_DIM).transpose(1, 0, 2)
    wide = project_weight.reshape(depth, 3, 2, HEAD_DIM).transpose(2, 0, 1, 3)
    wide = wide.reshape(2, depth, 3 * HEAD_DIM)
    weight = gather_plane(jnp.concatenate([wide, narrow], axis=2))

    asked = jnp.concatenate([candidate_owner, candidate_slot], axis=1)
    asked, weight = lax.optimization_barrier((asked, weight))
    weight = lax.all_gather(weight, "z", axis=0, tiled=True)
    asked = lax.all_gather(asked, ("y", "c"), axis=0, tiled=True)
    owner, place = asked[:, :pairs], asked[:, pairs:]
    owner_z, owner_y, owner_c = owner // plane, owner // SIZE["c"] % SIZE["y"], owner % SIZE["c"]
    wanted = ((owner_z * SIZE["c"] + owner_c) * stored + place).reshape(-1)
    outgoing = jnp.take(library, wanted, axis=0, mode="clip")
    arrived = lax.all_to_all(outgoing, "y", split_axis=0, concat_axis=0, tiled=True)

    begin = lax.axis_index("y") * SIZE["c"]
    source = lax.dynamic_slice_in_dim(owner_y, begin, SIZE["c"], axis=0)
    spots = jnp.arange(SIZE["c"] * pairs, dtype=i32).reshape(SIZE["c"], pairs)
    passages = jnp.take(
        arrived, (source * SIZE["c"] * pairs + spots).reshape(-1), axis=0, mode="clip"
    ).reshape(SIZE["c"], pairs, passage_rows, part)
    counts = jnp.take(
        passage_length,
        lax.dynamic_slice_in_dim(owner * stored + place, begin, SIZE["c"], axis=0),
        axis=0,
        mode="clip",
    )
    inside = jnp.arange(passage_rows, dtype=i32) < counts[:, :, None]
    passages = jnp.where(inside[..., None], passages, jnp.zeros((), bf16))
    gain, _ = halves(norm_gain, part)
    packed = jnp.concatenate(
        [
            queries,
            passages.reshape(SIZE["c"], -1, part),
            jnp.broadcast_to(gain, (SIZE["c"], 1, part)),
            jnp.zeros((SIZE["c"], rows - live - 1, part), bf16),
        ],
        axis=1,
    )

    far = partner(packed, "h", 1)
    low = lax.axis_index("h") == 0
    both = jnp.stack([jnp.where(low, packed, far), jnp.where(low, far, packed)])
    spread = jnp.broadcast_to(both[None], (SIZE["x"],) + both.shape)
    near_full = lax.all_to_all(spread, "x", split_axis=0, concat_axis=0, tiled=True)
    far_full = partner(near_full, "c", 1)

    row = jnp.arange(rows, dtype=i32)
    is_query = row < query_len
    slot = jnp.where(is_query, row, query_len + (row - query_len) % passage_rows)
    pair = jnp.where(is_query, -1, (row - query_len) // passage_rows)
    count_of = jnp.concatenate(
        [
            jnp.full((SIZE["c"], query_len), passage_rows, i32),
            jnp.repeat(counts, passage_rows, axis=1),
            jnp.zeros((SIZE["c"], rows - live), i32),
        ],
        axis=1,
    )
    allowed = (slot[None, :] <= slot[:, None])[None] & (
        is_query[None, None, :]
        | (
            (pair[None, :] == pair[:, None])[None]
            & (slot[None, :] < query_len + count_of)[:, None, :]
        )
    )
    half = HEAD_DIM // 2
    frequency = jnp.power(10000.0, -2.0 * jnp.arange(half, dtype=f32) / HEAD_DIM)
    angles = slot.astype(f32)[:, None] * frequency[None, :]
    cosine, sine = jnp.cos(angles), jnp.sin(angles)

    attended = pl.pallas_call(
        functools.partial(attention_kernel, gain_row=live),
        out_shape=jax.ShapeDtypeStruct((SIZE["c"], rows, HEAD_DIM), bf16),
        in_specs=[VMEM] * 6,
        out_specs=VMEM,
        scratch_shapes=[pltpu.VMEM((SIZE["c"] * rows, tensors * features), bf16)],
        compiler_params=pltpu.CompilerParams(vmem_limit_bytes=32 * 1024 * 1024),
        cost_estimate=pl.CostEstimate(
            flops=2 * rows * tensors * features * 6 * HEAD_DIM,
            bytes_accessed=8 * 1024 * 1024,
            transcendentals=2 * rows * rows,
        ),
        name="attention",
    )(
        near_full,
        far_full,
        weight,
        jnp.concatenate([cosine, cosine], axis=1),
        jnp.concatenate([-sine, sine], axis=1),
        allowed.astype(f32),
    )

    spread = jnp.broadcast_to(attended[:, None], (SIZE["c"], tensors, rows, HEAD_DIM))
    heads = lax.all_to_all(
        spread.reshape(-1, rows, HEAD_DIM),
        ("c",) + TENSOR,
        split_axis=0,
        concat_axis=0,
        tiled=True,
    )
    own_out = weight[:, 3 * HEAD_DIM :]
    own_out, _ = lax.optimization_barrier((own_out, attended))
    other_out = partner(own_out, "c", 1)
    core = lax.axis_index("c")
    near_rows = lax.dynamic_index_in_dim(packed, core, axis=0, keepdims=False)
    far_rows = lax.dynamic_slice(
        far_full,
        (lax.axis_index("x"), lax.axis_index("h"), core, 0, 0),
        (1, 1, 1, rows, part),
    ).reshape(rows, part)
    return pl.pallas_call(
        functools.partial(
            output_kernel, query_len=query_len, pairs=pairs, passage_rows=passage_rows
        ),
        out_shape=jax.ShapeDtypeStruct((pairs * (query_len + passage_rows), features), bf16),
        in_specs=[VMEM] * 5,
        out_specs=VMEM,
        compiler_params=pltpu.CompilerParams(vmem_limit_bytes=32 * 1024 * 1024),
        cost_estimate=pl.CostEstimate(
            flops=2 * rows * tensors * 2 * HEAD_DIM * features,
            bytes_accessed=3 * 1024 * 1024,
            transcendentals=0,
        ),
        name="output",
    )(heads, own_out, other_out, near_rows, far_rows)


def solution(mesh):
    fine = Mesh(mesh.devices.reshape([size for _, size in SPLIT]), AXES)
    placed = (
        P(CORPUS, None, TENSOR),
        P(CORPUS, None, TENSOR),
        P(),
        P(CORPUS, None),
        P(CORPUS, None),
        P(TENSOR),
        P(CORPUS, None, TENSOR),
        P(TENSOR, CORPUS),
    )
    return jax.shard_map(
        on_device, mesh=fine, in_specs=placed, out_specs=P(CORPUS, TENSOR), check_vma=False
    )
```

time: 215 us -> 193 us (0.90)
  the two profiles are of different devices: /device:TPU:8 before, /device:TPU:1 now
where the time goes in v3:
time: 193 us; the launch traced here: 192 us
  waiting for transfers between devices  81.7 us (42%)
  starting transfers between devices  57.9 us (30%)
  local copies, waits for them, and re-layouts  16.7 us (9%)
  between operations  13.7 us (7%)
  blocking collectives  10.4 us (5%)
  other arithmetic  6.03 us (3%)
  Pallas kernels  5.52 us (3%)
    ppermute x7, starting transfers between devices, partner(): return lax.ppermute(value, axis, [(i, i ^ bit) for i in range(SIZE[axis])])  41.6 us
    ppermute x7, waiting for transfers between devices, partner(): return lax.ppermute(value, axis, [(i, i ^ bit) for i in range(SIZE[axis])])  24.6 us
    all_to_all x1, waiting for transfers between devices, on_device(): lax.all_to_all(spread, 'x', split_axis=0, concat_axis=0, tiled=True)  20.2 us
    all_to_all x1, waiting for transfers between devices, on_device(): lax.all_to_all(spread.reshape(-1, rows, HEAD_DIM), ('c',) + TENSOR, split...  19.1 us
    all_to_all x1, waiting for transfers between devices, on_device(): lax.all_to_all(outgoing, 'y', split_axis=0, concat_axis=0, tiled=True)  13.8 us
    all_gather x1, blocking collectives, on_device(): asked = lax.all_gather(asked, ('y', 'c'), axis=0, tiled=True)  10.4 us
    all_to_all x1, starting transfers between devices, on_device(): lax.all_to_all(spread.reshape(-1, rows, HEAD_DIM), ('c',) + TENSOR, split...  6.45 us
    unnamed x20, local copies, waits for them, and re-layouts  4.74 us
  transfers between devices with their start and end apart: 13, of which 11 were waited for; matrix products, arithmetic and copies ran while one was open for 7% of the time, Pallas kernels for 0%

profile of v3, /device:TPU:1, one launch (start us, length us, event | category | flops | bytes accessed | tf_op | source)
XLA Modules:
  0.0 192.0 jit_solution(9080385809205727925)
XLA Ops:
  7.6 8.8 %collective-permute-start = (bf16[200,256]{1,0:T(8,128)(2,1)S(1)}, bf16[200,256]{1,0:T(8,128)(2,1)S(1)}, u32[]{:S(2)}, u32[]{:S(2)}) collective-permute-start(bf16[200,256]{1,0:T(8,128)(2,1)S(1)} %broadcast_select_fusion), channel_id=1, source_target_pairs={{0,8},{8,0},{1,9},{9,1},{2,10},{10,2},{3,11},{11,3},{4,12},{12,4},... | collective-permute-start | bytes 307208 | tf_op jit(solution)/shard_map/ppermute | solution.py:96
  19.2 1.4 collective-permute-start.1
  21.8 2.3 %collective-permute-start.2 = (bf16[64,512]{1,0:T(8,128)(2,1)S(1)}, bf16[64,512]{1,0:T(8,128)(2,1)S(1)}, u32[]{:S(2)}, u32[]{:S(2)}) collective-permute-start(bf16[64,512]{1,0:T(8,128)(2,1)S(1)} %select_bitcast_fusion.4), channel_id=1, source_target_pairs={{0,8},{8,0},{1,9},{9,1},{2,10},{10,2},{3,11},{11,3},{4,12},{12,4},... | collective-permute-start | bytes 196616 | tf_op jit(solution)/shard_map/ppermute | solution.py:96
  25.0 1.9 %collective-permute-start.3 = (bf16[2,64,512]{2,1,0:T(8,128)(2,1)S(1)}, bf16[2,64,512]{2,1,0:T(8,128)(2,1)S(1)}, u32[]{:S(2)}, u32[]{:S(2)}) collective-permute-start(bf16[2,64,512]{2,1,0:T(8,128)(2,1)S(1)} %get-tuple-element.20), channel_id=1, source_target_pairs={{0,32},{16,48},{32,0},{48,16},{1,33},{17,49},{33,1},{49,17},{2,34}... | collective-permute-start | bytes 393224 | tf_op jit(solution)/shard_map/ppermute | solution.py:96
  26.9 6.3 %collective-permute-done.3 = bf16[2,64,512]{2,1,0:T(8,128)(2,1)S(1)} collective-permute-done((bf16[2,64,512]{2,1,0:T(8,128)(2,1)S(1)}, bf16[2,64,512]{2,1,0:T(8,128)(2,1)S(1)}, u32[]{:S(2)}, u32[]{:S(2)}) %collective-permute-start.3) | collective-permute-done | bytes 131104 | tf_op jit(solution)/shard_map/ppermute | solution.py:96
  33.2 1.9 %collective-permute-start.4 = (bf16[2,2,64,512]{3,2,1,0:T(8,128)(2,1)S(1)}, bf16[2,2,64,512]{3,2,1,0:T(8,128)(2,1)S(1)}, u32[]{:S(2)}, u32[]{:S(2)}) collective-permute-start(bf16[2,2,64,512]{3,2,1,0:T(8,128)(2,1)S(1)} %pad_maximum_fusion.2), channel_id=1, source_target_pairs={{0,16},{16,0},{32,48},{48,32},{1,17},{17,1},{33,49},{49,33},{2,18}... | collective-permute-start | bytes 786440 | tf_op jit(solution)/shard_map/ppermute | solution.py:96
  35.3 6.6 %collective-permute-done.4 = bf16[2,2,64,512]{3,2,1,0:T(8,128)(2,1)S(1)} collective-permute-done((bf16[2,2,64,512]{3,2,1,0:T(8,128)(2,1)S(1)}, bf16[2,2,64,512]{3,2,1,0:T(8,128)(2,1)S(1)}, u32[]{:S(2)}, u32[]{:S(2)}) %collective-permute-start.4) | collective-permute-done | bytes 262176 | tf_op jit(solution)/shard_map/ppermute | solution.py:96
  43.3 10.4 %all-gather = s32[8,1,16]{2,1,0:T(1,128)S(1)} all-gather(s32[1,1,16]{2,1,0:T(1,128)S(1)} %bitcast.65), channel_id=1, replica_groups=mesh['z'=8,'y'=4,'c'=2,'h'=2,'x'=4] {'y','c'}, dimensions={0}, use_global_device_ids=true | all-gather | bytes 576 | tf_op jit(solution)/shard_map/all_gather | solution.py:162
  53.9 3.9 %all-gather.4.cloned.1.call-done = bf16[128,24,256]{2,1,0:T(8,128)(2,1)} async-done(((bf16[16,24,256]{2,1,0:T(8,128)(2,1)}), bf16[128,24,256]{2,1,0:T(8,128)(2,1)}) %all-gather.4.cloned.1.call-update) | async-done | bytes 1572880 | tf_op jit(solution)/shard_map/all_gather | solution.py:148
  57.8 2.9 %gather_fusion.2 = bf16[64,24,256]{2,1,0:T(8,128)(2,1)} fusion(bf16[128,24,256]{2,1,0:T(8,128)(2,1)} %all-gather.4.cloned.1.call-done, s32[1024]{0:T(1024)S(1)} %pad_clamp_fusion.1), kind=kCustom, calls=%fused_computation.2 | custom fusion | bytes 1573120 | tf_op jit(solution)/shard_map/jit(_take)/gather | solution.py:166
  60.7 4.3 %all-to-all-start = ((bf16[64,24,256]{2,1,0:T(8,128)(2,1)}), bf16[64,24,256]{2,1,0:T(8,128)(2,1)S(1)}, u32[]{:S(2)}, u32[]{:S(2)}) async-start(bf16[64,24,256]{2,1,0:T(8,128)(2,1)} %gather_fusion.2), calls=%async_computation | async-start | bytes 1572864 | tf_op jit(solution)/shard_map/all_to_all | solution.py:167
  66.3 13.8 %all-to-all-done = bf16[64,24,256]{2,1,0:T(8,128)(2,1)S(1)} async-done(((bf16[64,24,256]{2,1,0:T(8,128)(2,1)}), bf16[64,24,256]{2,1,0:T(8,128)(2,1)S(1)}, u32[]{:S(2)}, u32[]{:S(2)}) %all-to-all-start) | async-done | bytes 786464 | tf_op jit(solution)/shard_map/all_to_all | solution.py:167
  81.0 20.1 %collective-permute-start.5 = (bf16[2,208,256]{2,1,0:T(8,128)(2,1)S(1)}, bf16[2,208,256]{2,1,0:T(8,128)(2,1)S(1)}, u32[]{:S(2)}, u32[]{:S(2)}) collective-permute-start(bf16[2,208,256]{2,1,0:T(8,128)(2,1)S(1)} %fusion.2), channel_id=1, source_target_pairs={{0,4},{4,0},{1,5},{5,1},{2,6},{6,2},{3,7},{7,3},{8,12},{12,8},{9,1... | collective-permute-start | bytes 638984 | tf_op jit(solution)/shard_map/ppermute | solution.py:96
  101.1 7.6 %collective-permute-done.5 = bf16[2,208,256]{2,1,0:T(8,128)(2,1)S(1)} collective-permute-done((bf16[2,208,256]{2,1,0:T(8,128)(2,1)S(1)}, bf16[2,208,256]{2,1,0:T(8,128)(2,1)S(1)}, u32[]{:S(2)}, u32[]{:S(2)}) %collective-permute-start.5) | collective-permute-done | bytes 213024 | tf_op jit(solution)/shard_map/ppermute | solution.py:96
  110.2 4.1 %all-to-all-start.1 = ((bf16[4,2,2,208,256]{4,3,2,1,0:T(8,128)(2,1)}), bf16[4,2,2,208,256]{4,3,2,1,0:T(8,128)(2,1)S(1)}, u32[]{:S(2)}, u32[]{:S(2)}) async-start(bf16[4,2,2,208,256]{4,3,2,1,0:T(8,128)(2,1)} %broadcast_in_dim.70), calls=%async_computation.1 | async-start | bytes 3407872 | tf_op jit(solution)/shard_map/all_to_all | solution.py:198
  114.4 20.2 %all-to-all-done.1.near_ref = bf16[4,2,2,208,256]{4,3,2,1,0:T(8,128)(2,1)S(1)} async-done(((bf16[4,2,2,208,256]{4,3,2,1,0:T(8,128)(2,1)}), bf16[4,2,2,208,256]{4,3,2,1,0:T(8,128)(2,1)S(1)}, u32[]{:S(2)}, u32[]{:S(2)}) %all-to-all-start.1) | async-done | bytes 1703968 | tf_op jit(solution)/shard_map/all_to_all | solution.py:198
  134.6 4.6 %collective-permute-start.6 = (bf16[4,2,2,208,256]{4,3,2,1,0:T(8,128)(2,1)S(1)}, bf16[4,2,2,208,256]{4,3,2,1,0:T(8,128)(2,1)S(1)}, u32[]{:S(2)}, u32[]{:S(2)}) collective-permute-start(bf16[4,2,2,208,256]{4,3,2,1,0:T(8,128)(2,1)S(1)} %all-to-all-done.1.near_ref), channel_id=1, source_target_pairs={{0,8},{8,0},{1,9},{9,1},{2,10},{10,2},{3,11},{11,3},{4,12},{12,4},... | collective-permute-start | bytes 5111816 | tf_op jit(solution)/shard_map/ppermute | solution.py:96
  142.5 2.8 %copy-done.1 = bf16[4096,512]{1,0:T(8,128)(2,1)S(1)} copy-done((bf16[4096,512]{1,0:T(8,128)(2,1)S(1)}, bf16[4096,512]{1,0:T(8,128)(2,1)}, u32[]{:S(2)}) %copy-start.1) | copy-done | bytes 4194328
  147.2 3.8 %attention.1 = bf16[2,208,128]{2,1,0:T(8,128)(2,1)S(1)} custom-call(bf16[4,2,2,208,256]{4,3,2,1,0:T(8,128)(2,1)S(1)} %all-to-all-done.1.near_ref, bf16[4,2,2,208,256]{4,3,2,1,0:T(8,128)(2,1)S(1)} %collective-permute-done.6.far_ref, bf16[4096,512]{1,0:T(8,128)(2,1)S(1)} %copy-done.1, f32[208,128]{1,0:T(8,128)S(1)} %get-tuple-element.30.cos_ref, ...), custom_call_target="tpu_custom_call" | custom-call | flops 1308622848 | bytes 8388608 | tf_op jit(solution)/shard_map/attention/pallas_call | solution.py:225
  152.0 6.5 %all-to-all-start.2 = ((bf16[16,208,128]{2,1,0:T(8,128)(2,1)}), bf16[16,208,128]{2,1,0:T(8,128)(2,1)S(1)}, u32[]{:S(2)}, u32[]{:S(2)}) async-start(bf16[16,208,128]{2,1,0:T(8,128)(2,1)} %bitcast.21), calls=%async_computation.2 | async-start | bytes 1703936 | tf_op jit(solution)/shard_map/all_to_all | solution.py:248
  159.8 2.0 %collective-permute-start.7 = (bf16[4096,128]{1,0:T(8,128)(2,1)S(1)}, bf16[4096,128]{1,0:T(8,128)(2,1)S(1)}, u32[]{:S(2)}, u32[]{:S(2)}) collective-permute-start(bf16[4096,128]{1,0:T(8,128)(2,1)S(1)} %slice.58.own_ref), channel_id=1, source_target_pairs={{0,8},{8,0},{1,9},{9,1},{2,10},{10,2},{3,11},{11,3},{4,12},{12,4},... | collective-permute-start | bytes 3145736 | tf_op jit(solution)/shard_map/ppermute | solution.py:96
  162.7 1.6 collective-permute-done.7.other_ref
  164.3 19.1 %all-to-all-done.2.heads_ref = bf16[16,208,128]{2,1,0:T(8,128)(2,1)S(1)} async-done(((bf16[16,208,128]{2,1,0:T(8,128)(2,1)}), bf16[16,208,128]{2,1,0:T(8,128)(2,1)S(1)}, u32[]{:S(2)}, u32[]{:S(2)}) %all-to-all-start.2) | async-done | bytes 852000 | tf_op jit(solution)/shard_map/all_to_all | solution.py:248
  183.4 1.8 output.1
  (88 shorter events, 19.7 us)
Async XLA Ops:
  6.5 58.8 %copy-start = (s32[512]{0:T(512)S(1)}, s32[512]{0:T(512)}, u32[]{:S(2)}) copy-start(s32[512]{0:T(512)} %param.10) | copy-start | bytes 6148
  6.5 51.3 %all-gather.4.cloned.1.call-start = ((), (), s32[]{:S(2)}) async-start(), calls=%async_computation.3 | async-start | bytes 1769472 | tf_op jit(solution)/shard_map/all_gather | solution.py:148
  7.6 27.6 %copy-start.8 = (s32[1,8]{1,0:T(1,128)S(1)}, s32[1,8]{1,0:T(1,128)}, u32[]{:S(2)}) copy-start(s32[1,8]{1,0:T(1,128)} %param.12) | copy-start | bytes 100
  7.6 27.6 %copy-start.9 = (s32[1,8]{1,0:T(1,128)S(1)}, s32[1,8]{1,0:T(1,128)}, u32[]{:S(2)}) copy-start(s32[1,8]{1,0:T(1,128)} %param.11) | copy-start | bytes 100
  7.6 9.7 %collective-permute-start = (bf16[200,256]{1,0:T(8,128)(2,1)S(1)}, bf16[200,256]{1,0:T(8,128)(2,1)S(1)}, u32[]{:S(2)}, u32[]{:S(2)}) collective-permute-start(bf16[200,256]{1,0:T(8,128)(2,1)S(1)} %broadcast_select_fusion), channel_id=1, source_target_pairs={{0,8},{8,0},{1,9},{9,1},{2,10},{10,2},{3,11},{11,3},{4,12},{12,4},... | collective-permute-start | bytes 307208 | tf_op jit(solution)/shard_map/ppermute | solution.py:96
  19.1 123.4 %all-gather.6.cloned.1.call-start = ((), (), s32[]{:S(2)}) async-start(), calls=%async_computation.4 | async-start | bytes 4718592 | tf_op jit(solution)/shard_map/all_gather | solution.py:161
  19.2 2.5 %collective-permute-start.1 = (bf16[64,256]{1,0:T(8,128)(2,1)}, bf16[64,256]{1,0:T(8,128)(2,1)S(1)}, u32[]{:S(2)}, u32[]{:S(2)}) collective-permute-start(bf16[64,256]{1,0:T(8,128)(2,1)} %bitcast.66), channel_id=1, source_target_pairs={{0,0},{1,64},{2,128},{3,192},{4,256},{5,320},{6,384},{7,448},{8,8}... | collective-permute-start | bytes 98312 | tf_op jit(solution)/shard_map/ppermute | solution.py:153
  21.8 3.2 %collective-permute-start.2 = (bf16[64,512]{1,0:T(8,128)(2,1)S(1)}, bf16[64,512]{1,0:T(8,128)(2,1)S(1)}, u32[]{:S(2)}, u32[]{:S(2)}) collective-permute-start(bf16[64,512]{1,0:T(8,128)(2,1)S(1)} %select_bitcast_fusion.4), channel_id=1, source_target_pairs={{0,8},{8,0},{1,9},{9,1},{2,10},{10,2},{3,11},{11,3},{4,12},{12,4},... | collective-permute-start | bytes 196616 | tf_op jit(solution)/shard_map/ppermute | solution.py:96
  25.0 8.2 %collective-permute-start.3 = (bf16[2,64,512]{2,1,0:T(8,128)(2,1)S(1)}, bf16[2,64,512]{2,1,0:T(8,128)(2,1)S(1)}, u32[]{:S(2)}, u32[]{:S(2)}) collective-permute-start(bf16[2,64,512]{2,1,0:T(8,128)(2,1)S(1)} %get-tuple-element.20), channel_id=1, source_target_pairs={{0,32},{16,48},{32,0},{48,16},{1,33},{17,49},{33,1},{49,17},{2,34}... | collective-permute-start | bytes 393224 | tf_op jit(solution)/shard_map/ppermute | solution.py:96
  33.2 8.6 %collective-permute-start.4 = (bf16[2,2,64,512]{3,2,1,0:T(8,128)(2,1)S(1)}, bf16[2,2,64,512]{3,2,1,0:T(8,128)(2,1)S(1)}, u32[]{:S(2)}, u32[]{:S(2)}) collective-permute-start(bf16[2,2,64,512]{3,2,1,0:T(8,128)(2,1)S(1)} %pad_maximum_fusion.2), channel_id=1, source_target_pairs={{0,16},{16,0},{32,48},{48,32},{1,17},{17,1},{33,49},{49,33},{2,18}... | collective-permute-start | bytes 786440 | tf_op jit(solution)/shard_map/ppermute | solution.py:96
  43.3 21.9 %copy-start.7 = (bf16[512]{0:T(512)(128)(2,1)S(1)}, bf16[512]{0:T(512)(128)(2,1)}, u32[]{:S(2)}) copy-start(bf16[512]{0:T(512)(128)(2,1)} %param.13) | copy-start | bytes 3076
  60.7 19.4 %all-to-all-start = ((bf16[64,24,256]{2,1,0:T(8,128)(2,1)}), bf16[64,24,256]{2,1,0:T(8,128)(2,1)S(1)}, u32[]{:S(2)}, u32[]{:S(2)}) async-start(bf16[64,24,256]{2,1,0:T(8,128)(2,1)} %gather_fusion.2), calls=%async_computation | async-start | bytes 1572864 | tf_op jit(solution)/shard_map/all_to_all | solution.py:167
  81.0 20.1 %copy-start.5 = (bf16[2,208,256]{2,1,0:T(8,128)(2,1)}, bf16[2,208,256]{2,1,0:T(8,128)(2,1)S(1)}, u32[]{:S(2)}) copy-start(bf16[2,208,256]{2,1,0:T(8,128)(2,1)S(1)} %fusion.2) | copy-start | bytes 638980
  81.0 27.7 %collective-permute-start.5 = (bf16[2,208,256]{2,1,0:T(8,128)(2,1)S(1)}, bf16[2,208,256]{2,1,0:T(8,128)(2,1)S(1)}, u32[]{:S(2)}, u32[]{:S(2)}) collective-permute-start(bf16[2,208,256]{2,1,0:T(8,128)(2,1)S(1)} %fusion.2), channel_id=1, source_target_pairs={{0,4},{4,0},{1,5},{5,1},{2,6},{6,2},{3,7},{7,3},{8,12},{12,8},{9,1... | collective-permute-start | bytes 638984 | tf_op jit(solution)/shard_map/ppermute | solution.py:96
  110.2 24.4 %all-to-all-start.1 = ((bf16[4,2,2,208,256]{4,3,2,1,0:T(8,128)(2,1)}), bf16[4,2,2,208,256]{4,3,2,1,0:T(8,128)(2,1)S(1)}, u32[]{:S(2)}, u32[]{:S(2)}) async-start(bf16[4,2,2,208,256]{4,3,2,1,0:T(8,128)(2,1)} %broadcast_in_dim.70), calls=%async_computation.1 | async-start | bytes 3407872 | tf_op jit(solution)/shard_map/all_to_all | solution.py:198
  134.6 7.9 %collective-permute-start.6 = (bf16[4,2,2,208,256]{4,3,2,1,0:T(8,128)(2,1)S(1)}, bf16[4,2,2,208,256]{4,3,2,1,0:T(8,128)(2,1)S(1)}, u32[]{:S(2)}, u32[]{:S(2)}) collective-permute-start(bf16[4,2,2,208,256]{4,3,2,1,0:T(8,128)(2,1)S(1)} %all-to-all-done.1.near_ref), channel_id=1, source_target_pairs={{0,8},{8,0},{1,9},{9,1},{2,10},{10,2},{3,11},{11,3},{4,12},{12,4},... | collective-permute-start | bytes 5111816 | tf_op jit(solution)/shard_map/ppermute | solution.py:96
  142.5 8.5 %copy-start.2 = (bf16[4,2,2,208,256]{4,3,2,1,0:T(8,128)(2,1)}, bf16[4,2,2,208,256]{4,3,2,1,0:T(8,128)(2,1)S(1)}, u32[]{:S(2)}) copy-start(bf16[4,2,2,208,256]{4,3,2,1,0:T(8,128)(2,1)S(1)} %collective-permute-done.6.far_ref) | copy-start | bytes 5111812
  142.5 2.8 %copy-start.1 = (bf16[4096,512]{1,0:T(8,128)(2,1)S(1)}, bf16[4096,512]{1,0:T(8,128)(2,1)}, u32[]{:S(2)}) copy-start(bf16[4096,512]{1,0:T(8,128)(2,1)} %all-gather.6.cloned.1.call-done.weight_ref) | copy-start | bytes 12582916
  145.3 1.0 copy-start.3
  146.3 0.9 copy-start.4
  152.0 9.8 %copy-start.6 = (bf16[2,208,256]{2,1,0:T(8,128)(2,1)S(1)}, bf16[2,208,256]{2,1,0:T(8,128)(2,1)}, u32[]{:S(2)}) copy-start(bf16[2,208,256]{2,1,0:T(8,128)(2,1)} %copy-done.5) | copy-start | bytes 638980
  152.0 31.4 %all-to-all-start.2 = ((bf16[16,208,128]{2,1,0:T(8,128)(2,1)}), bf16[16,208,128]{2,1,0:T(8,128)(2,1)S(1)}, u32[]{:S(2)}, u32[]{:S(2)}) async-start(bf16[16,208,128]{2,1,0:T(8,128)(2,1)} %bitcast.21), calls=%async_computation.2 | async-start | bytes 1703936 | tf_op jit(solution)/shard_map/all_to_all | solution.py:248
  159.8 4.6 %collective-permute-start.7 = (bf16[4096,128]{1,0:T(8,128)(2,1)S(1)}, bf16[4096,128]{1,0:T(8,128)(2,1)S(1)}, u32[]{:S(2)}, u32[]{:S(2)}) collective-permute-start(bf16[4096,128]{1,0:T(8,128)(2,1)S(1)} %slice.58.own_ref), channel_id=1, source_target_pairs={{0,8},{8,0},{1,9},{9,1},{2,10},{10,2},{3,11},{11,3},{4,12},{12,4},... | collective-permute-start | bytes 3145736 | tf_op jit(solution)/shard_map/ppermute | solution.py:96
Sparse Core Ops, SparseCore 0:
  19.3 38.5 all-gather.3
  59.9 60.3 all-gather.5

commit v4 on v3

v4 whole, which is shorter than its diff:
```python
import functools

import jax
import jax.numpy as jnp
import numpy as np
from jax import lax
from jax.experimental import pallas as pl
from jax.experimental.pallas import tpu as pltpu
from jax.sharding import Mesh, PartitionSpec as P

HEAD_DIM = 128
ROW_TILE = 16
SPLIT = (("z", 8), ("y", 4), ("c", 2), ("h", 2), ("x", 4))
SIZE = dict(SPLIT)
AXES = tuple(name for name, _ in SPLIT)
CORPUS = ("z", "y", "c")
TENSOR = ("h", "x")
VMEM = pl.BlockSpec(memory_space=pltpu.VMEM)
SMEM = pl.BlockSpec(memory_space=pltpu.SMEM)
ANY = pl.BlockSpec(memory_space=pl.ANY)
LIMIT = 32 * 1024 * 1024
WEIGHT_PARTS = 4


def pick_kernel(index_ref, library_ref, *out_refs):
    count = out_refs[0].shape[0]
    for block, out_ref in enumerate(out_refs):
        for i in range(count):
            out_ref[i] = library_ref[index_ref[block * count + i]]


def pack_kernel(source_ref, count_ref, *refs):
    f32 = jnp.float32
    part_refs, (query_ref, gain_ref, packed_ref, spread_ref) = refs[:-4], refs[-4:]
    groups, rows, part = packed_ref.shape
    passage_rows = part_refs[0].shape[1]
    pairs = part_refs[0].shape[0] // groups
    place = lax.broadcasted_iota(jnp.int32, (passage_rows, part), 0)
    for group in range(groups):
        blocks = [query_ref[group].astype(f32)]
        for pair in range(pairs):
            spot = group * pairs + pair
            source = source_ref[spot]
            passage = part_refs[0][spot].astype(f32)
            for k in range(1, len(part_refs)):
                passage = jnp.where(source == k, part_refs[k][spot].astype(f32), passage)
            blocks.append(jnp.where(place < count_ref[spot], passage, 0.0))
        filled = blocks[0].shape[0] + pairs * passage_rows
        blocks.append(jnp.broadcast_to(gain_ref[...].astype(f32), (rows - filled, part)))
        value = jnp.concatenate(blocks, axis=0).astype(packed_ref.dtype)
        packed_ref[group] = value
        for x in range(spread_ref.shape[0]):
            spread_ref[x, group] = value


def attention_kernel(
    count_ref, own_ref, far_ref, own_swap_ref, far_swap_ref, weight_ref, cos_ref, sin_ref,
    out_ref, normed_ref, held_ref, semaphores, *, query_len, passage_rows,
):
    bf16, f32, i32 = jnp.bfloat16, jnp.float32, jnp.int32
    spread, groups, rows, part = own_ref.shape
    width = 4 * spread * part
    pairs = count_ref.shape[0] // groups
    gain_row = query_len + pairs * passage_rows
    depth = held_ref.shape[0] // WEIGHT_PARTS
    copies = []
    for i in range(WEIGHT_PARTS):
        block = pl.ds(i * depth, depth)
        copies.append(
            pltpu.make_async_copy(
                weight_ref.at[block, pl.ds(0, held_ref.shape[1])],
                held_ref.at[block],
                semaphores.at[i],
            )
        )
        copies[-1].start()
    core, high = lax.axis_index("c"), lax.axis_index("h")
    quarters = (
        (own_ref, high, core),
        (far_ref, 1 - high, core),
        (own_swap_ref, high, 1 - core),
        (far_swap_ref, 1 - high, 1 - core),
    )
    for group in range(groups):
        total = jnp.zeros((rows, HEAD_DIM), f32)
        for ref, _, _ in quarters:
            for x in range(spread):
                chunk = ref[x, group].astype(f32)
                square = chunk * chunk
                for lane in range(0, part, HEAD_DIM):
                    total = total + square[:, lane : lane + HEAD_DIM]
        inverse = lax.rsqrt(jnp.sum(total, axis=1, keepdims=True) / width + 1e-05)
        for ref, upper, half in quarters:
            for x in range(spread):
                chunk = ref[x, group].astype(f32)
                gain = chunk[gain_row : gain_row + 1, :]
                begin = pl.multiple_of(((upper * spread + x) * 2 + half) * part, part)
                normed_ref[group * rows : (group + 1) * rows, pl.ds(begin, part)] = (
                    chunk * inverse * gain
                ).astype(bf16)
    projected = None
    for i in range(WEIGHT_PARTS):
        copies[i].wait()
        block = slice(i * depth, (i + 1) * depth)
        product = jnp.dot(normed_ref[:, block], held_ref[block], preferred_element_type=f32)
        projected = product if projected is None else projected + product

    def rotate(inputs):
        return (
            inputs * cos_ref[...] + pltpu.roll(inputs, HEAD_DIM // 2, 1) * sin_ref[...]
        ).astype(bf16)

    def pair_of(row):
        pair = jnp.full(row.shape, -1, i32)
        for k in range(pairs + 1):
            pair = jnp.where(row >= query_len + k * passage_rows, k, pair)
        return pair

    query_row = lax.broadcasted_iota(i32, (rows, 1), 0)
    key_row = lax.broadcasted_iota(i32, (1, rows), 1)
    query_pair, key_pair = pair_of(query_row), pair_of(key_row)
    for group in range(groups):
        end = jnp.full((1, rows), query_len, i32)
        for k in range(pairs):
            last = query_len + k * passage_rows + count_ref[group * pairs + k]
            end = jnp.where(key_pair == k, last, end)
        key_live = jnp.where(key_row < end, key_pair, -2)
        allowed = (key_row <= query_row) & ((key_live == -1) | (key_live == query_pair))
        mine = projected[group * rows : (group + 1) * rows]
        queries = rotate(mine[:, :HEAD_DIM])
        keys = rotate(mine[:, HEAD_DIM : 2 * HEAD_DIM])
        values = mine[:, 2 * HEAD_DIM :].astype(bf16)
        scores = lax.dot_general(
            queries, keys, (((1,), (1,)), ((), ())), preferred_element_type=f32
        ) * (1.0 / float(HEAD_DIM) ** 0.5)
        scores = jnp.where(allowed, scores, -1e30)
        exponent = jnp.exp(scores - jnp.max(scores, axis=-1, keepdims=True))
        weights = (exponent / jnp.sum(exponent, axis=-1, keepdims=True)).astype(bf16)
        attended = jnp.dot(weights, values, preferred_element_type=f32).astype(bf16)
        for t in range(out_ref.shape[1]):
            out_ref[group, t] = attended


def output_kernel(heads_ref, own_ref, other_ref, near_ref, far_ref, out_ref, *, query_len, pairs, passage_rows):
    bf16, f32 = jnp.bfloat16, jnp.float32
    core = lax.axis_index("c")
    numbers = (((1,), (1,)), ((), ()))
    tensors = heads_ref.shape[0] // 2
    columns = own_ref.shape[0] // tensors
    near, far = near_ref[...], far_ref[...]
    first = core == 0
    final = jnp.concatenate(
        [jnp.where(first, near, far), jnp.where(first, far, near)], axis=1
    ).astype(f32)
    summed = jnp.zeros(final.shape, f32)
    for t in range(tensors):
        block = slice(t * columns, (t + 1) * columns)
        partial_value = lax.dot_general(
            heads_ref[core * tensors + t], own_ref[block], numbers, preferred_element_type=f32
        ) + lax.dot_general(
            heads_ref[(1 - core) * tensors + t], other_ref[block], numbers, preferred_element_type=f32
        )
        summed = summed + partial_value.astype(bf16).astype(f32)
    final = final + summed
    blocks = []
    for pair in range(pairs):
        begin = query_len + pair * passage_rows
        blocks += [final[:query_len], final[begin : begin + passage_rows]]
    out_ref[...] = jnp.concatenate(blocks, axis=0).astype(bf16)


def partner(value, axis, bit):
    return lax.ppermute(value, axis, [(i, i ^ bit) for i in range(SIZE[axis])])


def by_core(mine, got):
    first = lax.axis_index("c") == 0
    return jnp.stack([jnp.where(first, mine, got), jnp.where(first, got, mine)])


def halves(value, part):
    first = lax.axis_index("c") == 0
    low, high = value[..., :part], value[..., part:]
    return jnp.where(first, low, high), jnp.where(first, high, low)


def gather_plane(blocks):
    first = lax.axis_index("c") == 0
    keep = jnp.where(first, blocks[0], blocks[1])
    got = partner(jnp.where(first, blocks[1], blocks[0]), "c", 1)
    pair = by_core(keep, got)
    four = jnp.stack([pair] + [partner(pair, "y", k) for k in range(1, SIZE["y"])])
    return jnp.take(four, other_y(), axis=0, mode="clip")


def other_y():
    return jnp.arange(SIZE["y"], dtype=jnp.int32) ^ lax.axis_index("y")


def on_every(value, axis):
    spread = jnp.broadcast_to(value[None], (SIZE[axis],) + value.shape)
    return lax.all_to_all(spread, axis, split_axis=0, concat_axis=0, tiled=True)


def on_device(
    query_rows,
    corpus_rows,
    passage_length,
    candidate_owner,
    candidate_slot,
    norm_gain,
    project_weight,
    output_weight,
):
    bf16, f32, i32 = jnp.bfloat16, jnp.float32, jnp.int32
    cores, lines = SIZE["c"], SIZE["y"]
    plane = lines * cores
    tensors = SIZE["h"] * SIZE["x"]
    stored, passage_rows, features = corpus_rows.shape
    part = features // 2
    query_len = query_rows.shape[1]
    pairs = candidate_owner.shape[1]
    live = query_len + pairs * passage_rows
    rows = (live // ROW_TILE + 1) * ROW_TILE
    depth = project_weight.shape[0]
    options = pltpu.CompilerParams(vmem_limit_bytes=LIMIT)

    raw = jnp.concatenate([corpus_rows.reshape(-1, features), query_rows[0]], axis=0)
    keep, give = halves(raw, part)
    shared = by_core(keep, partner(give, "c", 1))
    held = shared[:, : stored * passage_rows].reshape(2 * stored, passage_rows, part)
    queries = shared[:, stored * passage_rows :]
    library = on_every(held, "z").reshape(-1, passage_rows, part)

    cells = [(z, q, t) for z in range(SIZE["z"]) for q in range(plane) for t in range(tensors)]
    number = {cell: i for i, cell in enumerate(cells)}
    turn = [(number[(z, q, t)], number[(t, q, z)]) for z, q, t in cells]
    narrow = lax.ppermute(output_weight.T, AXES, turn)
    narrow = narrow.reshape(depth, 2, HEAD_DIM).transpose(1, 0, 2)
    wide = project_weight.reshape(depth, 3, 2, HEAD_DIM).transpose(2, 0, 1, 3)
    wide = wide.reshape(2, depth, 3 * HEAD_DIM)
    asked = jnp.concatenate([candidate_owner, candidate_slot], axis=1).astype(bf16)
    asked = jnp.pad(asked, ((0, 7), (0, 4 * HEAD_DIM - 2 * pairs)))
    weight = jnp.concatenate([wide, narrow], axis=2)
    weight = jnp.concatenate([weight, jnp.broadcast_to(asked, (2,) + asked.shape)], axis=1)
    weight = gather_plane(weight)
    asked = weight[:, :, depth, : 2 * pairs].astype(i32)
    weight = weight[:, :, :depth].reshape(plane * depth, 4 * HEAD_DIM)
    weight = lax.all_gather(weight, "z", axis=0, tiled=True)

    owner, place = asked[:, :, :pairs], asked[:, :, pairs:]
    owner_z, owner_y, owner_c = owner // plane, owner // cores % lines, owner % cores
    wanted = (owner_z * cores + owner_c) * stored + place
    wanted = jnp.take(wanted, other_y(), axis=0, mode="clip").reshape(-1)
    block = jax.ShapeDtypeStruct((cores * pairs, passage_rows, part), bf16)
    outgoing = pl.pallas_call(
        pick_kernel,
        out_shape=[block] * lines,
        in_specs=[SMEM, VMEM],
        out_specs=[VMEM] * lines,
        compiler_params=options,
        name="pick",
    )(wanted, library)
    arrived = [outgoing[0]] + [partner(outgoing[k], "y", k) for k in range(1, lines)]

    here = lax.axis_index("y")
    source = lax.dynamic_index_in_dim(owner_y, here, axis=0, keepdims=False) ^ here
    stored_at = lax.dynamic_index_in_dim(owner * stored + place, here, axis=0, keepdims=False)
    counts = jnp.take(passage_length, stored_at.reshape(-1), axis=0, mode="clip")
    gain, _ = halves(norm_gain[None], part)
    packed, spread = pl.pallas_call(
        pack_kernel,
        out_shape=[
            jax.ShapeDtypeStruct((cores, rows, part), bf16),
            jax.ShapeDtypeStruct((SIZE["x"], cores, rows, part), bf16),
        ],
        in_specs=[SMEM] * 2 + [VMEM] * (lines + 2),
        out_specs=[VMEM] * 2,
        compiler_params=options,
        name="pack",
    )(source.reshape(-1), counts, *arrived, queries, gain)

    own_full = lax.all_to_all(spread, "x", split_axis=0, concat_axis=0, tiled=True)
    far_full = on_every(partner(packed, "h", 1), "x")
    own_swap = partner(own_full, "c", 1)
    far_swap = partner(far_full, "c", 1)

    row = np.arange(rows)
    slot = np.where(row < query_len, row, query_len + (row - query_len) % passage_rows)
    half = HEAD_DIM // 2
    frequency = np.power(10000.0, -2.0 * np.arange(half) / HEAD_DIM).astype(np.float32)
    angles = slot.astype(np.float32)[:, None] * frequency[None, :]
    cosine, sine = np.cos(angles), np.sin(angles)
    attended = pl.pallas_call(
        functools.partial(attention_kernel, query_len=query_len, passage_rows=passage_rows),
        out_shape=jax.ShapeDtypeStruct((cores, tensors, rows, HEAD_DIM), bf16),
        in_specs=[SMEM] + [VMEM] * 4 + [ANY] + [VMEM] * 2,
        out_specs=VMEM,
        scratch_shapes=[
            pltpu.VMEM((cores * rows, tensors * features), bf16),
            pltpu.VMEM((weight.shape[0], 3 * HEAD_DIM), bf16),
            pltpu.SemaphoreType.DMA((WEIGHT_PARTS,)),
        ],
        compiler_params=options,
        cost_estimate=pl.CostEstimate(
            flops=2 * rows * tensors * features * 6 * HEAD_DIM,
            bytes_accessed=8 * 1024 * 1024,
            transcendentals=2 * rows * rows,
        ),
        name="attention",
    )(
        counts,
        own_full,
        far_full,
        own_swap,
        far_swap,
        weight,
        jnp.asarray(np.concatenate([cosine, cosine], axis=1), f32),
        jnp.asarray(np.concatenate([-sine, sine], axis=1), f32),
    )

    heads = lax.all_to_all(
        attended.reshape(-1, rows, HEAD_DIM),
        ("c",) + TENSOR,
        split_axis=0,
        concat_axis=0,
        tiled=True,
    )
    own_out = weight[:, 3 * HEAD_DIM :]
    own_out, _ = lax.optimization_barrier((own_out, attended))
    other_out = partner(own_out, "c", 1)
    core = lax.axis_index("c")
    near_rows = lax.dynamic_index_in_dim(packed, core, axis=0, keepdims=False)
    far_rows = lax.dynamic_slice(
        own_swap, (lax.axis_index("x"), core, 0, 0), (1, 1, rows, part)
    ).reshape(rows, part)
    return pl.pallas_call(
        functools.partial(
            output_kernel, query_len=query_len, pairs=pairs, passage_rows=passage_rows
        ),
        out_shape=jax.ShapeDtypeStruct((pairs * (query_len + passage_rows), features), bf16),
        in_specs=[VMEM] * 5,
        out_specs=VMEM,
        compiler_params=options,
        cost_estimate=pl.CostEstimate(
            flops=2 * rows * tensors * 2 * HEAD_DIM * features,
            bytes_accessed=3 * 1024 * 1024,
            transcendentals=0,
        ),
        name="output",
    )(heads, own_out, other_out, near_rows, far_rows)


def solution(mesh):
    fine = Mesh(mesh.devices.reshape([size for _, size in SPLIT]), AXES)
    placed = (
        P(CORPUS, None, TENSOR),
        P(CORPUS, None, TENSOR),
        P(),
        P(CORPUS, None),
        P(CORPUS, None),
        P(TENSOR),
        P(CORPUS, None, TENSOR),
        P(TENSOR, CORPUS),
    )
    return jax.shard_map(
        on_device, mesh=fine, in_specs=placed, out_specs=P(CORPUS, TENSOR), check_vma=False
    )
```

time: 193 us -> 234 us (1.21)
  the two profiles are of different devices: /device:TPU:1 before, /device:TPU:17 now
where the time goes in v4:
time: 234 us; the launch traced here: 233 us
  waiting for transfers between devices  119 us (51%)
  starting transfers between devices  75.7 us (32%)
  between operations  13.8 us (6%)
  local copies, waits for them, and re-layouts  11.9 us (5%)
  Pallas kernels  11.5 us (5%)
    all_to_all x2, waiting for transfers between devices, on_every(): return lax.all_to_all(spread, axis, split_axis=0, concat_axis=0, tiled=True)  62.1 us
    ppermute x12, starting transfers between devices, partner(): return lax.ppermute(value, axis, [(i, i ^ bit) for i in range(SIZE[axis])])  42.5 us
    ppermute x12, waiting for transfers between devices, partner(): return lax.ppermute(value, axis, [(i, i ^ bit) for i in range(SIZE[axis])])  36.5 us
    all_to_all x2, starting transfers between devices, on_every(): return lax.all_to_all(spread, axis, split_axis=0, concat_axis=0, tiled=True)  22.6 us
    all_to_all x1, waiting for transfers between devices, on_device(): lax.all_to_all(attended.reshape(-1, rows, HEAD_DIM), ('c',) + TENSOR, spl...  20 us
    pallas_call x1, Pallas kernels, on_device(): pl.pallas_call(functools.partial(attention_kernel, query_len=query_len, p...  6.26 us
    all_to_all x1, starting transfers between devices, on_device(): lax.all_to_all(attended.reshape(-1, rows, HEAD_DIM), ('c',) + TENSOR, spl...  5.01 us
  transfers between devices with their start and end apart: 18, of which 12 were waited for; matrix products, arithmetic and copies ran while one was open for 3% of the time, Pallas kernels for 1%

profile of v4, /device:TPU:17, one launch (start us, length us, event | category | flops | bytes accessed | tf_op | source)
XLA Modules:
  0.0 233.3 jit_solution(12963520517994357435)
XLA Ops:
  10.7 2.6 %collective-permute-start.1 = (bf16[72,512]{1,0:T(8,128)(2,1)S(1)}, bf16[72,512]{1,0:T(8,128)(2,1)S(1)}, u32[]{:S(2)}, u32[]{:S(2)}) collective-permute-start(bf16[72,512]{1,0:T(8,128)(2,1)S(1)} %select_bitcast_fusion.2), channel_id=1, source_target_pairs={{0,8},{8,0},{1,9},{9,1},{2,10},{10,2},{3,11},{11,3},{4,12},{12,4},... | collective-permute-start | bytes 221192 | tf_op jit(solution)/shard_map/ppermute | solution.py:173
  16.3 8.4 %collective-permute-start.2 = (bf16[2,72,512]{2,1,0:T(8,128)(2,1)S(1)}, bf16[2,72,512]{2,1,0:T(8,128)(2,1)S(1)}, u32[]{:S(2)}, u32[]{:S(2)}) collective-permute-start(bf16[2,72,512]{2,1,0:T(8,128)(2,1)S(1)} %get-tuple-element.26), channel_id=1, source_target_pairs={{0,16},{16,0},{32,48},{48,32},{1,17},{17,1},{33,49},{49,33},{2,18}... | collective-permute-start | bytes 442376 | tf_op jit(solution)/shard_map/ppermute | solution.py:173
  26.6 3.6 %collective-permute-done.2 = bf16[2,72,512]{2,1,0:T(8,128)(2,1)S(1)} collective-permute-done((bf16[2,72,512]{2,1,0:T(8,128)(2,1)S(1)}, bf16[2,72,512]{2,1,0:T(8,128)(2,1)S(1)}, u32[]{:S(2)}, u32[]{:S(2)}) %collective-permute-start.2) | collective-permute-done | bytes 147488 | tf_op jit(solution)/shard_map/ppermute | solution.py:173
  33.6 3.7 %collective-permute-start.5 = (bf16[200,256]{1,0:T(8,128)(2,1)S(1)}, bf16[200,256]{1,0:T(8,128)(2,1)S(1)}, u32[]{:S(2)}, u32[]{:S(2)}) collective-permute-start(bf16[200,256]{1,0:T(8,128)(2,1)S(1)} %broadcast_select_fusion), channel_id=1, source_target_pairs={{0,8},{8,0},{1,9},{9,1},{2,10},{10,2},{3,11},{11,3},{4,12},{12,4},... | collective-permute-start | bytes 307208 | tf_op jit(solution)/shard_map/ppermute | solution.py:173
  39.6 18.6 %all-to-all-start = ((bf16[8,16,24,256]{3,2,1,0:T(8,128)(2,1)}), bf16[8,16,24,256]{3,2,1,0:T(8,128)(2,1)S(1)}, u32[]{:S(2)}, u32[]{:S(2)}) async-start(bf16[8,16,24,256]{3,2,1,0:T(8,128)(2,1)} %broadcast_in_dim.30), calls=%async_computation | async-start | bytes 3145728 | tf_op jit(solution)/shard_map/all_to_all | solution.py:202
  59.2 56.1 %all-to-all-done = bf16[8,16,24,256]{3,2,1,0:T(8,128)(2,1)S(1)} async-done(((bf16[8,16,24,256]{3,2,1,0:T(8,128)(2,1)}), bf16[8,16,24,256]{3,2,1,0:T(8,128)(2,1)S(1)}, u32[]{:S(2)}, u32[]{:S(2)}) %all-to-all-start) | async-done | bytes 1572896 | tf_op jit(solution)/shard_map/all_to_all | solution.py:202
  115.9 3.7 %collective-permute-start.6 = (bf16[16,24,256]{2,1,0:T(8,128)(2,1)S(1)}, bf16[16,24,256]{2,1,0:T(8,128)(2,1)S(1)}, u32[]{:S(2)}, u32[]{:S(2)}) collective-permute-start(bf16[16,24,256]{2,1,0:T(8,128)(2,1)S(1)} %get-tuple-element.13), channel_id=1, source_target_pairs={{0,16},{16,0},{32,48},{48,32},{1,17},{17,1},{33,49},{49,33},{2,18}... | collective-permute-start | bytes 589832 | tf_op jit(solution)/shard_map/ppermute | solution.py:173
  119.7 3.0 %collective-permute-start.7 = (bf16[16,24,256]{2,1,0:T(8,128)(2,1)S(1)}, bf16[16,24,256]{2,1,0:T(8,128)(2,1)S(1)}, u32[]{:S(2)}, u32[]{:S(2)}) collective-permute-start(bf16[16,24,256]{2,1,0:T(8,128)(2,1)S(1)} %get-tuple-element.14), channel_id=1, source_target_pairs={{0,32},{16,48},{32,0},{48,16},{1,33},{17,49},{33,1},{49,17},{2,34}... | collective-permute-start | bytes 589832 | tf_op jit(solution)/shard_map/ppermute | solution.py:173
  122.7 2.2 collective-permute-start.8
  125.6 8.9 %collective-permute-done.7.refs_2_ = bf16[16,24,256]{2,1,0:T(8,128)(2,1)S(1)} collective-permute-done((bf16[16,24,256]{2,1,0:T(8,128)(2,1)S(1)}, bf16[16,24,256]{2,1,0:T(8,128)(2,1)S(1)}, u32[]{:S(2)}, u32[]{:S(2)}) %collective-permute-start.7) | collective-permute-done | bytes 196640 | tf_op jit(solution)/shard_map/ppermute | solution.py:173
  134.6 5.1 %collective-permute-done.8.refs_3_ = bf16[16,24,256]{2,1,0:T(8,128)(2,1)S(1)} collective-permute-done((bf16[16,24,256]{2,1,0:T(8,128)(2,1)S(1)}, bf16[16,24,256]{2,1,0:T(8,128)(2,1)S(1)}, u32[]{:S(2)}, u32[]{:S(2)}) %collective-permute-start.8) | collective-permute-done | bytes 196640 | tf_op jit(solution)/shard_map/ppermute | solution.py:173
  141.3 4.1 %all-to-all-start.1 = ((bf16[4,2,208,256]{3,2,1,0:T(8,128)(2,1)}), bf16[4,2,208,256]{3,2,1,0:T(8,128)(2,1)S(1)}, u32[]{:S(2)}, u32[]{:S(2)}) async-start(bf16[4,2,208,256]{3,2,1,0:T(8,128)(2,1)} %get-tuple-element.16), calls=%async_computation.1 | async-start | bytes 1703936 | tf_op jit(solution)/shard_map/all_to_all | solution.py:283
  145.4 3.0 %collective-permute-start.9 = (bf16[2,208,256]{2,1,0:T(8,128)(2,1)S(1)}, bf16[2,208,256]{2,1,0:T(8,128)(2,1)S(1)}, u32[]{:S(2)}, u32[]{:S(2)}) collective-permute-start(bf16[2,208,256]{2,1,0:T(8,128)(2,1)S(1)} %get-tuple-element.17), channel_id=1, source_target_pairs={{0,4},{4,0},{1,5},{5,1},{2,6},{6,2},{3,7},{7,3},{8,12},{12,8},{9,1... | collective-permute-start | bytes 638984 | tf_op jit(solution)/shard_map/ppermute | solution.py:173
  148.4 10.7 %collective-permute-done.9 = bf16[2,208,256]{2,1,0:T(8,128)(2,1)S(1)} collective-permute-done((bf16[2,208,256]{2,1,0:T(8,128)(2,1)S(1)}, bf16[2,208,256]{2,1,0:T(8,128)(2,1)S(1)}, u32[]{:S(2)}, u32[]{:S(2)}) %collective-permute-start.9) | collective-permute-done | bytes 213024 | tf_op jit(solution)/shard_map/ppermute | solution.py:173
  160.1 4.0 %all-to-all-start.2 = ((bf16[4,2,208,256]{3,2,1,0:T(8,128)(2,1)}), bf16[4,2,208,256]{3,2,1,0:T(8,128)(2,1)S(1)}, u32[]{:S(2)}, u32[]{:S(2)}) async-start(bf16[4,2,208,256]{3,2,1,0:T(8,128)(2,1)} %broadcast_in_dim.32), calls=%async_computation.2 | async-start | bytes 1703936 | tf_op jit(solution)/shard_map/all_to_all | solution.py:202
  164.0 4.3 %collective-permute-start.10 = (bf16[4,2,208,256]{3,2,1,0:T(8,128)(2,1)S(1)}, bf16[4,2,208,256]{3,2,1,0:T(8,128)(2,1)S(1)}, u32[]{:S(2)}, u32[]{:S(2)}) collective-permute-start(bf16[4,2,208,256]{3,2,1,0:T(8,128)(2,1)S(1)} %all-to-all-done.1.own_ref), channel_id=1, source_target_pairs={{0,8},{8,0},{1,9},{9,1},{2,10},{10,2},{3,11},{11,3},{4,12},{12,4},... | collective-permute-start | bytes 2555912 | tf_op jit(solution)/shard_map/ppermute | solution.py:173
  168.4 5.9 %all-to-all-done.2.far_ref = bf16[4,2,208,256]{3,2,1,0:T(8,128)(2,1)S(1)} async-done(((bf16[4,2,208,256]{3,2,1,0:T(8,128)(2,1)}), bf16[4,2,208,256]{3,2,1,0:T(8,128)(2,1)S(1)}, u32[]{:S(2)}, u32[]{:S(2)}) %all-to-all-start.2) | async-done | bytes 852000 | tf_op jit(solution)/shard_map/all_to_all | solution.py:202
  174.3 5.6 %collective-permute-start.11 = (bf16[4,2,208,256]{3,2,1,0:T(8,128)(2,1)S(1)}, bf16[4,2,208,256]{3,2,1,0:T(8,128)(2,1)S(1)}, u32[]{:S(2)}, u32[]{:S(2)}) collective-permute-start(bf16[4,2,208,256]{3,2,1,0:T(8,128)(2,1)S(1)} %all-to-all-done.2.far_ref), channel_id=1, source_target_pairs={{0,8},{8,0},{1,9},{9,1},{2,10},{10,2},{3,11},{11,3},{4,12},{12,4},... | collective-permute-start | bytes 2555912 | tf_op jit(solution)/shard_map/ppermute | solution.py:173
  182.8 2.2 copy-done.1
  186.2 6.3 %attention.1 = bf16[2,8,208,128]{3,2,1,0:T(8,128)(2,1)} custom-call(s32[16]{0:T(128)S(1)} %gather_fusion.1, bf16[4,2,208,256]{3,2,1,0:T(8,128)(2,1)S(1)} %all-to-all-done.1.own_ref, bf16[4,2,208,256]{3,2,1,0:T(8,128)(2,1)S(1)} %all-to-all-done.2.far_ref, bf16[4,2,208,256]{3,2,1,0:T(8,128)(2,1)S(1)} %collective-permute-done.10.own_swap_ref, ...), custom_call_target="tpu_custom_call" | custom-call | flops 1308622848 | bytes 8388608 | tf_op jit(solution)/shard_map/attention/pallas_call | solution.py:294
  192.4 5.0 %all-to-all-start.3 = ((bf16[16,208,128]{2,1,0:T(8,128)(2,1)}), bf16[16,208,128]{2,1,0:T(8,128)(2,1)S(1)}, u32[]{:S(2)}, u32[]{:S(2)}) async-start(bf16[16,208,128]{2,1,0:T(8,128)(2,1)} %bitcast.20), calls=%async_computation.3 | async-start | bytes 1703936 | tf_op jit(solution)/shard_map/all_to_all | solution.py:322
  200.8 2.6 %collective-permute-done.12.other_ref = bf16[4096,128]{1,0:T(8,128)(2,1)} collective-permute-done((bf16[4096,128]{1,0:T(8,128)(2,1)S(1)}, bf16[4096,128]{1,0:T(8,128)(2,1)}, u32[]{:S(2)}, u32[]{:S(2)}) %collective-permute-start.12) | collective-permute-done | bytes 1048608 | tf_op jit(solution)/shard_map/ppermute | solution.py:173
  203.4 20.0 %all-to-all-done.3.heads_ref = bf16[16,208,128]{2,1,0:T(8,128)(2,1)S(1)} async-done(((bf16[16,208,128]{2,1,0:T(8,128)(2,1)}), bf16[16,208,128]{2,1,0:T(8,128)(2,1)S(1)}, u32[]{:S(2)}, u32[]{:S(2)}) %all-to-all-start.3) | async-done | bytes 852000 | tf_op jit(solution)/shard_map/all_to_all | solution.py:322
  223.5 3.0 %output.1 = bf16[256,512]{1,0:T(8,128)(2,1)} custom-call(bf16[16,208,128]{2,1,0:T(8,128)(2,1)S(1)} %all-to-all-done.3.heads_ref, bf16[4096,128]{1,0:T(8,128)(2,1)S(1)} %slice.72.own_ref, bf16[4096,128]{1,0:T(8,128)(2,1)} %collective-permute-done.12.other_ref, bf16[208,256]{1,0:T(8,128)(2,1)S(1)} %dynamic-slice_bitcast_fusion.1.near_ref, ...), custom_call_target="tpu_custom_call" | custom-call | flops 436207616 | bytes 3145728 | tf_op jit(solution)/shard_map/output/pallas_call | solution.py:337
  (75 shorter events, 27.0 us)
Async XLA Ops:
  6.5 118.4 %copy-start = (s32[512]{0:T(512)S(1)}, s32[512]{0:T(512)}, u32[]{:S(2)}) copy-start(s32[512]{0:T(512)} %param.12) | copy-start | bytes 6148
  6.5 176.3 %all-gather.2.cloned.1.call-start = ((), (), s32[]{:S(2)}) async-start(), calls=%async_computation.4 | async-start | bytes 4718592 | tf_op jit(solution)/shard_map/all_gather | solution.py:249
  6.5 4.0 %collective-permute-start = (bf16[64,256]{1,0:T(8,128)(2,1)}, bf16[64,256]{1,0:T(8,128)(2,1)S(1)}, u32[]{:S(2)}, u32[]{:S(2)}) collective-permute-start(bf16[64,256]{1,0:T(8,128)(2,1)} %bitcast.61), channel_id=1, source_target_pairs={{0,0},{1,64},{2,128},{3,192},{4,256},{5,320},{6,384},{7,448},{8,8}... | collective-permute-start | bytes 98312 | tf_op jit(solution)/shard_map/ppermute | solution.py:238
  10.7 3.5 %collective-permute-start.1 = (bf16[72,512]{1,0:T(8,128)(2,1)S(1)}, bf16[72,512]{1,0:T(8,128)(2,1)S(1)}, u32[]{:S(2)}, u32[]{:S(2)}) collective-permute-start(bf16[72,512]{1,0:T(8,128)(2,1)S(1)} %select_bitcast_fusion.2), channel_id=1, source_target_pairs={{0,8},{8,0},{1,9},{9,1},{2,10},{10,2},{3,11},{11,3},{4,12},{12,4},... | collective-permute-start | bytes 221192 | tf_op jit(solution)/shard_map/ppermute | solution.py:173
  14.2 12.4 %collective-permute-start.4 = (bf16[2,72,512]{2,1,0:T(8,128)(2,1)S(1)}, bf16[2,72,512]{2,1,0:T(8,128)(2,1)S(1)}, u32[]{:S(2)}, u32[]{:S(2)}) collective-permute-start(bf16[2,72,512]{2,1,0:T(8,128)(2,1)S(1)} %get-tuple-element.26), channel_id=1, source_target_pairs={{0,48},{16,32},{32,16},{48,0},{1,49},{17,33},{33,17},{49,1},{2,50}... | collective-permute-start | bytes 442376 | tf_op jit(solution)/shard_map/ppermute | solution.py:173
  16.3 13.9 %collective-permute-start.2 = (bf16[2,72,512]{2,1,0:T(8,128)(2,1)S(1)}, bf16[2,72,512]{2,1,0:T(8,128)(2,1)S(1)}, u32[]{:S(2)}, u32[]{:S(2)}) collective-permute-start(bf16[2,72,512]{2,1,0:T(8,128)(2,1)S(1)} %get-tuple-element.26), channel_id=1, source_target_pairs={{0,16},{16,0},{32,48},{48,32},{1,17},{17,1},{33,49},{49,33},{2,18}... | collective-permute-start | bytes 442376 | tf_op jit(solution)/shard_map/ppermute | solution.py:173
  24.6 7.3 %collective-permute-start.3 = (bf16[2,72,512]{2,1,0:T(8,128)(2,1)S(1)}, bf16[2,72,512]{2,1,0:T(8,128)(2,1)S(1)}, u32[]{:S(2)}, u32[]{:S(2)}) collective-permute-start(bf16[2,72,512]{2,1,0:T(8,128)(2,1)S(1)} %get-tuple-element.26), channel_id=1, source_target_pairs={{0,32},{16,48},{32,0},{48,16},{1,33},{17,49},{33,1},{49,17},{2,34}... | collective-permute-start | bytes 442376 | tf_op jit(solution)/shard_map/ppermute | solution.py:173
  32.1 1.5 copy-start.6
  33.6 4.7 %collective-permute-start.5 = (bf16[200,256]{1,0:T(8,128)(2,1)S(1)}, bf16[200,256]{1,0:T(8,128)(2,1)S(1)}, u32[]{:S(2)}, u32[]{:S(2)}) collective-permute-start(bf16[200,256]{1,0:T(8,128)(2,1)S(1)} %broadcast_select_fusion), channel_id=1, source_target_pairs={{0,8},{8,0},{1,9},{9,1},{2,10},{10,2},{3,11},{11,3},{4,12},{12,4},... | collective-permute-start | bytes 307208 | tf_op jit(solution)/shard_map/ppermute | solution.py:173
  39.6 18.6 %copy-start.8 = (bf16[512]{0:T(512)(128)(2,1)S(1)}, bf16[512]{0:T(512)(128)(2,1)}, u32[]{:S(2)}) copy-start(bf16[512]{0:T(512)(128)(2,1)} %param.15) | copy-start | bytes 3076
  39.6 75.7 %all-to-all-start = ((bf16[8,16,24,256]{3,2,1,0:T(8,128)(2,1)}), bf16[8,16,24,256]{3,2,1,0:T(8,128)(2,1)S(1)}, u32[]{:S(2)}, u32[]{:S(2)}) async-start(bf16[8,16,24,256]{3,2,1,0:T(8,128)(2,1)} %broadcast_in_dim.30), calls=%async_computation | async-start | bytes 3145728 | tf_op jit(solution)/shard_map/all_to_all | solution.py:202
  115.9 9.7 %collective-permute-start.6 = (bf16[16,24,256]{2,1,0:T(8,128)(2,1)S(1)}, bf16[16,24,256]{2,1,0:T(8,128)(2,1)S(1)}, u32[]{:S(2)}, u32[]{:S(2)}) collective-permute-start(bf16[16,24,256]{2,1,0:T(8,128)(2,1)S(1)} %get-tuple-element.13), channel_id=1, source_target_pairs={{0,16},{16,0},{32,48},{48,32},{1,17},{17,1},{33,49},{49,33},{2,18}... | collective-permute-start | bytes 589832 | tf_op jit(solution)/shard_map/ppermute | solution.py:173
  119.7 14.9 %collective-permute-start.7 = (bf16[16,24,256]{2,1,0:T(8,128)(2,1)S(1)}, bf16[16,24,256]{2,1,0:T(8,128)(2,1)S(1)}, u32[]{:S(2)}, u32[]{:S(2)}) collective-permute-start(bf16[16,24,256]{2,1,0:T(8,128)(2,1)S(1)} %get-tuple-element.14), channel_id=1, source_target_pairs={{0,32},{16,48},{32,0},{48,16},{1,33},{17,49},{33,1},{49,17},{2,34}... | collective-permute-start | bytes 589832 | tf_op jit(solution)/shard_map/ppermute | solution.py:173
  122.7 17.0 %collective-permute-start.8 = (bf16[16,24,256]{2,1,0:T(8,128)(2,1)S(1)}, bf16[16,24,256]{2,1,0:T(8,128)(2,1)S(1)}, u32[]{:S(2)}, u32[]{:S(2)}) collective-permute-start(bf16[16,24,256]{2,1,0:T(8,128)(2,1)S(1)} %get-tuple-element.15), channel_id=1, source_target_pairs={{0,48},{16,32},{32,16},{48,0},{1,49},{17,33},{33,17},{49,1},{2,50}... | collective-permute-start | bytes 589832 | tf_op jit(solution)/shard_map/ppermute | solution.py:173
  141.3 17.8 %all-to-all-start.1 = ((bf16[4,2,208,256]{3,2,1,0:T(8,128)(2,1)}), bf16[4,2,208,256]{3,2,1,0:T(8,128)(2,1)S(1)}, u32[]{:S(2)}, u32[]{:S(2)}) async-start(bf16[4,2,208,256]{3,2,1,0:T(8,128)(2,1)} %get-tuple-element.16), calls=%async_computation.1 | async-start | bytes 1703936 | tf_op jit(solution)/shard_map/all_to_all | solution.py:283
  145.4 37.5 %copy-start.4 = (f32[208,128]{1,0:T(8,128)S(1)}, f32[208,128]{1,0:T(8,128)}, u32[]{:S(2)}) copy-start(f32[208,128]{1,0:T(8,128)} %constant.80.clone.cos_ref) | copy-start | bytes 319492
  145.4 37.5 %copy-start.5 = (f32[208,128]{1,0:T(8,128)S(1)}, f32[208,128]{1,0:T(8,128)}, u32[]{:S(2)}) copy-start(f32[208,128]{1,0:T(8,128)} %constant.81.clone.sin_ref) | copy-start | bytes 319492
  145.4 13.7 %collective-permute-start.9 = (bf16[2,208,256]{2,1,0:T(8,128)(2,1)S(1)}, bf16[2,208,256]{2,1,0:T(8,128)(2,1)S(1)}, u32[]{:S(2)}, u32[]{:S(2)}) collective-permute-start(bf16[2,208,256]{2,1,0:T(8,128)(2,1)S(1)} %get-tuple-element.17), channel_id=1, source_target_pairs={{0,4},{4,0},{1,5},{5,1},{2,6},{6,2},{3,7},{7,3},{8,12},{12,8},{9,1... | collective-permute-start | bytes 638984 | tf_op jit(solution)/shard_map/ppermute | solution.py:173
  160.1 14.2 %all-to-all-start.2 = ((bf16[4,2,208,256]{3,2,1,0:T(8,128)(2,1)}), bf16[4,2,208,256]{3,2,1,0:T(8,128)(2,1)S(1)}, u32[]{:S(2)}, u32[]{:S(2)}) async-start(bf16[4,2,208,256]{3,2,1,0:T(8,128)(2,1)} %broadcast_in_dim.32), calls=%async_computation.2 | async-start | bytes 1703936 | tf_op jit(solution)/shard_map/all_to_all | solution.py:202
  164.0 15.9 %collective-permute-start.10 = (bf16[4,2,208,256]{3,2,1,0:T(8,128)(2,1)S(1)}, bf16[4,2,208,256]{3,2,1,0:T(8,128)(2,1)S(1)}, u32[]{:S(2)}, u32[]{:S(2)}) collective-permute-start(bf16[4,2,208,256]{3,2,1,0:T(8,128)(2,1)S(1)} %all-to-all-done.1.own_ref), channel_id=1, source_target_pairs={{0,8},{8,0},{1,9},{9,1},{2,10},{10,2},{3,11},{11,3},{4,12},{12,4},... | collective-permute-start | bytes 2555912 | tf_op jit(solution)/shard_map/ppermute | solution.py:173
  174.3 7.5 %collective-permute-start.11 = (bf16[4,2,208,256]{3,2,1,0:T(8,128)(2,1)S(1)}, bf16[4,2,208,256]{3,2,1,0:T(8,128)(2,1)S(1)}, u32[]{:S(2)}, u32[]{:S(2)}) collective-permute-start(bf16[4,2,208,256]{3,2,1,0:T(8,128)(2,1)S(1)} %all-to-all-done.2.far_ref), channel_id=1, source_target_pairs={{0,8},{8,0},{1,9},{9,1},{2,10},{10,2},{3,11},{11,3},{4,12},{12,4},... | collective-permute-start | bytes 2555912 | tf_op jit(solution)/shard_map/ppermute | solution.py:173
  182.8 2.2 copy-start.1
  192.4 31.0 %all-to-all-start.3 = ((bf16[16,208,128]{2,1,0:T(8,128)(2,1)}), bf16[16,208,128]{2,1,0:T(8,128)(2,1)S(1)}, u32[]{:S(2)}, u32[]{:S(2)}) async-start(bf16[16,208,128]{2,1,0:T(8,128)(2,1)} %bitcast.20), calls=%async_computation.3 | async-start | bytes 1703936 | tf_op jit(solution)/shard_map/all_to_all | solution.py:322
  198.7 4.7 %collective-permute-start.12 = (bf16[4096,128]{1,0:T(8,128)(2,1)S(1)}, bf16[4096,128]{1,0:T(8,128)(2,1)}, u32[]{:S(2)}, u32[]{:S(2)}) collective-permute-start(bf16[4096,128]{1,0:T(8,128)(2,1)S(1)} %slice.72.own_ref), channel_id=1, source_target_pairs={{0,8},{8,0},{1,9},{9,1},{2,10},{10,2},{3,11},{11,3},{4,12},{12,4},... | collective-permute-start | bytes 3145736 | tf_op jit(solution)/shard_map/ppermute | solution.py:173
  (3 other events, 3.6 us)
Sparse Core Ops, SparseCore 0:
  33.7 102.2 all-gather.1

commit v5 on v4

--- a/solution.py
+++ b/solution.py
@@ -17,9 +17,7 @@
 TENSOR = ("h", "x")
 VMEM = pl.BlockSpec(memory_space=pltpu.VMEM)
 SMEM = pl.BlockSpec(memory_space=pltpu.SMEM)
-ANY = pl.BlockSpec(memory_space=pl.ANY)
-LIMIT = 32 * 1024 * 1024
-WEIGHT_PARTS = 4
+MIB = 1024 * 1024
 
 
 def pick_kernel(index_ref, library_ref, *out_refs):
@@ -55,25 +53,13 @@
 
 def attention_kernel(
     count_ref, own_ref, far_ref, own_swap_ref, far_swap_ref, weight_ref, cos_ref, sin_ref,
-    out_ref, normed_ref, held_ref, semaphores, *, query_len, passage_rows,
+    out_ref, normed_ref, *, query_len, passage_rows,
 ):
     bf16, f32, i32 = jnp.bfloat16, jnp.float32, jnp.int32
     spread, groups, rows, part = own_ref.shape
     width = 4 * spread * part
     pairs = count_ref.shape[0] // groups
     gain_row = query_len + pairs * passage_rows
-    depth = held_ref.shape[0] // WEIGHT_PARTS
-    copies = []
-    for i in range(WEIGHT_PARTS):
-        block = pl.ds(i * depth, depth)
-        copies.append(
-            pltpu.make_async_copy(
-                weight_ref.at[block, pl.ds(0, held_ref.shape[1])],
-                held_ref.at[block],
-                semaphores.at[i],
-            )
-        )
-        copies[-1].start()
     core, high = lax.axis_index("c"), lax.axis_index("h")
     quarters = (
         (own_ref, high, core),
@@ -98,12 +84,9 @@
                 normed_ref[group * rows : (group + 1) * rows, pl.ds(begin, part)] = (
                     chunk * inverse * gain
                 ).astype(bf16)
-    projected = None
-    for i in range(WEIGHT_PARTS):
-        copies[i].wait()
-        block = slice(i * depth, (i + 1) * depth)
-        product = jnp.dot(normed_ref[:, block], held_ref[block], preferred_element_type=f32)
-        projected = product if projected is None else projected + product
+    projected = jnp.dot(
+        normed_ref[...], weight_ref[:, : 3 * HEAD_DIM], preferred_element_type=f32
+    )
 
     def rotate(inputs):
         return (
@@ -223,14 +206,17 @@
     live = query_len + pairs * passage_rows
     rows = (live // ROW_TILE + 1) * ROW_TILE
     depth = project_weight.shape[0]
-    options = pltpu.CompilerParams(vmem_limit_bytes=LIMIT)
+    options = pltpu.CompilerParams(vmem_limit_bytes=8 * MIB)
 
     raw = jnp.concatenate([corpus_rows.reshape(-1, features), query_rows[0]], axis=0)
     keep, give = halves(raw, part)
     shared = by_core(keep, partner(give, "c", 1))
     held = shared[:, : stored * passage_rows].reshape(2 * stored, passage_rows, part)
     queries = shared[:, stored * passage_rows :]
-    library = on_every(held, "z").reshape(-1, passage_rows, part)
+    output_weight, project_weight, held = lax.optimization_barrier(
+        (output_weight, project_weight, held)
+    )
+    library = lax.all_gather(held, "z", axis=0, tiled=True)
 
     cells = [(z, q, t) for z in range(SIZE["z"]) for q in range(plane) for t in range(tensors)]
     number = {cell: i for i, cell in enumerate(cells)}
@@ -294,14 +280,10 @@
     attended = pl.pallas_call(
         functools.partial(attention_kernel, query_len=query_len, passage_rows=passage_rows),
         out_shape=jax.ShapeDtypeStruct((cores, tensors, rows, HEAD_DIM), bf16),
-        in_specs=[SMEM] + [VMEM] * 4 + [ANY] + [VMEM] * 2,
+        in_specs=[SMEM] + [VMEM] * 7,
         out_specs=VMEM,
-        scratch_shapes=[
-            pltpu.VMEM((cores * rows, tensors * features), bf16),
-            pltpu.VMEM((weight.shape[0], 3 * HEAD_DIM), bf16),
-            pltpu.SemaphoreType.DMA((WEIGHT_PARTS,)),
-        ],
-        compiler_params=options,
+        scratch_shapes=[pltpu.VMEM((cores * rows, tensors * features), bf16)],
+        compiler_params=pltpu.CompilerParams(vmem_limit_bytes=24 * MIB),
         cost_estimate=pl.CostEstimate(
             flops=2 * rows * tensors * features * 6 * HEAD_DIM,
             bytes_accessed=8 * 1024 * 1024,

time: 234 us -> 177 us (0.76)
  the two profiles are of different devices: /device:TPU:17 before, /device:TPU:9 now
where the time goes in v5:
time: 177 us; the launch traced here: 176 us
  starting transfers between devices  68.4 us (39%)
  waiting for transfers between devices  66 us (37%)
  between operations  13.7 us (8%)
  local copies, waits for them, and re-layouts  12.1 us (7%)
  Pallas kernels  10.9 us (6%)
  other arithmetic  4.52 us (3%)
    ppermute x12, starting transfers between devices, partner(): return lax.ppermute(value, axis, [(i, i ^ bit) for i in range(SIZE[axis])])  53 us
    ppermute x12, waiting for transfers between devices, partner(): return lax.ppermute(value, axis, [(i, i ^ bit) for i in range(SIZE[axis])])  28.1 us
    all_to_all x1, waiting for transfers between devices, on_device(): lax.all_to_all(attended.reshape(-1, rows, HEAD_DIM), ('c',) + TENSOR, spl...  20.9 us
    all_gather x1, waiting for transfers between devices, on_device(): library = lax.all_gather(held, 'z', axis=0, tiled=True)  16.9 us
    unnamed x16, local copies, waits for them, and re-layouts  5.71 us
    pallas_call x1, Pallas kernels, on_device(): pl.pallas_call(functools.partial(attention_kernel, query_len=query_len, p...  5.67 us
    all_to_all x1, starting transfers between devices, on_device(): lax.all_to_all(attended.reshape(-1, rows, HEAD_DIM), ('c',) + TENSOR, spl...  5.52 us
    all_to_all x1, starting transfers between devices, on_every(): return lax.all_to_all(spread, axis, split_axis=0, concat_axis=0, tiled=True)  4.21 us
  transfers between devices with their start and end apart: 18, of which 11 were waited for; matrix products, arithmetic and copies ran while one was open for 5% of the time, Pallas kernels for 1%

profile of v5, /device:TPU:9, one launch (start us, length us, event | category | flops | bytes accessed | tf_op | source)
XLA Modules:
  0.0 175.6 jit_solution(16870508736848215018)
XLA Ops:
  7.6 2.6 %collective-permute-start = (bf16[200,256]{1,0:T(8,128)(2,1)S(1)}, bf16[200,256]{1,0:T(8,128)(2,1)S(1)}, u32[]{:S(2)}, u32[]{:S(2)}) collective-permute-start(bf16[200,256]{1,0:T(8,128)(2,1)S(1)} %broadcast_select_fusion), channel_id=1, source_target_pairs={{0,8},{8,0},{1,9},{9,1},{2,10},{10,2},{3,11},{11,3},{4,12},{12,4},... | collective-permute-start | bytes 307208 | tf_op jit(solution)/shard_map/ppermute | solution.py:156
  16.9 2.3 %collective-permute-start.2 = (bf16[72,512]{1,0:T(8,128)(2,1)S(1)}, bf16[72,512]{1,0:T(8,128)(2,1)S(1)}, u32[]{:S(2)}, u32[]{:S(2)}) collective-permute-start(bf16[72,512]{1,0:T(8,128)(2,1)S(1)} %select_bitcast_fusion.2), channel_id=1, source_target_pairs={{0,8},{8,0},{1,9},{9,1},{2,10},{10,2},{3,11},{11,3},{4,12},{12,4},... | collective-permute-start | bytes 221192 | tf_op jit(solution)/shard_map/ppermute | solution.py:156
  20.2 4.2 %collective-permute-start.4 = (bf16[2,72,512]{2,1,0:T(8,128)(2,1)S(1)}, bf16[2,72,512]{2,1,0:T(8,128)(2,1)S(1)}, u32[]{:S(2)}, u32[]{:S(2)}) collective-permute-start(bf16[2,72,512]{2,1,0:T(8,128)(2,1)S(1)} %get-tuple-element.32), channel_id=1, source_target_pairs={{0,32},{16,48},{32,0},{48,16},{1,33},{17,49},{33,1},{49,17},{2,34}... | collective-permute-start | bytes 442376 | tf_op jit(solution)/shard_map/ppermute | solution.py:156
  24.4 5.2 %collective-permute-start.3 = (bf16[2,72,512]{2,1,0:T(8,128)(2,1)S(1)}, bf16[2,72,512]{2,1,0:T(8,128)(2,1)S(1)}, u32[]{:S(2)}, u32[]{:S(2)}) collective-permute-start(bf16[2,72,512]{2,1,0:T(8,128)(2,1)S(1)} %get-tuple-element.32), channel_id=1, source_target_pairs={{0,16},{16,0},{32,48},{48,32},{1,17},{17,1},{33,49},{49,33},{2,18}... | collective-permute-start | bytes 442376 | tf_op jit(solution)/shard_map/ppermute | solution.py:156
  29.6 3.1 %collective-permute-start.5 = (bf16[2,72,512]{2,1,0:T(8,128)(2,1)S(1)}, bf16[2,72,512]{2,1,0:T(8,128)(2,1)S(1)}, u32[]{:S(2)}, u32[]{:S(2)}) collective-permute-start(bf16[2,72,512]{2,1,0:T(8,128)(2,1)S(1)} %get-tuple-element.32), channel_id=1, source_target_pairs={{0,48},{16,32},{32,16},{48,0},{1,49},{17,33},{33,17},{49,1},{2,50}... | collective-permute-start | bytes 442376 | tf_op jit(solution)/shard_map/ppermute | solution.py:156
  32.7 2.9 %collective-permute-done.3 = bf16[2,72,512]{2,1,0:T(8,128)(2,1)S(1)} collective-permute-done((bf16[2,72,512]{2,1,0:T(8,128)(2,1)S(1)}, bf16[2,72,512]{2,1,0:T(8,128)(2,1)S(1)}, u32[]{:S(2)}, u32[]{:S(2)}) %collective-permute-start.3) | collective-permute-done | bytes 147488 | tf_op jit(solution)/shard_map/ppermute | solution.py:156
  39.9 16.9 %all-gather.3.cloned.1.call-done.library_ref = bf16[128,24,256]{2,1,0:T(8,128)(2,1)} async-done(((bf16[16,24,256]{2,1,0:T(8,128)(2,1)}), bf16[128,24,256]{2,1,0:T(8,128)(2,1)}) %all-gather.3.cloned.1.call-update) | async-done | bytes 1572880 | tf_op jit(solution)/shard_map/all_gather | solution.py:219
  58.8 2.2 %collective-permute-start.6 = (bf16[16,24,256]{2,1,0:T(8,128)(2,1)S(1)}, bf16[16,24,256]{2,1,0:T(8,128)(2,1)S(1)}, u32[]{:S(2)}, u32[]{:S(2)}) collective-permute-start(bf16[16,24,256]{2,1,0:T(8,128)(2,1)S(1)} %get-tuple-element.19), channel_id=1, source_target_pairs={{0,16},{16,0},{32,48},{48,32},{1,17},{17,1},{33,49},{49,33},{2,18}... | collective-permute-start | bytes 589832 | tf_op jit(solution)/shard_map/ppermute | solution.py:156
  61.0 4.2 %collective-permute-start.7 = (bf16[16,24,256]{2,1,0:T(8,128)(2,1)S(1)}, bf16[16,24,256]{2,1,0:T(8,128)(2,1)S(1)}, u32[]{:S(2)}, u32[]{:S(2)}) collective-permute-start(bf16[16,24,256]{2,1,0:T(8,128)(2,1)S(1)} %get-tuple-element.20), channel_id=1, source_target_pairs={{0,32},{16,48},{32,0},{48,16},{1,33},{17,49},{33,1},{49,17},{2,34}... | collective-permute-start | bytes 589832 | tf_op jit(solution)/shard_map/ppermute | solution.py:156
  65.2 2.0 %collective-permute-start.8 = (bf16[16,24,256]{2,1,0:T(8,128)(2,1)S(1)}, bf16[16,24,256]{2,1,0:T(8,128)(2,1)S(1)}, u32[]{:S(2)}, u32[]{:S(2)}) collective-permute-start(bf16[16,24,256]{2,1,0:T(8,128)(2,1)S(1)} %get-tuple-element.21), channel_id=1, source_target_pairs={{0,48},{16,32},{32,16},{48,0},{1,49},{17,33},{33,17},{49,1},{2,50}... | collective-permute-start | bytes 589832 | tf_op jit(solution)/shard_map/ppermute | solution.py:156
  69.8 10.7 %collective-permute-done.8.refs_3_ = bf16[16,24,256]{2,1,0:T(8,128)(2,1)S(1)} collective-permute-done((bf16[16,24,256]{2,1,0:T(8,128)(2,1)S(1)}, bf16[16,24,256]{2,1,0:T(8,128)(2,1)S(1)}, u32[]{:S(2)}, u32[]{:S(2)}) %collective-permute-start.8) | collective-permute-done | bytes 196640 | tf_op jit(solution)/shard_map/ppermute | solution.py:156
  82.1 4.2 %all-to-all-start = ((bf16[4,2,208,256]{3,2,1,0:T(8,128)(2,1)}), bf16[4,2,208,256]{3,2,1,0:T(8,128)(2,1)S(1)}, u32[]{:S(2)}, u32[]{:S(2)}) async-start(bf16[4,2,208,256]{3,2,1,0:T(8,128)(2,1)} %get-tuple-element.22), calls=%async_computation | async-start | bytes 1703936 | tf_op jit(solution)/shard_map/all_to_all | solution.py:269
  86.2 6.0 %collective-permute-start.9 = (bf16[2,208,256]{2,1,0:T(8,128)(2,1)S(1)}, bf16[2,208,256]{2,1,0:T(8,128)(2,1)S(1)}, u32[]{:S(2)}, u32[]{:S(2)}) collective-permute-start(bf16[2,208,256]{2,1,0:T(8,128)(2,1)S(1)} %get-tuple-element.23), channel_id=1, source_target_pairs={{0,4},{4,0},{1,5},{5,1},{2,6},{6,2},{3,7},{7,3},{8,12},{12,8},{9,1... | collective-permute-start | bytes 638984 | tf_op jit(solution)/shard_map/ppermute | solution.py:156
  92.2 4.5 %collective-permute-done.9 = bf16[2,208,256]{2,1,0:T(8,128)(2,1)S(1)} collective-permute-done((bf16[2,208,256]{2,1,0:T(8,128)(2,1)S(1)}, bf16[2,208,256]{2,1,0:T(8,128)(2,1)S(1)}, u32[]{:S(2)}, u32[]{:S(2)}) %collective-permute-start.9) | collective-permute-done | bytes 213024 | tf_op jit(solution)/shard_map/ppermute | solution.py:156
  97.8 4.2 %all-to-all-start.1 = ((bf16[4,2,208,256]{3,2,1,0:T(8,128)(2,1)}), bf16[4,2,208,256]{3,2,1,0:T(8,128)(2,1)S(1)}, u32[]{:S(2)}, u32[]{:S(2)}) async-start(bf16[4,2,208,256]{3,2,1,0:T(8,128)(2,1)} %broadcast_in_dim.23), calls=%async_computation.1 | async-start | bytes 1703936 | tf_op jit(solution)/shard_map/all_to_all | solution.py:185
  102.0 9.6 %collective-permute-start.10 = (bf16[4,2,208,256]{3,2,1,0:T(8,128)(2,1)S(1)}, bf16[4,2,208,256]{3,2,1,0:T(8,128)(2,1)S(1)}, u32[]{:S(2)}, u32[]{:S(2)}) collective-permute-start(bf16[4,2,208,256]{3,2,1,0:T(8,128)(2,1)S(1)} %all-to-all-done.own_ref), channel_id=1, source_target_pairs={{0,8},{8,0},{1,9},{9,1},{2,10},{10,2},{3,11},{11,3},{4,12},{12,4},... | collective-permute-start | bytes 2555912 | tf_op jit(solution)/shard_map/ppermute | solution.py:156
  111.5 9.8 %collective-permute-start.11 = (bf16[4,2,208,256]{3,2,1,0:T(8,128)(2,1)S(1)}, bf16[4,2,208,256]{3,2,1,0:T(8,128)(2,1)S(1)}, u32[]{:S(2)}, u32[]{:S(2)}) collective-permute-start(bf16[4,2,208,256]{3,2,1,0:T(8,128)(2,1)S(1)} %all-to-all-done.1.far_ref), channel_id=1, source_target_pairs={{0,8},{8,0},{1,9},{9,1},{2,10},{10,2},{3,11},{11,3},{4,12},{12,4},... | collective-permute-start | bytes 2555912 | tf_op jit(solution)/shard_map/ppermute | solution.py:156
  124.3 2.2 %copy-done.1 = bf16[4096,512]{1,0:T(8,128)(2,1)S(1)} copy-done((bf16[4096,512]{1,0:T(8,128)(2,1)S(1)}, bf16[4096,512]{1,0:T(8,128)(2,1)}, u32[]{:S(2)}) %copy-start.1) | copy-done | bytes 4194328
  127.7 5.7 %attention.1 = bf16[2,8,208,128]{3,2,1,0:T(8,128)(2,1)} custom-call(s32[16]{0:T(128)S(1)} %gather_fusion.1, bf16[4,2,208,256]{3,2,1,0:T(8,128)(2,1)S(1)} %all-to-all-done.own_ref, bf16[4,2,208,256]{3,2,1,0:T(8,128)(2,1)S(1)} %all-to-all-done.1.far_ref, bf16[4,2,208,256]{3,2,1,0:T(8,128)(2,1)S(1)} %collective-permute-done.10.own_swap_ref, ...), custom_call_target="tpu_custom_call" | custom-call | flops 1308622848 | bytes 8388608 | tf_op jit(solution)/shard_map/attention/pallas_call | solution.py:280
  133.3 5.5 %all-to-all-start.2 = ((bf16[16,208,128]{2,1,0:T(8,128)(2,1)}), bf16[16,208,128]{2,1,0:T(8,128)(2,1)S(1)}, u32[]{:S(2)}, u32[]{:S(2)}) async-start(bf16[16,208,128]{2,1,0:T(8,128)(2,1)} %bitcast.19), calls=%async_computation.2 | async-start | bytes 1703936 | tf_op jit(solution)/shard_map/all_to_all | solution.py:304
  140.1 2.0 %collective-permute-start.12 = (bf16[4096,128]{1,0:T(8,128)(2,1)S(1)}, bf16[4096,128]{1,0:T(8,128)(2,1)}, u32[]{:S(2)}, u32[]{:S(2)}) collective-permute-start(bf16[4096,128]{1,0:T(8,128)(2,1)S(1)} %slice.72.own_ref), channel_id=1, source_target_pairs={{0,8},{8,0},{1,9},{9,1},{2,10},{10,2},{3,11},{11,3},{4,12},{12,4},... | collective-permute-start | bytes 3145736 | tf_op jit(solution)/shard_map/ppermute | solution.py:156
  142.2 2.6 %collective-permute-done.12.other_ref = bf16[4096,128]{1,0:T(8,128)(2,1)} collective-permute-done((bf16[4096,128]{1,0:T(8,128)(2,1)S(1)}, bf16[4096,128]{1,0:T(8,128)(2,1)}, u32[]{:S(2)}, u32[]{:S(2)}) %collective-permute-start.12) | collective-permute-done | bytes 1048608 | tf_op jit(solution)/shard_map/ppermute | solution.py:156
  144.8 20.9 %all-to-all-done.2.heads_ref = bf16[16,208,128]{2,1,0:T(8,128)(2,1)S(1)} async-done(((bf16[16,208,128]{2,1,0:T(8,128)(2,1)}), bf16[16,208,128]{2,1,0:T(8,128)(2,1)S(1)}, u32[]{:S(2)}, u32[]{:S(2)}) %all-to-all-start.2) | async-done | bytes 852000 | tf_op jit(solution)/shard_map/all_to_all | solution.py:304
  165.7 3.0 %output.1 = bf16[256,512]{1,0:T(8,128)(2,1)} custom-call(bf16[16,208,128]{2,1,0:T(8,128)(2,1)S(1)} %all-to-all-done.2.heads_ref, bf16[4096,128]{1,0:T(8,128)(2,1)S(1)} %slice.72.own_ref, bf16[4096,128]{1,0:T(8,128)(2,1)} %collective-permute-done.12.other_ref, bf16[208,256]{1,0:T(8,128)(2,1)S(1)} %dynamic-slice_bitcast_fusion.1.near_ref, ...), custom_call_target="tpu_custom_call" | custom-call | flops 436207616 | bytes 3145728 | tf_op jit(solution)/shard_map/output/pallas_call | solution.py:319
  (73 shorter events, 25.5 us)
Async XLA Ops:
  6.5 60.8 %copy-start = (s32[512]{0:T(512)S(1)}, s32[512]{0:T(512)}, u32[]{:S(2)}) copy-start(s32[512]{0:T(512)} %param.12) | copy-start | bytes 6148
  6.5 32.4 %copy-start.7 = (bf16[512]{0:T(512)(128)(2,1)S(1)}, bf16[512]{0:T(512)(128)(2,1)}, u32[]{:S(2)}) copy-start(bf16[512]{0:T(512)(128)(2,1)} %param.15) | copy-start | bytes 3076
  6.5 50.3 %all-gather.3.cloned.1.call-start = ((), (), s32[]{:S(2)}) async-start(), calls=%async_computation.3 | async-start | bytes 1769472 | tf_op jit(solution)/shard_map/all_gather | solution.py:219
  7.6 3.5 %collective-permute-start = (bf16[200,256]{1,0:T(8,128)(2,1)S(1)}, bf16[200,256]{1,0:T(8,128)(2,1)S(1)}, u32[]{:S(2)}, u32[]{:S(2)}) collective-permute-start(bf16[200,256]{1,0:T(8,128)(2,1)S(1)} %broadcast_select_fusion), channel_id=1, source_target_pairs={{0,8},{8,0},{1,9},{9,1},{2,10},{10,2},{3,11},{11,3},{4,12},{12,4},... | collective-permute-start | bytes 307208 | tf_op jit(solution)/shard_map/ppermute | solution.py:156
  12.9 111.4 %all-gather.5.cloned.1.call-start = ((), (), s32[]{:S(2)}) async-start(), calls=%async_computation.4 | async-start | bytes 4718592 | tf_op jit(solution)/shard_map/all_gather | solution.py:235
  14.3 2.6 %collective-permute-start.1 = (bf16[64,256]{1,0:T(8,128)(2,1)}, bf16[64,256]{1,0:T(8,128)(2,1)S(1)}, u32[]{:S(2)}, u32[]{:S(2)}) collective-permute-start(bf16[64,256]{1,0:T(8,128)(2,1)} %bitcast.59), channel_id=1, source_target_pairs={{0,0},{1,64},{2,128},{3,192},{4,256},{5,320},{6,384},{7,448},{8,8}... | collective-permute-start | bytes 98312 | tf_op jit(solution)/shard_map/ppermute | solution.py:224
  16.9 3.2 %collective-permute-start.2 = (bf16[72,512]{1,0:T(8,128)(2,1)S(1)}, bf16[72,512]{1,0:T(8,128)(2,1)S(1)}, u32[]{:S(2)}, u32[]{:S(2)}) collective-permute-start(bf16[72,512]{1,0:T(8,128)(2,1)S(1)} %select_bitcast_fusion.2), channel_id=1, source_target_pairs={{0,8},{8,0},{1,9},{9,1},{2,10},{10,2},{3,11},{11,3},{4,12},{12,4},... | collective-permute-start | bytes 221192 | tf_op jit(solution)/shard_map/ppermute | solution.py:156
  20.2 12.5 %collective-permute-start.4 = (bf16[2,72,512]{2,1,0:T(8,128)(2,1)S(1)}, bf16[2,72,512]{2,1,0:T(8,128)(2,1)S(1)}, u32[]{:S(2)}, u32[]{:S(2)}) collective-permute-start(bf16[2,72,512]{2,1,0:T(8,128)(2,1)S(1)} %get-tuple-element.32), channel_id=1, source_target_pairs={{0,32},{16,48},{32,0},{48,16},{1,33},{17,49},{33,1},{49,17},{2,34}... | collective-permute-start | bytes 442376 | tf_op jit(solution)/shard_map/ppermute | solution.py:156
  24.4 11.2 %collective-permute-start.3 = (bf16[2,72,512]{2,1,0:T(8,128)(2,1)S(1)}, bf16[2,72,512]{2,1,0:T(8,128)(2,1)S(1)}, u32[]{:S(2)}, u32[]{:S(2)}) collective-permute-start(bf16[2,72,512]{2,1,0:T(8,128)(2,1)S(1)} %get-tuple-element.32), channel_id=1, source_target_pairs={{0,16},{16,0},{32,48},{48,32},{1,17},{17,1},{33,49},{49,33},{2,18}... | collective-permute-start | bytes 442376 | tf_op jit(solution)/shard_map/ppermute | solution.py:156
  29.6 7.8 %collective-permute-start.5 = (bf16[2,72,512]{2,1,0:T(8,128)(2,1)S(1)}, bf16[2,72,512]{2,1,0:T(8,128)(2,1)S(1)}, u32[]{:S(2)}, u32[]{:S(2)}) collective-permute-start(bf16[2,72,512]{2,1,0:T(8,128)(2,1)S(1)} %get-tuple-element.32), channel_id=1, source_target_pairs={{0,48},{16,32},{32,16},{48,0},{1,49},{17,33},{33,17},{49,1},{2,50}... | collective-permute-start | bytes 442376 | tf_op jit(solution)/shard_map/ppermute | solution.py:156
  38.9 85.4 %copy-start.5 = (f32[208,128]{1,0:T(8,128)S(1)}, f32[208,128]{1,0:T(8,128)}, u32[]{:S(2)}) copy-start(f32[208,128]{1,0:T(8,128)} %constant.81.clone.sin_ref) | copy-start | bytes 319492
  38.9 85.4 %copy-start.6 = (f32[208,128]{1,0:T(8,128)S(1)}, f32[208,128]{1,0:T(8,128)}, u32[]{:S(2)}) copy-start(f32[208,128]{1,0:T(8,128)} %constant.80.clone.cos_ref) | copy-start | bytes 319492
  56.8 1.4 copy-start.2
  58.8 9.2 %collective-permute-start.6 = (bf16[16,24,256]{2,1,0:T(8,128)(2,1)S(1)}, bf16[16,24,256]{2,1,0:T(8,128)(2,1)S(1)}, u32[]{:S(2)}, u32[]{:S(2)}) collective-permute-start(bf16[16,24,256]{2,1,0:T(8,128)(2,1)S(1)} %get-tuple-element.19), channel_id=1, source_target_pairs={{0,16},{16,0},{32,48},{48,32},{1,17},{17,1},{33,49},{49,33},{2,18}... | collective-permute-start | bytes 589832 | tf_op jit(solution)/shard_map/ppermute | solution.py:156
  61.0 8.8 %collective-permute-start.7 = (bf16[16,24,256]{2,1,0:T(8,128)(2,1)S(1)}, bf16[16,24,256]{2,1,0:T(8,128)(2,1)S(1)}, u32[]{:S(2)}, u32[]{:S(2)}) collective-permute-start(bf16[16,24,256]{2,1,0:T(8,128)(2,1)S(1)} %get-tuple-element.20), channel_id=1, source_target_pairs={{0,32},{16,48},{32,0},{48,16},{1,33},{17,49},{33,1},{49,17},{2,34}... | collective-permute-start | bytes 589832 | tf_op jit(solution)/shard_map/ppermute | solution.py:156
  65.2 15.3 %collective-permute-start.8 = (bf16[16,24,256]{2,1,0:T(8,128)(2,1)S(1)}, bf16[16,24,256]{2,1,0:T(8,128)(2,1)S(1)}, u32[]{:S(2)}, u32[]{:S(2)}) collective-permute-start(bf16[16,24,256]{2,1,0:T(8,128)(2,1)S(1)} %get-tuple-element.21), channel_id=1, source_target_pairs={{0,48},{16,32},{32,16},{48,0},{1,49},{17,33},{33,17},{49,1},{2,50}... | collective-permute-start | bytes 589832 | tf_op jit(solution)/shard_map/ppermute | solution.py:156
  82.1 14.7 %all-to-all-start = ((bf16[4,2,208,256]{3,2,1,0:T(8,128)(2,1)}), bf16[4,2,208,256]{3,2,1,0:T(8,128)(2,1)S(1)}, u32[]{:S(2)}, u32[]{:S(2)}) async-start(bf16[4,2,208,256]{3,2,1,0:T(8,128)(2,1)} %get-tuple-element.22), calls=%async_computation | async-start | bytes 1703936 | tf_op jit(solution)/shard_map/all_to_all | solution.py:269
  86.2 10.5 %collective-permute-start.9 = (bf16[2,208,256]{2,1,0:T(8,128)(2,1)S(1)}, bf16[2,208,256]{2,1,0:T(8,128)(2,1)S(1)}, u32[]{:S(2)}, u32[]{:S(2)}) collective-permute-start(bf16[2,208,256]{2,1,0:T(8,128)(2,1)S(1)} %get-tuple-element.23), channel_id=1, source_target_pairs={{0,4},{4,0},{1,5},{5,1},{2,6},{6,2},{3,7},{7,3},{8,12},{12,8},{9,1... | collective-permute-start | bytes 638984 | tf_op jit(solution)/shard_map/ppermute | solution.py:156
  97.8 13.8 %all-to-all-start.1 = ((bf16[4,2,208,256]{3,2,1,0:T(8,128)(2,1)}), bf16[4,2,208,256]{3,2,1,0:T(8,128)(2,1)S(1)}, u32[]{:S(2)}, u32[]{:S(2)}) async-start(bf16[4,2,208,256]{3,2,1,0:T(8,128)(2,1)} %broadcast_in_dim.23), calls=%async_computation.1 | async-start | bytes 1703936 | tf_op jit(solution)/shard_map/all_to_all | solution.py:185
  102.0 19.4 %collective-permute-start.10 = (bf16[4,2,208,256]{3,2,1,0:T(8,128)(2,1)S(1)}, bf16[4,2,208,256]{3,2,1,0:T(8,128)(2,1)S(1)}, u32[]{:S(2)}, u32[]{:S(2)}) collective-permute-start(bf16[4,2,208,256]{3,2,1,0:T(8,128)(2,1)S(1)} %all-to-all-done.own_ref), channel_id=1, source_target_pairs={{0,8},{8,0},{1,9},{9,1},{2,10},{10,2},{3,11},{11,3},{4,12},{12,4},... | collective-permute-start | bytes 2555912 | tf_op jit(solution)/shard_map/ppermute | solution.py:156
  111.5 11.8 %collective-permute-start.11 = (bf16[4,2,208,256]{3,2,1,0:T(8,128)(2,1)S(1)}, bf16[4,2,208,256]{3,2,1,0:T(8,128)(2,1)S(1)}, u32[]{:S(2)}, u32[]{:S(2)}) collective-permute-start(bf16[4,2,208,256]{3,2,1,0:T(8,128)(2,1)S(1)} %all-to-all-done.1.far_ref), channel_id=1, source_target_pairs={{0,8},{8,0},{1,9},{9,1},{2,10},{10,2},{3,11},{11,3},{4,12},{12,4},... | collective-permute-start | bytes 2555912 | tf_op jit(solution)/shard_map/ppermute | solution.py:156
  124.3 2.2 %copy-start.1 = (bf16[4096,512]{1,0:T(8,128)(2,1)S(1)}, bf16[4096,512]{1,0:T(8,128)(2,1)}, u32[]{:S(2)}) copy-start(bf16[4096,512]{1,0:T(8,128)(2,1)} %all-gather.5.cloned.1.call-done.weight_ref) | copy-start | bytes 12582916
  133.3 32.4 %all-to-all-start.2 = ((bf16[16,208,128]{2,1,0:T(8,128)(2,1)}), bf16[16,208,128]{2,1,0:T(8,128)(2,1)S(1)}, u32[]{:S(2)}, u32[]{:S(2)}) async-start(bf16[16,208,128]{2,1,0:T(8,128)(2,1)} %bitcast.19), calls=%async_computation.2 | async-start | bytes 1703936 | tf_op jit(solution)/shard_map/all_to_all | solution.py:304
  140.1 4.7 %collective-permute-start.12 = (bf16[4096,128]{1,0:T(8,128)(2,1)S(1)}, bf16[4096,128]{1,0:T(8,128)(2,1)}, u32[]{:S(2)}, u32[]{:S(2)}) collective-permute-start(bf16[4096,128]{1,0:T(8,128)(2,1)S(1)} %slice.72.own_ref), channel_id=1, source_target_pairs={{0,8},{8,0},{1,9},{9,1},{2,10},{10,2},{3,11},{11,3},{4,12},{12,4},... | collective-permute-start | bytes 3145736 | tf_op jit(solution)/shard_map/ppermute | solution.py:156
  (2 other events, 2.1 us)
Sparse Core Ops, SparseCore 0:
  13.0 43.7 all-gather.2
  58.9 60.3 all-gather.4

commit v6 on v5

--- a/solution.py
+++ b/solution.py
@@ -29,7 +29,7 @@
 
 def pack_kernel(source_ref, count_ref, *refs):
     f32 = jnp.float32
-    part_refs, (query_ref, gain_ref, packed_ref, spread_ref) = refs[:-4], refs[-4:]
+    part_refs, (query_ref, gain_ref, packed_ref) = refs[:-3], refs[-3:]
     groups, rows, part = packed_ref.shape
     passage_rows = part_refs[0].shape[1]
     pairs = part_refs[0].shape[0] // groups
@@ -45,21 +45,13 @@
             blocks.append(jnp.where(place < count_ref[spot], passage, 0.0))
         filled = blocks[0].shape[0] + pairs * passage_rows
         blocks.append(jnp.broadcast_to(gain_ref[...].astype(f32), (rows - filled, part)))
-        value = jnp.concatenate(blocks, axis=0).astype(packed_ref.dtype)
-        packed_ref[group] = value
-        for x in range(spread_ref.shape[0]):
-            spread_ref[x, group] = value
-
-
-def attention_kernel(
-    count_ref, own_ref, far_ref, own_swap_ref, far_swap_ref, weight_ref, cos_ref, sin_ref,
-    out_ref, normed_ref, *, query_len, passage_rows,
-):
-    bf16, f32, i32 = jnp.bfloat16, jnp.float32, jnp.int32
+        packed_ref[group] = jnp.concatenate(blocks, axis=0).astype(packed_ref.dtype)
+
+
+def norm_kernel(own_ref, far_ref, own_swap_ref, far_swap_ref, normed_ref, *, gain_row):
+    bf16, f32 = jnp.bfloat16, jnp.float32
     spread, groups, rows, part = own_ref.shape
     width = 4 * spread * part
-    pairs = count_ref.shape[0] // groups
-    gain_row = query_len + pairs * passage_rows
     core, high = lax.axis_index("c"), lax.axis_index("h")
     quarters = (
         (own_ref, high, core),
@@ -84,6 +76,14 @@
                 normed_ref[group * rows : (group + 1) * rows, pl.ds(begin, part)] = (
                     chunk * inverse * gain
                 ).astype(bf16)
+
+
+def attention_kernel(
+    count_ref, normed_ref, weight_ref, cos_ref, sin_ref, out_ref, spread_ref, *, query_len, passage_rows
+):
+    bf16, f32, i32 = jnp.bfloat16, jnp.float32, jnp.int32
+    groups, rows, _ = out_ref.shape
+    pairs = count_ref.shape[0] // groups
     projected = jnp.dot(
         normed_ref[...], weight_ref[:, : 3 * HEAD_DIM], preferred_element_type=f32
     )
@@ -120,30 +120,33 @@
         exponent = jnp.exp(scores - jnp.max(scores, axis=-1, keepdims=True))
         weights = (exponent / jnp.sum(exponent, axis=-1, keepdims=True)).astype(bf16)
         attended = jnp.dot(weights, values, preferred_element_type=f32).astype(bf16)
-        for t in range(out_ref.shape[1]):
-            out_ref[group, t] = attended
-
-
-def output_kernel(heads_ref, own_ref, other_ref, near_ref, far_ref, out_ref, *, query_len, pairs, passage_rows):
+        out_ref[group] = attended
+        for x in range(spread_ref.shape[1]):
+            spread_ref[group, x] = attended
+
+
+def output_kernel(own_heads_ref, far_heads_ref, own_ref, other_ref, near_ref, far_ref, out_ref, *, query_len, pairs, passage_rows):
     bf16, f32 = jnp.bfloat16, jnp.float32
     core = lax.axis_index("c")
     numbers = (((1,), (1,)), ((), ()))
-    tensors = heads_ref.shape[0] // 2
-    columns = own_ref.shape[0] // tensors
+    spread = own_heads_ref.shape[0] // 2
+    columns = own_ref.shape[0] // (2 * spread)
     near, far = near_ref[...], far_ref[...]
     first = core == 0
     final = jnp.concatenate(
         [jnp.where(first, near, far), jnp.where(first, far, near)], axis=1
     ).astype(f32)
     summed = jnp.zeros(final.shape, f32)
-    for t in range(tensors):
-        block = slice(t * columns, (t + 1) * columns)
-        partial_value = lax.dot_general(
-            heads_ref[core * tensors + t], own_ref[block], numbers, preferred_element_type=f32
-        ) + lax.dot_general(
-            heads_ref[(1 - core) * tensors + t], other_ref[block], numbers, preferred_element_type=f32
-        )
-        summed = summed + partial_value.astype(bf16).astype(f32)
+    high = lax.axis_index("h")
+    for heads_ref, upper in ((own_heads_ref, high), (far_heads_ref, 1 - high)):
+        for x in range(spread):
+            block = pl.ds(pl.multiple_of((upper * spread + x) * columns, columns), columns)
+            partial_value = lax.dot_general(
+                heads_ref[core * spread + x], own_ref[block], numbers, preferred_element_type=f32
+            ) + lax.dot_general(
+                heads_ref[(1 - core) * spread + x], other_ref[block], numbers, preferred_element_type=f32
+            )
+            summed = summed + partial_value.astype(bf16).astype(f32)
     final = final + summed
     blocks = []
     for pair in range(pairs):
@@ -206,7 +209,7 @@
     live = query_len + pairs * passage_rows
     rows = (live // ROW_TILE + 1) * ROW_TILE
     depth = project_weight.shape[0]
-    options = pltpu.CompilerParams(vmem_limit_bytes=8 * MIB)
+    options = pltpu.CompilerParams(vmem_limit_bytes=6 * MIB)
 
     raw = jnp.concatenate([corpus_rows.reshape(-1, features), query_rows[0]], axis=0)
     keep, give = halves(raw, part)
@@ -254,22 +257,20 @@
     stored_at = lax.dynamic_index_in_dim(owner * stored + place, here, axis=0, keepdims=False)
     counts = jnp.take(passage_length, stored_at.reshape(-1), axis=0, mode="clip")
     gain, _ = halves(norm_gain[None], part)
-    packed, spread = pl.pallas_call(
+    packed = pl.pallas_call(
         pack_kernel,
-        out_shape=[
-            jax.ShapeDtypeStruct((cores, rows, part), bf16),
-            jax.ShapeDtypeStruct((SIZE["x"], cores, rows, part), bf16),
-        ],
+        out_shape=jax.ShapeDtypeStruct((cores, rows, part), bf16),
         in_specs=[SMEM] * 2 + [VMEM] * (lines + 2),
-        out_specs=[VMEM] * 2,
+        out_specs=VMEM,
         compiler_params=options,
         name="pack",
     )(source.reshape(-1), counts, *arrived, queries, gain)
 
-    own_full = lax.all_to_all(spread, "x", split_axis=0, concat_axis=0, tiled=True)
+    own_full = on_every(packed, "x")
     far_full = on_every(partner(packed, "h", 1), "x")
     own_swap = partner(own_full, "c", 1)
     far_swap = partner(far_full, "c", 1)
+    far_swap, weight = lax.optimization_barrier((far_swap, weight))
 
     row = np.arange(rows)
     slot = np.where(row < query_len, row, query_len + (row - query_len) % passage_rows)
@@ -277,37 +278,48 @@
     frequency = np.power(10000.0, -2.0 * np.arange(half) / HEAD_DIM).astype(np.float32)
     angles = slot.astype(np.float32)[:, None] * frequency[None, :]
     cosine, sine = np.cos(angles), np.sin(angles)
-    attended = pl.pallas_call(
+    normed = pl.pallas_call(
+        functools.partial(norm_kernel, gain_row=live),
+        out_shape=jax.ShapeDtypeStruct((cores * rows, tensors * features), bf16),
+        in_specs=[VMEM] * 4,
+        out_specs=VMEM,
+        compiler_params=pltpu.CompilerParams(vmem_limit_bytes=16 * MIB),
+        cost_estimate=pl.CostEstimate(
+            flops=8 * rows * tensors * features,
+            bytes_accessed=8 * MIB,
+            transcendentals=2 * rows,
+        ),
+        name="norm",
+    )(own_full, far_full, own_swap, far_swap)
+    attended, spread = pl.pallas_call(
         functools.partial(attention_kernel, query_len=query_len, passage_rows=passage_rows),
-        out_shape=jax.ShapeDtypeStruct((cores, tensors, rows, HEAD_DIM), bf16),
-        in_specs=[SMEM] + [VMEM] * 7,
-        out_specs=VMEM,
-        scratch_shapes=[pltpu.VMEM((cores * rows, tensors * features), bf16)],
-        compiler_params=pltpu.CompilerParams(vmem_limit_bytes=24 * MIB),
+        out_shape=[
+            jax.ShapeDtypeStruct((cores, rows, HEAD_DIM), bf16),
+            jax.ShapeDtypeStruct((cores, SIZE["x"], rows, HEAD_DIM), bf16),
+        ],
+        in_specs=[SMEM] + [VMEM] * 4,
+        out_specs=[VMEM] * 2,
+        compiler_params=pltpu.CompilerParams(vmem_limit_bytes=16 * MIB),
         cost_estimate=pl.CostEstimate(
             flops=2 * rows * tensors * features * 6 * HEAD_DIM,
-            bytes_accessed=8 * 1024 * 1024,
+            bytes_accessed=8 * MIB,
             transcendentals=2 * rows * rows,
         ),
         name="attention",
     )(
         counts,
-        own_full,
-        far_full,
-        own_swap,
-        far_swap,
+        normed,
         weight,
         jnp.asarray(np.concatenate([cosine, cosine], axis=1), f32),
         jnp.asarray(np.concatenate([-sine, sine], axis=1), f32),
     )
 
-    heads = lax.all_to_all(
-        attended.reshape(-1, rows, HEAD_DIM),
-        ("c",) + TENSOR,
-        split_axis=0,
-        concat_axis=0,
-        tiled=True,
-    )
+    far = partner(attended, "h", 1)
+    own_heads = lax.all_to_all(
+        spread.reshape(-1, rows, HEAD_DIM), ("c", "x"), split_axis=0, concat_axis=0, tiled=True
+    )
+    far = jnp.broadcast_to(far[:, None], spread.shape).reshape(own_heads.shape)
+    far_heads = lax.all_to_all(far, ("c", "x"), split_axis=0, concat_axis=0, tiled=True)
     own_out = weight[:, 3 * HEAD_DIM :]
     own_out, _ = lax.optimization_barrier((own_out, attended))
     other_out = partner(own_out, "c", 1)
@@ -321,7 +333,7 @@
             output_kernel, query_len=query_len, pairs=pairs, passage_rows=passage_rows
         ),
         out_shape=jax.ShapeDtypeStruct((pairs * (query_len + passage_rows), features), bf16),
-        in_specs=[VMEM] * 5,
+        in_specs=[VMEM] * 6,
         out_specs=VMEM,
         compiler_params=options,
         cost_estimate=pl.CostEstimate(
@@ -330,7 +342,7 @@
             transcendentals=0,
         ),
         name="output",
-    )(heads, own_out, other_out, near_rows, far_rows)
+    )(own_heads, far_heads, own_out, other_out, near_rows, far_rows)
 
 
 def solution(mesh):

time: 177 us -> 184 us (1.040)
  the two profiles are of different devices: /device:TPU:9 before, /device:TPU:1 now
where the time goes in v6:
time: 184 us; the launch traced here: 182 us
  starting transfers between devices  83.1 us (45%)
  waiting for transfers between devices  44.4 us (24%)
  between operations  13.8 us (8%)
  blocking collectives  13.1 us (7%)
  local copies, waits for them, and re-layouts  11.8 us (6%)
  Pallas kernels  11.2 us (6%)
  other arithmetic  4.51 us (2%)
    ppermute x13, starting transfers between devices, partner(): return lax.ppermute(value, axis, [(i, i ^ bit) for i in range(SIZE[axis])])  69.1 us
    ppermute x13, waiting for transfers between devices, partner(): return lax.ppermute(value, axis, [(i, i ^ bit) for i in range(SIZE[axis])])  21.9 us
    all_gather x1, waiting for transfers between devices, on_device(): library = lax.all_gather(held, 'z', axis=0, tiled=True)  15.1 us
    all_to_all x1, blocking collectives, on_every(): return lax.all_to_all(spread, axis, split_axis=0, concat_axis=0, tiled=True)  13.1 us
    all_to_all x1, waiting for transfers between devices, on_device(): lax.all_to_all(far, ('c', 'x'), split_axis=0, concat_axis=0, tiled=True)  7.39 us
    all_to_all x1, starting transfers between devices, on_device(): lax.all_to_all(far, ('c', 'x'), split_axis=0, concat_axis=0, tiled=True)  5.21 us
    pallas_call x1, Pallas kernels, on_device(): pl.pallas_call(functools.partial(attention_kernel, query_len=query_len, p...  3.85 us
    all_to_all x1, starting transfers between devices, on_device(): lax.all_to_all(spread.reshape(-1, rows, HEAD_DIM), ('c', 'x'), split_axis...  3.82 us
  transfers between devices with their start and end apart: 19, of which 10 were waited for; matrix products, arithmetic and copies ran while one was open for 5% of the time, Pallas kernels for 1%

profile of v6, /device:TPU:1, one launch (start us, length us, event | category | flops | bytes accessed | tf_op | source)
XLA Modules:
  0.0 181.8 jit_solution(11238346832314484442)
XLA Ops:
  7.6 8.8 %collective-permute-start = (bf16[200,256]{1,0:T(8,128)(2,1)S(1)}, bf16[200,256]{1,0:T(8,128)(2,1)S(1)}, u32[]{:S(2)}, u32[]{:S(2)}) collective-permute-start(bf16[200,256]{1,0:T(8,128)(2,1)S(1)} %broadcast_select_fusion), channel_id=1, source_target_pairs={{0,8},{8,0},{1,9},{9,1},{2,10},{10,2},{3,11},{11,3},{4,12},{12,4},... | collective-permute-start | bytes 307208 | tf_op jit(solution)/shard_map/ppermute | solution.py:159
  23.1 2.3 %collective-permute-start.2 = (bf16[72,512]{1,0:T(8,128)(2,1)S(1)}, bf16[72,512]{1,0:T(8,128)(2,1)S(1)}, u32[]{:S(2)}, u32[]{:S(2)}) collective-permute-start(bf16[72,512]{1,0:T(8,128)(2,1)S(1)} %select_bitcast_fusion.2), channel_id=1, source_target_pairs={{0,8},{8,0},{1,9},{9,1},{2,10},{10,2},{3,11},{11,3},{4,12},{12,4},... | collective-permute-start | bytes 221192 | tf_op jit(solution)/shard_map/ppermute | solution.py:159
  30.2 5.4 %collective-permute-start.5 = (bf16[2,72,512]{2,1,0:T(8,128)(2,1)S(1)}, bf16[2,72,512]{2,1,0:T(8,128)(2,1)S(1)}, u32[]{:S(2)}, u32[]{:S(2)}) collective-permute-start(bf16[2,72,512]{2,1,0:T(8,128)(2,1)S(1)} %get-tuple-element.36), channel_id=1, source_target_pairs={{0,48},{16,32},{32,16},{48,0},{1,49},{17,33},{33,17},{49,1},{2,50}... | collective-permute-start | bytes 442376 | tf_op jit(solution)/shard_map/ppermute | solution.py:159
  35.7 3.1 %collective-permute-done.3 = bf16[2,72,512]{2,1,0:T(8,128)(2,1)S(1)} collective-permute-done((bf16[2,72,512]{2,1,0:T(8,128)(2,1)S(1)}, bf16[2,72,512]{2,1,0:T(8,128)(2,1)S(1)}, u32[]{:S(2)}, u32[]{:S(2)}) %collective-permute-start.3) | collective-permute-done | bytes 147488 | tf_op jit(solution)/shard_map/ppermute | solution.py:159
  42.7 15.1 %all-gather.3.cloned.1.call-done.library_ref = bf16[128,24,256]{2,1,0:T(8,128)(2,1)} async-done(((bf16[16,24,256]{2,1,0:T(8,128)(2,1)}), bf16[128,24,256]{2,1,0:T(8,128)(2,1)}) %all-gather.3.cloned.1.call-update) | async-done | bytes 1572880 | tf_op jit(solution)/shard_map/all_gather | solution.py:222
  59.7 3.1 %collective-permute-start.6 = (bf16[16,24,256]{2,1,0:T(8,128)(2,1)S(1)}, bf16[16,24,256]{2,1,0:T(8,128)(2,1)S(1)}, u32[]{:S(2)}, u32[]{:S(2)}) collective-permute-start(bf16[16,24,256]{2,1,0:T(8,128)(2,1)S(1)} %get-tuple-element.21), channel_id=1, source_target_pairs={{0,16},{16,0},{32,48},{48,32},{1,17},{17,1},{33,49},{49,33},{2,18}... | collective-permute-start | bytes 589832 | tf_op jit(solution)/shard_map/ppermute | solution.py:159
  62.9 4.1 %collective-permute-start.7 = (bf16[16,24,256]{2,1,0:T(8,128)(2,1)S(1)}, bf16[16,24,256]{2,1,0:T(8,128)(2,1)S(1)}, u32[]{:S(2)}, u32[]{:S(2)}) collective-permute-start(bf16[16,24,256]{2,1,0:T(8,128)(2,1)S(1)} %get-tuple-element.22), channel_id=1, source_target_pairs={{0,32},{16,48},{32,0},{48,16},{1,33},{17,49},{33,1},{49,17},{2,34}... | collective-permute-start | bytes 589832 | tf_op jit(solution)/shard_map/ppermute | solution.py:159
  67.0 2.0 %collective-permute-start.8 = (bf16[16,24,256]{2,1,0:T(8,128)(2,1)S(1)}, bf16[16,24,256]{2,1,0:T(8,128)(2,1)S(1)}, u32[]{:S(2)}, u32[]{:S(2)}) collective-permute-start(bf16[16,24,256]{2,1,0:T(8,128)(2,1)S(1)} %get-tuple-element.23), channel_id=1, source_target_pairs={{0,48},{16,32},{32,16},{48,0},{1,49},{17,33},{33,17},{49,1},{2,50}... | collective-permute-start | bytes 589832 | tf_op jit(solution)/shard_map/ppermute | solution.py:159
  69.8 2.6 %collective-permute-done.7.refs_2_ = bf16[16,24,256]{2,1,0:T(8,128)(2,1)S(1)} collective-permute-done((bf16[16,24,256]{2,1,0:T(8,128)(2,1)S(1)}, bf16[16,24,256]{2,1,0:T(8,128)(2,1)S(1)}, u32[]{:S(2)}, u32[]{:S(2)}) %collective-permute-start.7) | collective-permute-done | bytes 196640 | tf_op jit(solution)/shard_map/ppermute | solution.py:159
  72.4 4.7 %collective-permute-done.8.refs_3_ = bf16[16,24,256]{2,1,0:T(8,128)(2,1)S(1)} collective-permute-done((bf16[16,24,256]{2,1,0:T(8,128)(2,1)S(1)}, bf16[16,24,256]{2,1,0:T(8,128)(2,1)S(1)}, u32[]{:S(2)}, u32[]{:S(2)}) %collective-permute-start.8) | collective-permute-done | bytes 196640 | tf_op jit(solution)/shard_map/ppermute | solution.py:159
  77.8 5.5 %collective-permute-start.9 = (bf16[2,208,256]{2,1,0:T(8,128)(2,1)S(1)}, bf16[2,208,256]{2,1,0:T(8,128)(2,1)S(1)}, u32[]{:S(2)}, u32[]{:S(2)}) collective-permute-start(bf16[2,208,256]{2,1,0:T(8,128)(2,1)S(1)} %pack.1), channel_id=1, source_target_pairs={{0,4},{4,0},{1,5},{5,1},{2,6},{6,2},{3,7},{7,3},{8,12},{12,8},{9,1... | collective-permute-start | bytes 638984 | tf_op jit(solution)/shard_map/ppermute | solution.py:159
  83.3 5.1 %collective-permute-done.9 = bf16[2,208,256]{2,1,0:T(8,128)(2,1)S(1)} collective-permute-done((bf16[2,208,256]{2,1,0:T(8,128)(2,1)S(1)}, bf16[2,208,256]{2,1,0:T(8,128)(2,1)S(1)}, u32[]{:S(2)}, u32[]{:S(2)}) %collective-permute-start.9) | collective-permute-done | bytes 213024 | tf_op jit(solution)/shard_map/ppermute | solution.py:159
  88.4 13.1 %all_to_all.20.far_ref = bf16[4,2,208,256]{3,2,1,0:T(8,128)(2,1)S(1)} all-to-all(bf16[4,2,208,256]{3,2,1,0:T(8,128)(2,1)S(1)} %broadcast_in_dim.36), channel_id=1, replica_groups=mesh['z'=8,'y'=4,'c'=2,'h'=2,'x'=4] {'x'}, dimensions={0} | all-to-all | bytes 1703936 | tf_op jit(solution)/shard_map/all_to_all | solution.py:188
  102.6 3.5 %all-to-all-start = ((bf16[4,2,208,256]{3,2,1,0:T(8,128)(2,1)}), bf16[4,2,208,256]{3,2,1,0:T(8,128)(2,1)S(1)}, u32[]{:S(2)}, u32[]{:S(2)}) async-start(bf16[4,2,208,256]{3,2,1,0:T(8,128)(2,1)} %broadcast_in_dim.35), calls=%async_computation | async-start | bytes 1703936 | tf_op jit(solution)/shard_map/all_to_all | solution.py:188
  106.1 14.3 %collective-permute-start.11 = (bf16[4,2,208,256]{3,2,1,0:T(8,128)(2,1)S(1)}, bf16[4,2,208,256]{3,2,1,0:T(8,128)(2,1)S(1)}, u32[]{:S(2)}, u32[]{:S(2)}) collective-permute-start(bf16[4,2,208,256]{3,2,1,0:T(8,128)(2,1)S(1)} %all_to_all.20.far_ref), channel_id=1, source_target_pairs={{0,8},{8,0},{1,9},{9,1},{2,10},{10,2},{3,11},{11,3},{4,12},{12,4},... | collective-permute-start | bytes 2555912 | tf_op jit(solution)/shard_map/ppermute | solution.py:159
  120.4 9.8 %collective-permute-start.10 = (bf16[4,2,208,256]{3,2,1,0:T(8,128)(2,1)S(1)}, bf16[4,2,208,256]{3,2,1,0:T(8,128)(2,1)}, u32[]{:S(2)}, u32[]{:S(2)}) collective-permute-start(bf16[4,2,208,256]{3,2,1,0:T(8,128)(2,1)S(1)} %all-to-all-done.own_ref), channel_id=1, source_target_pairs={{0,8},{8,0},{1,9},{9,1},{2,10},{10,2},{3,11},{11,3},{4,12},{12,4},... | collective-permute-start | bytes 2555912 | tf_op jit(solution)/shard_map/ppermute | solution.py:159
  133.8 3.0 %norm.1.normed_ref = bf16[416,4096]{1,0:T(8,128)(2,1)S(1)} custom-call(bf16[4,2,208,256]{3,2,1,0:T(8,128)(2,1)S(1)} %all-to-all-done.own_ref, bf16[4,2,208,256]{3,2,1,0:T(8,128)(2,1)S(1)} %all_to_all.20.far_ref, bf16[4,2,208,256]{3,2,1,0:T(8,128)(2,1)} %collective-permute-done.10.own_swap_ref, bf16[4,2,208,256]{3,2,1,0:T(8,128)(2,1)S(1)} %copy-done.4), custom_call_target="tpu_custom_call" | custom-call | flops 6815744 | bytes 8388608 | tf_op jit(solution)/shard_map/norm/pallas_call | solution.py:281
  136.8 3.9 %attention.1 = (bf16[2,208,128]{2,1,0:T(8,128)(2,1)S(1)}, bf16[2,4,208,128]{3,2,1,0:T(8,128)(2,1)}) custom-call(s32[16]{0:T(128)S(1)} %gather_fusion.1, bf16[416,4096]{1,0:T(8,128)(2,1)S(1)} %norm.1.normed_ref, bf16[4096,512]{1,0:T(8,128)(2,1)S(1)} %copy-done.1, f32[208,128]{1,0:T(8,128)S(1)} %copy-done.6, f32[208,128]{1,0:T(8,128)S(1)} %copy-done.5), custom_call_target="tpu_custom_call" | custom-call | flops 1308622848 | bytes 8388608 | tf_op jit(solution)/shard_map/attention/pallas_call | solution.py:294
  142.7 3.8 %all-to-all-start.2 = ((bf16[8,208,128]{2,1,0:T(8,128)(2,1)}), bf16[8,208,128]{2,1,0:T(8,128)(2,1)S(1)}, u32[]{:S(2)}, u32[]{:S(2)}) async-start(bf16[8,208,128]{2,1,0:T(8,128)(2,1)} %bitcast.19), calls=%async_computation.2 | async-start | bytes 851968 | tf_op jit(solution)/shard_map/all_to_all | solution.py:318
  146.5 7.9 %collective-permute-start.12 = (bf16[2,208,128]{2,1,0:T(8,128)(2,1)S(1)}, bf16[2,208,128]{2,1,0:T(8,128)(2,1)S(1)}, u32[]{:S(2)}, u32[]{:S(2)}) collective-permute-start(bf16[2,208,128]{2,1,0:T(8,128)(2,1)S(1)} %get-tuple-element.27), channel_id=1, source_target_pairs={{0,4},{4,0},{1,5},{5,1},{2,6},{6,2},{3,7},{7,3},{8,12},{12,8},{9,1... | collective-permute-start | bytes 319496 | tf_op jit(solution)/shard_map/ppermute | solution.py:159
  154.4 3.2 %collective-permute-done.12 = bf16[2,208,128]{2,1,0:T(8,128)(2,1)S(1)} collective-permute-done((bf16[2,208,128]{2,1,0:T(8,128)(2,1)S(1)}, bf16[2,208,128]{2,1,0:T(8,128)(2,1)S(1)}, u32[]{:S(2)}, u32[]{:S(2)}) %collective-permute-start.12) | collective-permute-done | bytes 106528 | tf_op jit(solution)/shard_map/ppermute | solution.py:159
  158.5 5.2 %all-to-all-start.3 = ((bf16[8,208,128]{2,1,0:T(8,128)(2,1)}), bf16[8,208,128]{2,1,0:T(8,128)(2,1)S(1)}, u32[]{:S(2)}, u32[]{:S(2)}) async-start(bf16[8,208,128]{2,1,0:T(8,128)(2,1)} %bitcast.20), calls=%async_computation.3 | async-start | bytes 851968 | tf_op jit(solution)/shard_map/all_to_all | solution.py:322
  164.6 7.4 %all-to-all-done.3.far_heads_ref = bf16[8,208,128]{2,1,0:T(8,128)(2,1)S(1)} async-done(((bf16[8,208,128]{2,1,0:T(8,128)(2,1)}), bf16[8,208,128]{2,1,0:T(8,128)(2,1)S(1)}, u32[]{:S(2)}, u32[]{:S(2)}) %all-to-all-start.3) | async-done | bytes 426016 | tf_op jit(solution)/shard_map/all_to_all | solution.py:322
  172.0 3.0 %output.1 = bf16[256,512]{1,0:T(8,128)(2,1)} custom-call(bf16[8,208,128]{2,1,0:T(8,128)(2,1)S(1)} %all-to-all-done.2.own_heads_ref, bf16[8,208,128]{2,1,0:T(8,128)(2,1)S(1)} %all-to-all-done.3.far_heads_ref, bf16[4096,128]{1,0:T(8,128)(2,1)S(1)} %slice.53.own_ref, bf16[4096,128]{1,0:T(8,128)(2,1)} %collective-permute-done.13.other_ref, ...), custom_call_target="tpu_custom_call" | custom-call | flops 436207616 | bytes 3145728 | tf_op jit(solution)/shard_map/output/pallas_call | solution.py:331
  (79 shorter events, 28.1 us)
Async XLA Ops:
  6.5 62.6 %copy-start = (s32[512]{0:T(512)S(1)}, s32[512]{0:T(512)}, u32[]{:S(2)}) copy-start(s32[512]{0:T(512)} %param.12) | copy-start | bytes 6148
  6.5 51.2 %all-gather.3.cloned.1.call-start = ((), (), s32[]{:S(2)}) async-start(), calls=%async_computation.4 | async-start | bytes 1769472 | tf_op jit(solution)/shard_map/all_gather | solution.py:222
  7.6 9.7 %collective-permute-start = (bf16[200,256]{1,0:T(8,128)(2,1)S(1)}, bf16[200,256]{1,0:T(8,128)(2,1)S(1)}, u32[]{:S(2)}, u32[]{:S(2)}) collective-permute-start(bf16[200,256]{1,0:T(8,128)(2,1)S(1)} %broadcast_select_fusion), channel_id=1, source_target_pairs={{0,8},{8,0},{1,9},{9,1},{2,10},{10,2},{3,11},{11,3},{4,12},{12,4},... | collective-permute-start | bytes 307208 | tf_op jit(solution)/shard_map/ppermute | solution.py:159
  18.4 23.3 %copy-start.7 = (bf16[512]{0:T(512)(128)(2,1)S(1)}, bf16[512]{0:T(512)(128)(2,1)}, u32[]{:S(2)}) copy-start(bf16[512]{0:T(512)(128)(2,1)} %param.15) | copy-start | bytes 3076
  19.1 112.0 %all-gather.5.cloned.1.call-start = ((), (), s32[]{:S(2)}) async-start(), calls=%async_computation.5 | async-start | bytes 4718592 | tf_op jit(solution)/shard_map/all_gather | solution.py:238
  20.5 2.6 %collective-permute-start.1 = (bf16[64,256]{1,0:T(8,128)(2,1)}, bf16[64,256]{1,0:T(8,128)(2,1)S(1)}, u32[]{:S(2)}, u32[]{:S(2)}) collective-permute-start(bf16[64,256]{1,0:T(8,128)(2,1)} %bitcast.60), channel_id=1, source_target_pairs={{0,0},{1,64},{2,128},{3,192},{4,256},{5,320},{6,384},{7,448},{8,8}... | collective-permute-start | bytes 98312 | tf_op jit(solution)/shard_map/ppermute | solution.py:227
  23.1 3.2 %collective-permute-start.2 = (bf16[72,512]{1,0:T(8,128)(2,1)S(1)}, bf16[72,512]{1,0:T(8,128)(2,1)S(1)}, u32[]{:S(2)}, u32[]{:S(2)}) collective-permute-start(bf16[72,512]{1,0:T(8,128)(2,1)S(1)} %select_bitcast_fusion.2), channel_id=1, source_target_pairs={{0,8},{8,0},{1,9},{9,1},{2,10},{10,2},{3,11},{11,3},{4,12},{12,4},... | collective-permute-start | bytes 221192 | tf_op jit(solution)/shard_map/ppermute | solution.py:159
  26.4 9.3 %collective-permute-start.4 = (bf16[2,72,512]{2,1,0:T(8,128)(2,1)S(1)}, bf16[2,72,512]{2,1,0:T(8,128)(2,1)S(1)}, u32[]{:S(2)}, u32[]{:S(2)}) collective-permute-start(bf16[2,72,512]{2,1,0:T(8,128)(2,1)S(1)} %get-tuple-element.36), channel_id=1, source_target_pairs={{0,32},{16,48},{32,0},{48,16},{1,33},{17,49},{33,1},{49,17},{2,34}... | collective-permute-start | bytes 442376 | tf_op jit(solution)/shard_map/ppermute | solution.py:159
  28.3 10.5 %collective-permute-start.3 = (bf16[2,72,512]{2,1,0:T(8,128)(2,1)S(1)}, bf16[2,72,512]{2,1,0:T(8,128)(2,1)S(1)}, u32[]{:S(2)}, u32[]{:S(2)}) collective-permute-start(bf16[2,72,512]{2,1,0:T(8,128)(2,1)S(1)} %get-tuple-element.36), channel_id=1, source_target_pairs={{0,16},{16,0},{32,48},{48,32},{1,17},{17,1},{33,49},{49,33},{2,18}... | collective-permute-start | bytes 442376 | tf_op jit(solution)/shard_map/ppermute | solution.py:159
  30.2 10.0 %collective-permute-start.5 = (bf16[2,72,512]{2,1,0:T(8,128)(2,1)S(1)}, bf16[2,72,512]{2,1,0:T(8,128)(2,1)S(1)}, u32[]{:S(2)}, u32[]{:S(2)}) collective-permute-start(bf16[2,72,512]{2,1,0:T(8,128)(2,1)S(1)} %get-tuple-element.36), channel_id=1, source_target_pairs={{0,48},{16,32},{32,16},{48,0},{1,49},{17,33},{33,17},{49,1},{2,50}... | collective-permute-start | bytes 442376 | tf_op jit(solution)/shard_map/ppermute | solution.py:159
  59.7 10.1 %collective-permute-start.6 = (bf16[16,24,256]{2,1,0:T(8,128)(2,1)S(1)}, bf16[16,24,256]{2,1,0:T(8,128)(2,1)S(1)}, u32[]{:S(2)}, u32[]{:S(2)}) collective-permute-start(bf16[16,24,256]{2,1,0:T(8,128)(2,1)S(1)} %get-tuple-element.21), channel_id=1, source_target_pairs={{0,16},{16,0},{32,48},{48,32},{1,17},{17,1},{33,49},{49,33},{2,18}... | collective-permute-start | bytes 589832 | tf_op jit(solution)/shard_map/ppermute | solution.py:159
  62.9 9.5 %collective-permute-start.7 = (bf16[16,24,256]{2,1,0:T(8,128)(2,1)S(1)}, bf16[16,24,256]{2,1,0:T(8,128)(2,1)S(1)}, u32[]{:S(2)}, u32[]{:S(2)}) collective-permute-start(bf16[16,24,256]{2,1,0:T(8,128)(2,1)S(1)} %get-tuple-element.22), channel_id=1, source_target_pairs={{0,32},{16,48},{32,0},{48,16},{1,33},{17,49},{33,1},{49,17},{2,34}... | collective-permute-start | bytes 589832 | tf_op jit(solution)/shard_map/ppermute | solution.py:159
  67.0 10.1 %collective-permute-start.8 = (bf16[16,24,256]{2,1,0:T(8,128)(2,1)S(1)}, bf16[16,24,256]{2,1,0:T(8,128)(2,1)S(1)}, u32[]{:S(2)}, u32[]{:S(2)}) collective-permute-start(bf16[16,24,256]{2,1,0:T(8,128)(2,1)S(1)} %get-tuple-element.23), channel_id=1, source_target_pairs={{0,48},{16,32},{32,16},{48,0},{1,49},{17,33},{33,17},{49,1},{2,50}... | collective-permute-start | bytes 589832 | tf_op jit(solution)/shard_map/ppermute | solution.py:159
  77.8 10.6 %collective-permute-start.9 = (bf16[2,208,256]{2,1,0:T(8,128)(2,1)S(1)}, bf16[2,208,256]{2,1,0:T(8,128)(2,1)S(1)}, u32[]{:S(2)}, u32[]{:S(2)}) collective-permute-start(bf16[2,208,256]{2,1,0:T(8,128)(2,1)S(1)} %pack.1), channel_id=1, source_target_pairs={{0,4},{4,0},{1,5},{5,1},{2,6},{6,2},{3,7},{7,3},{8,12},{12,8},{9,1... | collective-permute-start | bytes 638984 | tf_op jit(solution)/shard_map/ppermute | solution.py:159
  102.6 17.8 %all-to-all-start = ((bf16[4,2,208,256]{3,2,1,0:T(8,128)(2,1)}), bf16[4,2,208,256]{3,2,1,0:T(8,128)(2,1)S(1)}, u32[]{:S(2)}, u32[]{:S(2)}) async-start(bf16[4,2,208,256]{3,2,1,0:T(8,128)(2,1)} %broadcast_in_dim.35), calls=%async_computation | async-start | bytes 1703936 | tf_op jit(solution)/shard_map/all_to_all | solution.py:188
  106.1 24.1 %collective-permute-start.11 = (bf16[4,2,208,256]{3,2,1,0:T(8,128)(2,1)S(1)}, bf16[4,2,208,256]{3,2,1,0:T(8,128)(2,1)S(1)}, u32[]{:S(2)}, u32[]{:S(2)}) collective-permute-start(bf16[4,2,208,256]{3,2,1,0:T(8,128)(2,1)S(1)} %all_to_all.20.far_ref), channel_id=1, source_target_pairs={{0,8},{8,0},{1,9},{9,1},{2,10},{10,2},{3,11},{11,3},{4,12},{12,4},... | collective-permute-start | bytes 2555912 | tf_op jit(solution)/shard_map/ppermute | solution.py:159
  120.4 12.0 %collective-permute-start.10 = (bf16[4,2,208,256]{3,2,1,0:T(8,128)(2,1)S(1)}, bf16[4,2,208,256]{3,2,1,0:T(8,128)(2,1)}, u32[]{:S(2)}, u32[]{:S(2)}) collective-permute-start(bf16[4,2,208,256]{3,2,1,0:T(8,128)(2,1)S(1)} %all-to-all-done.own_ref), channel_id=1, source_target_pairs={{0,8},{8,0},{1,9},{9,1},{2,10},{10,2},{3,11},{11,3},{4,12},{12,4},... | collective-permute-start | bytes 2555912 | tf_op jit(solution)/shard_map/ppermute | solution.py:159
  132.4 4.4 %copy-start.1 = (bf16[4096,512]{1,0:T(8,128)(2,1)S(1)}, bf16[4096,512]{1,0:T(8,128)(2,1)}, u32[]{:S(2)}) copy-start(bf16[4096,512]{1,0:T(8,128)(2,1)} %all-gather.5.cloned.1.call-done.weight_ref) | copy-start | bytes 12582916
  133.8 3.1 %copy-start.5 = (f32[208,128]{1,0:T(8,128)S(1)}, f32[208,128]{1,0:T(8,128)}, u32[]{:S(2)}) copy-start(f32[208,128]{1,0:T(8,128)} %constant.81.clone.sin_ref) | copy-start | bytes 319492
  133.8 3.1 %copy-start.6 = (f32[208,128]{1,0:T(8,128)S(1)}, f32[208,128]{1,0:T(8,128)}, u32[]{:S(2)}) copy-start(f32[208,128]{1,0:T(8,128)} %constant.80.clone.cos_ref) | copy-start | bytes 319492
  140.7 31.3 %collective-permute-start.13 = (bf16[4096,128]{1,0:T(8,128)(2,1)S(1)}, bf16[4096,128]{1,0:T(8,128)(2,1)}, u32[]{:S(2)}, u32[]{:S(2)}) collective-permute-start(bf16[4096,128]{1,0:T(8,128)(2,1)S(1)} %slice.53.own_ref), channel_id=1, source_target_pairs={{0,8},{8,0},{1,9},{9,1},{2,10},{10,2},{3,11},{11,3},{4,12},{12,4},... | collective-permute-start | bytes 3145736 | tf_op jit(solution)/shard_map/ppermute | solution.py:159
  142.7 15.0 %all-to-all-start.2 = ((bf16[8,208,128]{2,1,0:T(8,128)(2,1)}), bf16[8,208,128]{2,1,0:T(8,128)(2,1)S(1)}, u32[]{:S(2)}, u32[]{:S(2)}) async-start(bf16[8,208,128]{2,1,0:T(8,128)(2,1)} %bitcast.19), calls=%async_computation.2 | async-start | bytes 851968 | tf_op jit(solution)/shard_map/all_to_all | solution.py:318
  146.5 11.2 %collective-permute-start.12 = (bf16[2,208,128]{2,1,0:T(8,128)(2,1)S(1)}, bf16[2,208,128]{2,1,0:T(8,128)(2,1)S(1)}, u32[]{:S(2)}, u32[]{:S(2)}) collective-permute-start(bf16[2,208,128]{2,1,0:T(8,128)(2,1)S(1)} %get-tuple-element.27), channel_id=1, source_target_pairs={{0,4},{4,0},{1,5},{5,1},{2,6},{6,2},{3,7},{7,3},{8,12},{12,8},{9,1... | collective-permute-start | bytes 319496 | tf_op jit(solution)/shard_map/ppermute | solution.py:159
  158.5 13.5 %all-to-all-start.3 = ((bf16[8,208,128]{2,1,0:T(8,128)(2,1)}), bf16[8,208,128]{2,1,0:T(8,128)(2,1)S(1)}, u32[]{:S(2)}, u32[]{:S(2)}) async-start(bf16[8,208,128]{2,1,0:T(8,128)(2,1)} %bitcast.20), calls=%async_computation.3 | async-start | bytes 851968 | tf_op jit(solution)/shard_map/all_to_all | solution.py:322
  (3 other events, 3.6 us)
Sparse Core Ops, SparseCore 0:
  19.2 38.4 all-gather.2
  59.8 60.3 all-gather.4

commit v7 on v5

--- a/solution.py
+++ b/solution.py
@@ -29,7 +29,7 @@
 
 def pack_kernel(source_ref, count_ref, *refs):
     f32 = jnp.float32
-    part_refs, (query_ref, gain_ref, packed_ref, spread_ref) = refs[:-4], refs[-4:]
+    part_refs, (query_ref, gain_ref, packed_ref) = refs[:-3], refs[-3:]
     groups, rows, part = packed_ref.shape
     passage_rows = part_refs[0].shape[1]
     pairs = part_refs[0].shape[0] // groups
@@ -45,10 +45,12 @@
             blocks.append(jnp.where(place < count_ref[spot], passage, 0.0))
         filled = blocks[0].shape[0] + pairs * passage_rows
         blocks.append(jnp.broadcast_to(gain_ref[...].astype(f32), (rows - filled, part)))
-        value = jnp.concatenate(blocks, axis=0).astype(packed_ref.dtype)
-        packed_ref[group] = value
-        for x in range(spread_ref.shape[0]):
-            spread_ref[x, group] = value
+        packed_ref[group] = jnp.concatenate(blocks, axis=0).astype(packed_ref.dtype)
+
+
+def spread_kernel(packed_ref, spread_ref):
+    for x in range(spread_ref.shape[0]):
+        spread_ref[x] = packed_ref[...]
 
 
 def attention_kernel(
@@ -85,7 +87,7 @@
                     chunk * inverse * gain
                 ).astype(bf16)
     projected = jnp.dot(
-        normed_ref[...], weight_ref[:, : 3 * HEAD_DIM], preferred_element_type=f32
+        normed_ref[...], weight_ref[...], preferred_element_type=f32
     )
 
     def rotate(inputs):
@@ -206,7 +208,7 @@
     live = query_len + pairs * passage_rows
     rows = (live // ROW_TILE + 1) * ROW_TILE
     depth = project_weight.shape[0]
-    options = pltpu.CompilerParams(vmem_limit_bytes=8 * MIB)
+    options = pltpu.CompilerParams(vmem_limit_bytes=6 * MIB)
 
     raw = jnp.concatenate([corpus_rows.reshape(-1, features), query_rows[0]], axis=0)
     keep, give = halves(raw, part)
@@ -232,7 +234,8 @@
     weight = gather_plane(weight)
     asked = weight[:, :, depth, : 2 * pairs].astype(i32)
     weight = weight[:, :, :depth].reshape(plane * depth, 4 * HEAD_DIM)
-    weight = lax.all_gather(weight, "z", axis=0, tiled=True)
+    own_out = lax.all_gather(weight[:, 3 * HEAD_DIM :], "z", axis=0, tiled=True)
+    weight = lax.all_gather(weight[:, : 3 * HEAD_DIM], "z", axis=0, tiled=True)
 
     owner, place = asked[:, :, :pairs], asked[:, :, pairs:]
     owner_z, owner_y, owner_c = owner // plane, owner // cores % lines, owner % cores
@@ -254,21 +257,29 @@
     stored_at = lax.dynamic_index_in_dim(owner * stored + place, here, axis=0, keepdims=False)
     counts = jnp.take(passage_length, stored_at.reshape(-1), axis=0, mode="clip")
     gain, _ = halves(norm_gain[None], part)
-    packed, spread = pl.pallas_call(
+    packed = pl.pallas_call(
         pack_kernel,
-        out_shape=[
-            jax.ShapeDtypeStruct((cores, rows, part), bf16),
-            jax.ShapeDtypeStruct((SIZE["x"], cores, rows, part), bf16),
-        ],
+        out_shape=jax.ShapeDtypeStruct((cores, rows, part), bf16),
         in_specs=[SMEM] * 2 + [VMEM] * (lines + 2),
-        out_specs=[VMEM] * 2,
+        out_specs=VMEM,
         compiler_params=options,
         name="pack",
     )(source.reshape(-1), counts, *arrived, queries, gain)
 
-    own_full = lax.all_to_all(spread, "x", split_axis=0, concat_axis=0, tiled=True)
-    far_full = on_every(partner(packed, "h", 1), "x")
+    far = partner(packed, "h", 1)
+    own_full = on_every(packed, "x")
+    far = pl.pallas_call(
+        spread_kernel,
+        out_shape=jax.ShapeDtypeStruct((SIZE["x"],) + packed.shape, bf16),
+        in_specs=[VMEM],
+        out_specs=VMEM,
+        compiler_params=options,
+        cost_estimate=pl.CostEstimate(flops=0, bytes_accessed=4 * MIB, transcendentals=0),
+        name="spread",
+    )(far)
+    far_full = lax.all_to_all(far, "x", split_axis=0, concat_axis=0, tiled=True)
     own_swap = partner(own_full, "c", 1)
+    far_full, weight = lax.optimization_barrier((far_full, weight))
     far_swap = partner(far_full, "c", 1)
 
     row = np.arange(rows)
@@ -283,7 +294,7 @@
         in_specs=[SMEM] + [VMEM] * 7,
         out_specs=VMEM,
         scratch_shapes=[pltpu.VMEM((cores * rows, tensors * features), bf16)],
-        compiler_params=pltpu.CompilerParams(vmem_limit_bytes=24 * MIB),
+        compiler_params=pltpu.CompilerParams(vmem_limit_bytes=18 * MIB),
         cost_estimate=pl.CostEstimate(
             flops=2 * rows * tensors * features * 6 * HEAD_DIM,
             bytes_accessed=8 * 1024 * 1024,
@@ -308,14 +319,13 @@
         concat_axis=0,
         tiled=True,
     )
-    own_out = weight[:, 3 * HEAD_DIM :]
     own_out, _ = lax.optimization_barrier((own_out, attended))
-    other_out = partner(own_out, "c", 1)
     core = lax.axis_index("c")
     near_rows = lax.dynamic_index_in_dim(packed, core, axis=0, keepdims=False)
     far_rows = lax.dynamic_slice(
         own_swap, (lax.axis_index("x"), core, 0, 0), (1, 1, rows, part)
     ).reshape(rows, part)
+    other_out = partner(own_out, "c", 1)
     return pl.pallas_call(
         functools.partial(
             output_kernel, query_len=query_len, pairs=pairs, passage_rows=passage_rows

time: 177 us -> 173 us (0.977)
  the two profiles are of different devices: /device:TPU:9 before, /device:TPU:1 now
where the time goes in v7:
time: 173 us; the launch traced here: 170 us
  starting transfers between devices  78.3 us (45%)
  waiting for transfers between devices  53.6 us (31%)
  between operations  13.5 us (8%)
  local copies, waits for them, and re-layouts  10.2 us (6%)
  Pallas kernels  9.71 us (6%)
  other arithmetic  4.51 us (3%)
    ppermute x12, starting transfers between devices, partner(): return lax.ppermute(value, axis, [(i, i ^ bit) for i in range(SIZE[axis])])  62.4 us
    ppermute x12, waiting for transfers between devices, partner(): return lax.ppermute(value, axis, [(i, i ^ bit) for i in range(SIZE[axis])])  27 us
    all_gather x1, waiting for transfers between devices, on_device(): own_out = lax.all_gather(weight[:, 3 * HEAD_DIM:], 'z', axis=0, tiled=True)  14.5 us
    all_gather x1, waiting for transfers between devices, on_device(): library = lax.all_gather(held, 'z', axis=0, tiled=True)  12 us
    pallas_call x1, Pallas kernels, on_device(): pl.pallas_call(functools.partial(attention_kernel, query_len=query_len, p...  5.65 us
    all_to_all x1, starting transfers between devices, on_device(): lax.all_to_all(attended.reshape(-1, rows, HEAD_DIM), ('c',) + TENSOR, spl...  5.62 us
    all_to_all x1, starting transfers between devices, on_every(): return lax.all_to_all(spread, axis, split_axis=0, concat_axis=0, tiled=True)  4.6 us
    unnamed x14, local copies, waits for them, and re-layouts  4.55 us
  transfers between devices with their start and end apart: 19, of which 10 were waited for; matrix products, arithmetic and copies ran while one was open for 4% of the time, Pallas kernels for 5%

profile of v7, /device:TPU:1, one launch (start us, length us, event | category | flops | bytes accessed | tf_op | source)
XLA Modules:
  0.0 169.8 jit_solution(14556215826686470313)
XLA Ops:
  7.6 8.8 %collective-permute-start = (bf16[200,256]{1,0:T(8,128)(2,1)S(1)}, bf16[200,256]{1,0:T(8,128)(2,1)S(1)}, u32[]{:S(2)}, u32[]{:S(2)}) collective-permute-start(bf16[200,256]{1,0:T(8,128)(2,1)S(1)} %broadcast_select_fusion), channel_id=1, source_target_pairs={{0,8},{8,0},{1,9},{9,1},{2,10},{10,2},{3,11},{11,3},{4,12},{12,4},... | collective-permute-start | bytes 307208 | tf_op jit(solution)/shard_map/ppermute | solution.py:158
  23.1 2.3 %collective-permute-start.2 = (bf16[72,512]{1,0:T(8,128)(2,1)S(1)}, bf16[72,512]{1,0:T(8,128)(2,1)S(1)}, u32[]{:S(2)}, u32[]{:S(2)}) collective-permute-start(bf16[72,512]{1,0:T(8,128)(2,1)S(1)} %select_bitcast_fusion.2), channel_id=1, source_target_pairs={{0,8},{8,0},{1,9},{9,1},{2,10},{10,2},{3,11},{11,3},{4,12},{12,4},... | collective-permute-start | bytes 221192 | tf_op jit(solution)/shard_map/ppermute | solution.py:158
  26.4 1.9 %collective-permute-start.3 = (bf16[2,72,512]{2,1,0:T(8,128)(2,1)S(1)}, bf16[2,72,512]{2,1,0:T(8,128)(2,1)S(1)}, u32[]{:S(2)}, u32[]{:S(2)}) collective-permute-start(bf16[2,72,512]{2,1,0:T(8,128)(2,1)S(1)} %get-tuple-element.32), channel_id=1, source_target_pairs={{0,16},{16,0},{32,48},{48,32},{1,17},{17,1},{33,49},{49,33},{2,18}... | collective-permute-start | bytes 442376 | tf_op jit(solution)/shard_map/ppermute | solution.py:158
  28.3 1.9 %collective-permute-start.4 = (bf16[2,72,512]{2,1,0:T(8,128)(2,1)S(1)}, bf16[2,72,512]{2,1,0:T(8,128)(2,1)S(1)}, u32[]{:S(2)}, u32[]{:S(2)}) collective-permute-start(bf16[2,72,512]{2,1,0:T(8,128)(2,1)S(1)} %get-tuple-element.32), channel_id=1, source_target_pairs={{0,32},{16,48},{32,0},{48,16},{1,33},{17,49},{33,1},{49,17},{2,34}... | collective-permute-start | bytes 442376 | tf_op jit(solution)/shard_map/ppermute | solution.py:158
  30.2 5.4 %collective-permute-start.5 = (bf16[2,72,512]{2,1,0:T(8,128)(2,1)S(1)}, bf16[2,72,512]{2,1,0:T(8,128)(2,1)S(1)}, u32[]{:S(2)}, u32[]{:S(2)}) collective-permute-start(bf16[2,72,512]{2,1,0:T(8,128)(2,1)S(1)} %get-tuple-element.32), channel_id=1, source_target_pairs={{0,48},{16,32},{32,16},{48,0},{1,49},{17,33},{33,17},{49,1},{2,50}... | collective-permute-start | bytes 442376 | tf_op jit(solution)/shard_map/ppermute | solution.py:158
  35.7 7.5 %collective-permute-done.4 = bf16[2,72,512]{2,1,0:T(8,128)(2,1)S(1)} collective-permute-done((bf16[2,72,512]{2,1,0:T(8,128)(2,1)S(1)}, bf16[2,72,512]{2,1,0:T(8,128)(2,1)S(1)}, u32[]{:S(2)}, u32[]{:S(2)}) %collective-permute-start.4) | collective-permute-done | bytes 147488 | tf_op jit(solution)/shard_map/ppermute | solution.py:158
  45.7 12.0 %all-gather.4.cloned.1.call-done.library_ref = bf16[128,24,256]{2,1,0:T(8,128)(2,1)} async-done(((bf16[16,24,256]{2,1,0:T(8,128)(2,1)}), bf16[128,24,256]{2,1,0:T(8,128)(2,1)}) %all-gather.4.cloned.1.call-update) | async-done | bytes 1572880 | tf_op jit(solution)/shard_map/all_gather | solution.py:221
  59.7 3.1 %collective-permute-start.6 = (bf16[16,24,256]{2,1,0:T(8,128)(2,1)S(1)}, bf16[16,24,256]{2,1,0:T(8,128)(2,1)S(1)}, u32[]{:S(2)}, u32[]{:S(2)}) collective-permute-start(bf16[16,24,256]{2,1,0:T(8,128)(2,1)S(1)} %get-tuple-element.19), channel_id=1, source_target_pairs={{0,16},{16,0},{32,48},{48,32},{1,17},{17,1},{33,49},{49,33},{2,18}... | collective-permute-start | bytes 589832 | tf_op jit(solution)/shard_map/ppermute | solution.py:158
  62.9 4.1 %collective-permute-start.7 = (bf16[16,24,256]{2,1,0:T(8,128)(2,1)S(1)}, bf16[16,24,256]{2,1,0:T(8,128)(2,1)S(1)}, u32[]{:S(2)}, u32[]{:S(2)}) collective-permute-start(bf16[16,24,256]{2,1,0:T(8,128)(2,1)S(1)} %get-tuple-element.20), channel_id=1, source_target_pairs={{0,32},{16,48},{32,0},{48,16},{1,33},{17,49},{33,1},{49,17},{2,34}... | collective-permute-start | bytes 589832 | tf_op jit(solution)/shard_map/ppermute | solution.py:158
  67.0 2.0 %collective-permute-start.8 = (bf16[16,24,256]{2,1,0:T(8,128)(2,1)S(1)}, bf16[16,24,256]{2,1,0:T(8,128)(2,1)S(1)}, u32[]{:S(2)}, u32[]{:S(2)}) collective-permute-start(bf16[16,24,256]{2,1,0:T(8,128)(2,1)S(1)} %get-tuple-element.21), channel_id=1, source_target_pairs={{0,48},{16,32},{32,16},{48,0},{1,49},{17,33},{33,17},{49,1},{2,50}... | collective-permute-start | bytes 589832 | tf_op jit(solution)/shard_map/ppermute | solution.py:158
  69.8 2.6 %collective-permute-done.7.refs_2_ = bf16[16,24,256]{2,1,0:T(8,128)(2,1)S(1)} collective-permute-done((bf16[16,24,256]{2,1,0:T(8,128)(2,1)S(1)}, bf16[16,24,256]{2,1,0:T(8,128)(2,1)S(1)}, u32[]{:S(2)}, u32[]{:S(2)}) %collective-permute-start.7) | collective-permute-done | bytes 196640 | tf_op jit(solution)/shard_map/ppermute | solution.py:158
  72.4 4.7 %collective-permute-done.8.refs_3_ = bf16[16,24,256]{2,1,0:T(8,128)(2,1)S(1)} collective-permute-done((bf16[16,24,256]{2,1,0:T(8,128)(2,1)S(1)}, bf16[16,24,256]{2,1,0:T(8,128)(2,1)S(1)}, u32[]{:S(2)}, u32[]{:S(2)}) %collective-permute-start.8) | collective-permute-done | bytes 196640 | tf_op jit(solution)/shard_map/ppermute | solution.py:158
  78.8 4.6 %all-to-all-start = ((bf16[4,2,208,256]{3,2,1,0:T(8,128)(2,1)}), bf16[4,2,208,256]{3,2,1,0:T(8,128)(2,1)S(1)}, u32[]{:S(2)}, u32[]{:S(2)}) async-start(bf16[4,2,208,256]{3,2,1,0:T(8,128)(2,1)} %broadcast_in_dim.23), calls=%async_computation | async-start | bytes 1703936 | tf_op jit(solution)/shard_map/all_to_all | solution.py:187
  83.4 4.5 %collective-permute-start.9 = (bf16[2,208,256]{2,1,0:T(8,128)(2,1)S(1)}, bf16[2,208,256]{2,1,0:T(8,128)(2,1)S(1)}, u32[]{:S(2)}, u32[]{:S(2)}) collective-permute-start(bf16[2,208,256]{2,1,0:T(8,128)(2,1)S(1)} %pack.1), channel_id=1, source_target_pairs={{0,4},{4,0},{1,5},{5,1},{2,6},{6,2},{3,7},{7,3},{8,12},{12,8},{9,1... | collective-permute-start | bytes 638984 | tf_op jit(solution)/shard_map/ppermute | solution.py:158
  87.9 6.0 %collective-permute-done.9.packed_ref = bf16[2,208,256]{2,1,0:T(8,128)(2,1)S(1)} collective-permute-done((bf16[2,208,256]{2,1,0:T(8,128)(2,1)S(1)}, bf16[2,208,256]{2,1,0:T(8,128)(2,1)S(1)}, u32[]{:S(2)}, u32[]{:S(2)}) %collective-permute-start.9) | collective-permute-done | bytes 213024 | tf_op jit(solution)/shard_map/ppermute | solution.py:158
  94.9 4.2 %all-to-all-start.1 = ((bf16[4,2,208,256]{3,2,1,0:T(8,128)(2,1)}), bf16[4,2,208,256]{3,2,1,0:T(8,128)(2,1)S(1)}, u32[]{:S(2)}, u32[]{:S(2)}) async-start(bf16[4,2,208,256]{3,2,1,0:T(8,128)(2,1)} %spread.1), calls=%async_computation.1 | async-start | bytes 1703936 | tf_op jit(solution)/shard_map/all_to_all | solution.py:280
  99.8 11.9 %collective-permute-start.10 = (bf16[4,2,208,256]{3,2,1,0:T(8,128)(2,1)S(1)}, bf16[4,2,208,256]{3,2,1,0:T(8,128)(2,1)S(1)}, u32[]{:S(2)}, u32[]{:S(2)}) collective-permute-start(bf16[4,2,208,256]{3,2,1,0:T(8,128)(2,1)S(1)} %all-to-all-done.own_ref), channel_id=1, source_target_pairs={{0,8},{8,0},{1,9},{9,1},{2,10},{10,2},{3,11},{11,3},{4,12},{12,4},... | collective-permute-start | bytes 2555912 | tf_op jit(solution)/shard_map/ppermute | solution.py:158
  111.8 9.1 %collective-permute-start.11 = (bf16[4,2,208,256]{3,2,1,0:T(8,128)(2,1)S(1)}, bf16[4,2,208,256]{3,2,1,0:T(8,128)(2,1)S(1)}, u32[]{:S(2)}, u32[]{:S(2)}) collective-permute-start(bf16[4,2,208,256]{3,2,1,0:T(8,128)(2,1)S(1)} %all-to-all-done.1.far_ref), channel_id=1, source_target_pairs={{0,8},{8,0},{1,9},{9,1},{2,10},{10,2},{3,11},{11,3},{4,12},{12,4},... | collective-permute-start | bytes 2555912 | tf_op jit(solution)/shard_map/ppermute | solution.py:158
  120.8 2.0 %collective-permute-done.11.far_swap_ref = bf16[4,2,208,256]{3,2,1,0:T(8,128)(2,1)S(1)} collective-permute-done((bf16[4,2,208,256]{3,2,1,0:T(8,128)(2,1)S(1)}, bf16[4,2,208,256]{3,2,1,0:T(8,128)(2,1)S(1)}, u32[]{:S(2)}, u32[]{:S(2)}) %collective-permute-start.11) | collective-permute-done | bytes 852000 | tf_op jit(solution)/shard_map/ppermute | solution.py:158
  124.7 5.7 %attention.1 = bf16[2,8,208,128]{3,2,1,0:T(8,128)(2,1)} custom-call(s32[16]{0:T(128)S(1)} %gather_fusion.1, bf16[4,2,208,256]{3,2,1,0:T(8,128)(2,1)S(1)} %all-to-all-done.own_ref, bf16[4,2,208,256]{3,2,1,0:T(8,128)(2,1)S(1)} %all-to-all-done.1.far_ref, bf16[4,2,208,256]{3,2,1,0:T(8,128)(2,1)S(1)} %collective-permute-done.10.own_swap_ref, ...), custom_call_target="tpu_custom_call" | custom-call | flops 1308622848 | bytes 8388608 | tf_op jit(solution)/shard_map/attention/pallas_call | solution.py:291
  130.4 5.6 %all-to-all-start.2 = ((bf16[16,208,128]{2,1,0:T(8,128)(2,1)}), bf16[16,208,128]{2,1,0:T(8,128)(2,1)S(1)}, u32[]{:S(2)}, u32[]{:S(2)}) async-start(bf16[16,208,128]{2,1,0:T(8,128)(2,1)} %bitcast.19), calls=%async_computation.2 | async-start | bytes 1703936 | tf_op jit(solution)/shard_map/all_to_all | solution.py:315
  136.0 14.5 %all-gather.8.cloned.1.call-done.own_ref = bf16[4096,128]{1,0:T(8,128)(2,1)} async-done(((bf16[512,128]{1,0:T(8,128)(2,1)}), bf16[4096,128]{1,0:T(8,128)(2,1)}) %all-gather.8.cloned.1.call-update) | async-done | bytes 1048592 | tf_op jit(solution)/shard_map/all_gather | solution.py:237
  150.4 7.3 %collective-permute-start.12 = (bf16[4096,128]{1,0:T(8,128)(2,1)}, bf16[4096,128]{1,0:T(8,128)(2,1)S(1)}, u32[]{:S(2)}, u32[]{:S(2)}) collective-permute-start(bf16[4096,128]{1,0:T(8,128)(2,1)} %all-gather.8.cloned.1.call-done.own_ref), channel_id=1, source_target_pairs={{0,8},{8,0},{1,9},{9,1},{2,10},{10,2},{3,11},{11,3},{4,12},{12,4},... | collective-permute-start | bytes 3145736 | tf_op jit(solution)/shard_map/ppermute | solution.py:158
  157.8 2.4 %collective-permute-done.12.other_ref = bf16[4096,128]{1,0:T(8,128)(2,1)S(1)} collective-permute-done((bf16[4096,128]{1,0:T(8,128)(2,1)}, bf16[4096,128]{1,0:T(8,128)(2,1)S(1)}, u32[]{:S(2)}, u32[]{:S(2)}) %collective-permute-start.12) | collective-permute-done | bytes 1048608 | tf_op jit(solution)/shard_map/ppermute | solution.py:158
  (76 shorter events, 22.2 us)
Async XLA Ops:
  6.5 62.6 %copy-start = (s32[512]{0:T(512)S(1)}, s32[512]{0:T(512)}, u32[]{:S(2)}) copy-start(s32[512]{0:T(512)} %param.12) | copy-start | bytes 6148
  6.5 51.2 %all-gather.4.cloned.1.call-start = ((), (), s32[]{:S(2)}) async-start(), calls=%async_computation.3 | async-start | bytes 1769472 | tf_op jit(solution)/shard_map/all_gather | solution.py:221
  7.6 9.7 %collective-permute-start = (bf16[200,256]{1,0:T(8,128)(2,1)S(1)}, bf16[200,256]{1,0:T(8,128)(2,1)S(1)}, u32[]{:S(2)}, u32[]{:S(2)}) collective-permute-start(bf16[200,256]{1,0:T(8,128)(2,1)S(1)} %broadcast_select_fusion), channel_id=1, source_target_pairs={{0,8},{8,0},{1,9},{9,1},{2,10},{10,2},{3,11},{11,3},{4,12},{12,4},... | collective-permute-start | bytes 307208 | tf_op jit(solution)/shard_map/ppermute | solution.py:158
  19.1 92.6 %all-gather.6.cloned.1.call-start = ((), (), s32[]{:S(2)}) async-start(), calls=%async_computation.4 | async-start | bytes 3538944 | tf_op jit(solution)/shard_map/all_gather | solution.py:238
  20.5 2.6 %collective-permute-start.1 = (bf16[64,256]{1,0:T(8,128)(2,1)}, bf16[64,256]{1,0:T(8,128)(2,1)S(1)}, u32[]{:S(2)}, u32[]{:S(2)}) collective-permute-start(bf16[64,256]{1,0:T(8,128)(2,1)} %bitcast.60), channel_id=1, source_target_pairs={{0,0},{1,64},{2,128},{3,192},{4,256},{5,320},{6,384},{7,448},{8,8}... | collective-permute-start | bytes 98312 | tf_op jit(solution)/shard_map/ppermute | solution.py:226
  23.0 21.8 %copy-start.6 = (bf16[512]{0:T(512)(128)(2,1)S(1)}, bf16[512]{0:T(512)(128)(2,1)}, u32[]{:S(2)}) copy-start(bf16[512]{0:T(512)(128)(2,1)} %param.15) | copy-start | bytes 3076
  23.1 3.2 %collective-permute-start.2 = (bf16[72,512]{1,0:T(8,128)(2,1)S(1)}, bf16[72,512]{1,0:T(8,128)(2,1)S(1)}, u32[]{:S(2)}, u32[]{:S(2)}) collective-permute-start(bf16[72,512]{1,0:T(8,128)(2,1)S(1)} %select_bitcast_fusion.2), channel_id=1, source_target_pairs={{0,8},{8,0},{1,9},{9,1},{2,10},{10,2},{3,11},{11,3},{4,12},{12,4},... | collective-permute-start | bytes 221192 | tf_op jit(solution)/shard_map/ppermute | solution.py:158
  26.4 9.3 %collective-permute-start.3 = (bf16[2,72,512]{2,1,0:T(8,128)(2,1)S(1)}, bf16[2,72,512]{2,1,0:T(8,128)(2,1)S(1)}, u32[]{:S(2)}, u32[]{:S(2)}) collective-permute-start(bf16[2,72,512]{2,1,0:T(8,128)(2,1)S(1)} %get-tuple-element.32), channel_id=1, source_target_pairs={{0,16},{16,0},{32,48},{48,32},{1,17},{17,1},{33,49},{49,33},{2,18}... | collective-permute-start | bytes 442376 | tf_op jit(solution)/shard_map/ppermute | solution.py:158
  28.3 14.9 %collective-permute-start.4 = (bf16[2,72,512]{2,1,0:T(8,128)(2,1)S(1)}, bf16[2,72,512]{2,1,0:T(8,128)(2,1)S(1)}, u32[]{:S(2)}, u32[]{:S(2)}) collective-permute-start(bf16[2,72,512]{2,1,0:T(8,128)(2,1)S(1)} %get-tuple-element.32), channel_id=1, source_target_pairs={{0,32},{16,48},{32,0},{48,16},{1,33},{17,49},{33,1},{49,17},{2,34}... | collective-permute-start | bytes 442376 | tf_op jit(solution)/shard_map/ppermute | solution.py:158
  30.2 13.0 %collective-permute-start.5 = (bf16[2,72,512]{2,1,0:T(8,128)(2,1)S(1)}, bf16[2,72,512]{2,1,0:T(8,128)(2,1)S(1)}, u32[]{:S(2)}, u32[]{:S(2)}) collective-permute-start(bf16[2,72,512]{2,1,0:T(8,128)(2,1)S(1)} %get-tuple-element.32), channel_id=1, source_target_pairs={{0,48},{16,32},{32,16},{48,0},{1,49},{17,33},{33,17},{49,1},{2,50}... | collective-permute-start | bytes 442376 | tf_op jit(solution)/shard_map/ppermute | solution.py:158
  59.7 10.1 %collective-permute-start.6 = (bf16[16,24,256]{2,1,0:T(8,128)(2,1)S(1)}, bf16[16,24,256]{2,1,0:T(8,128)(2,1)S(1)}, u32[]{:S(2)}, u32[]{:S(2)}) collective-permute-start(bf16[16,24,256]{2,1,0:T(8,128)(2,1)S(1)} %get-tuple-element.19), channel_id=1, source_target_pairs={{0,16},{16,0},{32,48},{48,32},{1,17},{17,1},{33,49},{49,33},{2,18}... | collective-permute-start | bytes 589832 | tf_op jit(solution)/shard_map/ppermute | solution.py:158
  62.9 9.5 %collective-permute-start.7 = (bf16[16,24,256]{2,1,0:T(8,128)(2,1)S(1)}, bf16[16,24,256]{2,1,0:T(8,128)(2,1)S(1)}, u32[]{:S(2)}, u32[]{:S(2)}) collective-permute-start(bf16[16,24,256]{2,1,0:T(8,128)(2,1)S(1)} %get-tuple-element.20), channel_id=1, source_target_pairs={{0,32},{16,48},{32,0},{48,16},{1,33},{17,49},{33,1},{49,17},{2,34}... | collective-permute-start | bytes 589832 | tf_op jit(solution)/shard_map/ppermute | solution.py:158
  67.0 10.1 %collective-permute-start.8 = (bf16[16,24,256]{2,1,0:T(8,128)(2,1)S(1)}, bf16[16,24,256]{2,1,0:T(8,128)(2,1)S(1)}, u32[]{:S(2)}, u32[]{:S(2)}) collective-permute-start(bf16[16,24,256]{2,1,0:T(8,128)(2,1)S(1)} %get-tuple-element.21), channel_id=1, source_target_pairs={{0,48},{16,32},{32,16},{48,0},{1,49},{17,33},{33,17},{49,1},{2,50}... | collective-permute-start | bytes 589832 | tf_op jit(solution)/shard_map/ppermute | solution.py:158
  77.8 45.0 %copy-start.4 = (f32[208,128]{1,0:T(8,128)S(1)}, f32[208,128]{1,0:T(8,128)}, u32[]{:S(2)}) copy-start(f32[208,128]{1,0:T(8,128)} %constant.80.clone.cos_ref) | copy-start | bytes 319492
  77.8 45.0 %copy-start.5 = (f32[208,128]{1,0:T(8,128)S(1)}, f32[208,128]{1,0:T(8,128)}, u32[]{:S(2)}) copy-start(f32[208,128]{1,0:T(8,128)} %constant.81.clone.sin_ref) | copy-start | bytes 319492
  78.8 16.1 %all-to-all-start = ((bf16[4,2,208,256]{3,2,1,0:T(8,128)(2,1)}), bf16[4,2,208,256]{3,2,1,0:T(8,128)(2,1)S(1)}, u32[]{:S(2)}, u32[]{:S(2)}) async-start(bf16[4,2,208,256]{3,2,1,0:T(8,128)(2,1)} %broadcast_in_dim.23), calls=%async_computation | async-start | bytes 1703936 | tf_op jit(solution)/shard_map/all_to_all | solution.py:187
  83.4 10.5 %collective-permute-start.9 = (bf16[2,208,256]{2,1,0:T(8,128)(2,1)S(1)}, bf16[2,208,256]{2,1,0:T(8,128)(2,1)S(1)}, u32[]{:S(2)}, u32[]{:S(2)}) collective-permute-start(bf16[2,208,256]{2,1,0:T(8,128)(2,1)S(1)} %pack.1), channel_id=1, source_target_pairs={{0,4},{4,0},{1,5},{5,1},{2,6},{6,2},{3,7},{7,3},{8,12},{12,8},{9,1... | collective-permute-start | bytes 638984 | tf_op jit(solution)/shard_map/ppermute | solution.py:158
  94.9 16.9 %all-to-all-start.1 = ((bf16[4,2,208,256]{3,2,1,0:T(8,128)(2,1)}), bf16[4,2,208,256]{3,2,1,0:T(8,128)(2,1)S(1)}, u32[]{:S(2)}, u32[]{:S(2)}) async-start(bf16[4,2,208,256]{3,2,1,0:T(8,128)(2,1)} %spread.1), calls=%async_computation.1 | async-start | bytes 1703936 | tf_op jit(solution)/shard_map/all_to_all | solution.py:280
  99.1 51.3 %all-gather.8.cloned.1.call-start = ((), (), s32[]{:S(2)}) async-start(), calls=%async_computation.5 | async-start | bytes 1179648 | tf_op jit(solution)/shard_map/all_gather | solution.py:237
  99.8 21.0 %collective-permute-start.10 = (bf16[4,2,208,256]{3,2,1,0:T(8,128)(2,1)S(1)}, bf16[4,2,208,256]{3,2,1,0:T(8,128)(2,1)S(1)}, u32[]{:S(2)}, u32[]{:S(2)}) collective-permute-start(bf16[4,2,208,256]{3,2,1,0:T(8,128)(2,1)S(1)} %all-to-all-done.own_ref), channel_id=1, source_target_pairs={{0,8},{8,0},{1,9},{9,1},{2,10},{10,2},{3,11},{11,3},{4,12},{12,4},... | collective-permute-start | bytes 2555912 | tf_op jit(solution)/shard_map/ppermute | solution.py:158
  111.8 11.1 %collective-permute-start.11 = (bf16[4,2,208,256]{3,2,1,0:T(8,128)(2,1)S(1)}, bf16[4,2,208,256]{3,2,1,0:T(8,128)(2,1)S(1)}, u32[]{:S(2)}, u32[]{:S(2)}) collective-permute-start(bf16[4,2,208,256]{3,2,1,0:T(8,128)(2,1)S(1)} %all-to-all-done.1.far_ref), channel_id=1, source_target_pairs={{0,8},{8,0},{1,9},{9,1},{2,10},{10,2},{3,11},{11,3},{4,12},{12,4},... | collective-permute-start | bytes 2555912 | tf_op jit(solution)/shard_map/ppermute | solution.py:158
  122.8 1.9 %copy-start.1 = (bf16[4096,384]{1,0:T(8,128)(2,1)S(1)}, bf16[4096,384]{1,0:T(8,128)(2,1)}, u32[]{:S(2)}) copy-start(bf16[4096,384]{1,0:T(8,128)(2,1)} %all-gather.6.cloned.1.call-done.weight_ref) | copy-start | bytes 9437188
  130.4 29.9 %all-to-all-start.2 = ((bf16[16,208,128]{2,1,0:T(8,128)(2,1)}), bf16[16,208,128]{2,1,0:T(8,128)(2,1)S(1)}, u32[]{:S(2)}, u32[]{:S(2)}) async-start(bf16[16,208,128]{2,1,0:T(8,128)(2,1)} %bitcast.19), calls=%async_computation.2 | async-start | bytes 1703936 | tf_op jit(solution)/shard_map/all_to_all | solution.py:315
  150.4 9.8 %collective-permute-start.12 = (bf16[4096,128]{1,0:T(8,128)(2,1)}, bf16[4096,128]{1,0:T(8,128)(2,1)S(1)}, u32[]{:S(2)}, u32[]{:S(2)}) collective-permute-start(bf16[4096,128]{1,0:T(8,128)(2,1)} %all-gather.8.cloned.1.call-done.own_ref), channel_id=1, source_target_pairs={{0,8},{8,0},{1,9},{9,1},{2,10},{10,2},{3,11},{11,3},{4,12},{12,4},... | collective-permute-start | bytes 3145736 | tf_op jit(solution)/shard_map/ppermute | solution.py:158
  (2 other events, 2.6 us)
Sparse Core Ops, SparseCore 0:
  19.2 38.4 all-gather.3
  59.8 50.5 all-gather.5
  112.5 37.9 all-gather.7

commit v8 on v7

--- a/solution.py
+++ b/solution.py
@@ -10,10 +10,11 @@
 
 HEAD_DIM = 128
 ROW_TILE = 16
-SPLIT = (("z", 8), ("y", 4), ("c", 2), ("h", 2), ("x", 4))
+SPLIT = (("zr", 4), ("zb", 2), ("y", 4), ("c", 2), ("h", 2), ("x", 4))
 SIZE = dict(SPLIT)
 AXES = tuple(name for name, _ in SPLIT)
-CORPUS = ("z", "y", "c")
+Z = ("zr", "zb")
+CORPUS = Z + ("y", "c")
 TENSOR = ("h", "x")
 VMEM = pl.BlockSpec(memory_space=pltpu.VMEM)
 SMEM = pl.BlockSpec(memory_space=pltpu.SMEM)
@@ -158,8 +159,8 @@
     return lax.ppermute(value, axis, [(i, i ^ bit) for i in range(SIZE[axis])])
 
 
-def by_core(mine, got):
-    first = lax.axis_index("c") == 0
+def in_order(mine, got, axis):
+    first = lax.axis_index(axis) == 0
     return jnp.stack([jnp.where(first, mine, got), jnp.where(first, got, mine)])
 
 
@@ -173,7 +174,7 @@
     first = lax.axis_index("c") == 0
     keep = jnp.where(first, blocks[0], blocks[1])
     got = partner(jnp.where(first, blocks[1], blocks[0]), "c", 1)
-    pair = by_core(keep, got)
+    pair = in_order(keep, got, "c")
     four = jnp.stack([pair] + [partner(pair, "y", k) for k in range(1, SIZE["y"])])
     return jnp.take(four, other_y(), axis=0, mode="clip")
 
@@ -212,15 +213,15 @@
 
     raw = jnp.concatenate([corpus_rows.reshape(-1, features), query_rows[0]], axis=0)
     keep, give = halves(raw, part)
-    shared = by_core(keep, partner(give, "c", 1))
+    shared = in_order(keep, partner(give, "c", 1), "c")
     held = shared[:, : stored * passage_rows].reshape(2 * stored, passage_rows, part)
     queries = shared[:, stored * passage_rows :]
     output_weight, project_weight, held = lax.optimization_barrier(
         (output_weight, project_weight, held)
     )
-    library = lax.all_gather(held, "z", axis=0, tiled=True)
-
-    cells = [(z, q, t) for z in range(SIZE["z"]) for q in range(plane) for t in range(tensors)]
+    library = lax.all_gather(held, Z, axis=0, tiled=True)
+
+    cells = [(z, q, t) for z in range(tensors) for q in range(plane) for t in range(tensors)]
     number = {cell: i for i, cell in enumerate(cells)}
     turn = [(number[(z, q, t)], number[(t, q, z)]) for z, q, t in cells]
     narrow = lax.ppermute(output_weight.T, AXES, turn)
@@ -234,8 +235,11 @@
     weight = gather_plane(weight)
     asked = weight[:, :, depth, : 2 * pairs].astype(i32)
     weight = weight[:, :, :depth].reshape(plane * depth, 4 * HEAD_DIM)
-    own_out = lax.all_gather(weight[:, 3 * HEAD_DIM :], "z", axis=0, tiled=True)
-    weight = lax.all_gather(weight[:, : 3 * HEAD_DIM], "z", axis=0, tiled=True)
+    narrow = weight[:, 3 * HEAD_DIM :]
+    narrow = in_order(narrow, partner(narrow, "zb", 1), "zb").reshape(-1, HEAD_DIM)
+    narrow, asked = lax.optimization_barrier((narrow, asked))
+    own_out = lax.all_gather(narrow, "zr", axis=0, tiled=True)
+    weight = lax.all_gather(weight[:, : 3 * HEAD_DIM], Z, axis=0, tiled=True)
 
     owner, place = asked[:, :, :pairs], asked[:, :, pairs:]
     owner_z, owner_y, owner_c = owner // plane, owner // cores % lines, owner % cores
@@ -267,7 +271,8 @@
     )(source.reshape(-1), counts, *arrived, queries, gain)
 
     far = partner(packed, "h", 1)
-    own_full = on_every(packed, "x")
+    own_full = lax.all_gather(packed, "x", axis=0)
+    far, own_full = lax.optimization_barrier((far, own_full))
     far = pl.pallas_call(
         spread_kernel,
         out_shape=jax.ShapeDtypeStruct((SIZE["x"],) + packed.shape, bf16),

time: 173 us -> 178 us (1.029)
  blocking collectives: 0 us -> 13 us
  waiting for transfers between devices: 53.6 us -> 48.9 us
  starting transfers between devices: 78.3 us -> 76.1 us
    all_gather x0 -> x1, blocking collectives: none -> 13 us  [on_device(): own_full = lax.all_gather(packed, 'x', axis=0)]
    all_to_all x1 -> x0, starting transfers between devices: 4.6 us -> none  [on_every(): return lax.all_to_all(spread, axis, split_axis=0, concat_axis=0, tiled=True)]
    all_gather x3, waiting for transfers between devices: 26.5 us -> 21.9 us  [the longest x1 18.2 us: on_device(): own_out = lax.all_gather(narrow, 'zr', axis=0, tiled=True)]
    ppermute x12 -> x13, starting transfers between devices: 62.4 us -> 66.2 us  [partner(): return lax.ppermute(value, axis, [(i, i ^ bit) for i in range(SIZE[axis])])]
    ppermute x12 -> x13, waiting for transfers between devices: 27 us -> 24.6 us  [partner(): return lax.ppermute(value, axis, [(i, i ^ bit) for i in range(SIZE[axis])])]
    another operation x6 -> x8, other arithmetic: 3.14 us -> 3.88 us  [the longest x6 2.56 us: in_order(): return jnp.stack([jnp.where(first, mine, got), jnp.where(first, got, mine)])]
  transfers between devices with their start and end apart: 19 -> 19, of which waited for: 10 -> 11; matrix products, arithmetic and copies ran while one was open for 4% -> 4% of each run, Pallas kernels for 5% -> 5%
where the time goes in v8:
time: 178 us; the launch traced here: 175 us
  starting transfers between devices  76.1 us (43%)
  waiting for transfers between devices  48.9 us (27%)
  between operations  13.5 us (8%)
  blocking collectives  13 us (7%)
  Pallas kernels  9.71 us (5%)
  local copies, waits for them, and re-layouts  8.61 us (5%)
  other arithmetic  5.25 us (3%)
    ppermute x13, starting transfers between devices, partner(): return lax.ppermute(value, axis, [(i, i ^ bit) for i in range(SIZE[axis])])  66.2 us
    ppermute x13, waiting for transfers between devices, partner(): return lax.ppermute(value, axis, [(i, i ^ bit) for i in range(SIZE[axis])])  24.6 us
    all_gather x1, waiting for transfers between devices, on_device(): own_out = lax.all_gather(narrow, 'zr', axis=0, tiled=True)  18.2 us
    all_gather x1, blocking collectives, on_device(): own_full = lax.all_gather(packed, 'x', axis=0)  13 us
    pallas_call x1, Pallas kernels, on_device(): pl.pallas_call(functools.partial(attention_kernel, query_len=query_len, p...  5.65 us
    all_to_all x1, starting transfers between devices, on_device(): far_full = lax.all_to_all(far, 'x', split_axis=0, concat_axis=0, tiled=True)  4.57 us
    unnamed x14, local copies, waits for them, and re-layouts  4.55 us
    all_to_all x1, starting transfers between devices, on_device(): lax.all_to_all(attended.reshape(-1, rows, HEAD_DIM), ('c',) + TENSOR, spl...  3.84 us
  transfers between devices with their start and end apart: 19, of which 11 were waited for; matrix products, arithmetic and copies ran while one was open for 4% of the time, Pallas kernels for 5%

profile of v8, /device:TPU:1, one launch (start us, length us, event | category | flops | bytes accessed | tf_op | source)
XLA Modules:
  0.0 175.0 jit_solution(12397543239094127022)
XLA Ops:
  7.6 8.8 %collective-permute-start = (bf16[200,256]{1,0:T(8,128)(2,1)S(1)}, bf16[200,256]{1,0:T(8,128)(2,1)S(1)}, u32[]{:S(2)}, u32[]{:S(2)}) collective-permute-start(bf16[200,256]{1,0:T(8,128)(2,1)S(1)} %broadcast_select_fusion), channel_id=1, source_target_pairs={{0,8},{8,0},{1,9},{9,1},{2,10},{10,2},{3,11},{11,3},{4,12},{12,4},... | collective-permute-start | bytes 307208 | tf_op jit(solution)/shard_map/ppermute | solution.py:159
  23.1 2.3 %collective-permute-start.2 = (bf16[72,512]{1,0:T(8,128)(2,1)S(1)}, bf16[72,512]{1,0:T(8,128)(2,1)S(1)}, u32[]{:S(2)}, u32[]{:S(2)}) collective-permute-start(bf16[72,512]{1,0:T(8,128)(2,1)S(1)} %select_bitcast_fusion.4), channel_id=1, source_target_pairs={{0,8},{8,0},{1,9},{9,1},{2,10},{10,2},{3,11},{11,3},{4,12},{12,4},... | collective-permute-start | bytes 221192 | tf_op jit(solution)/shard_map/ppermute | solution.py:159
  26.4 1.9 %collective-permute-start.3 = (bf16[2,72,512]{2,1,0:T(8,128)(2,1)S(1)}, bf16[2,72,512]{2,1,0:T(8,128)(2,1)S(1)}, u32[]{:S(2)}, u32[]{:S(2)}) collective-permute-start(bf16[2,72,512]{2,1,0:T(8,128)(2,1)S(1)} %get-tuple-element.42), channel_id=1, source_target_pairs={{0,16},{16,0},{32,48},{48,32},{1,17},{17,1},{33,49},{49,33},{2,18}... | collective-permute-start | bytes 442376 | tf_op jit(solution)/shard_map/ppermute | solution.py:159
  30.2 5.4 %collective-permute-start.5 = (bf16[2,72,512]{2,1,0:T(8,128)(2,1)S(1)}, bf16[2,72,512]{2,1,0:T(8,128)(2,1)S(1)}, u32[]{:S(2)}, u32[]{:S(2)}) collective-permute-start(bf16[2,72,512]{2,1,0:T(8,128)(2,1)S(1)} %get-tuple-element.42), channel_id=1, source_target_pairs={{0,48},{16,32},{32,16},{48,0},{1,49},{17,33},{33,17},{49,1},{2,50}... | collective-permute-start | bytes 442376 | tf_op jit(solution)/shard_map/ppermute | solution.py:159
  35.7 7.5 %collective-permute-done.4 = bf16[2,72,512]{2,1,0:T(8,128)(2,1)S(1)} collective-permute-done((bf16[2,72,512]{2,1,0:T(8,128)(2,1)S(1)}, bf16[2,72,512]{2,1,0:T(8,128)(2,1)S(1)}, u32[]{:S(2)}, u32[]{:S(2)}) %collective-permute-start.4) | collective-permute-done | bytes 147488 | tf_op jit(solution)/shard_map/ppermute | solution.py:159
  44.8 3.2 %collective-permute-start.6 = (bf16[512,128]{1,0:T(8,128)(2,1)S(1)}, bf16[512,128]{1,0:T(8,128)(2,1)S(1)}, u32[]{:S(2)}, u32[]{:S(2)}) collective-permute-start(bf16[512,128]{1,0:T(8,128)(2,1)S(1)} %slice.71), channel_id=1, source_target_pairs={{0,64},{64,0},{1,65},{65,1},{2,66},{66,2},{3,67},{67,3},{4,68},{68... | collective-permute-start | bytes 393224 | tf_op jit(solution)/shard_map/ppermute | solution.py:159
  48.0 4.3 %collective-permute-done.6 = bf16[512,128]{1,0:T(8,128)(2,1)S(1)} collective-permute-done((bf16[512,128]{1,0:T(8,128)(2,1)S(1)}, bf16[512,128]{1,0:T(8,128)(2,1)S(1)}, u32[]{:S(2)}, u32[]{:S(2)}) %collective-permute-start.6) | collective-permute-done | bytes 131104 | tf_op jit(solution)/shard_map/ppermute | solution.py:159
  53.9 3.8 %all-gather.5.cloned.1.call-done.library_ref = bf16[128,24,256]{2,1,0:T(8,128)(2,1)} async-done(((bf16[16,24,256]{2,1,0:T(8,128)(2,1)}), bf16[128,24,256]{2,1,0:T(8,128)(2,1)}) %all-gather.5.cloned.1.call-update) | async-done | bytes 1572880 | tf_op jit(solution)/shard_map/all_gather | solution.py:222
  59.7 4.4 %collective-permute-start.7 = (bf16[16,24,256]{2,1,0:T(8,128)(2,1)S(1)}, bf16[16,24,256]{2,1,0:T(8,128)(2,1)S(1)}, u32[]{:S(2)}, u32[]{:S(2)}) collective-permute-start(bf16[16,24,256]{2,1,0:T(8,128)(2,1)S(1)} %get-tuple-element.24), channel_id=1, source_target_pairs={{0,16},{16,0},{32,48},{48,32},{1,17},{17,1},{33,49},{49,33},{2,18}... | collective-permute-start | bytes 589832 | tf_op jit(solution)/shard_map/ppermute | solution.py:159
  64.2 3.2 %collective-permute-start.8 = (bf16[16,24,256]{2,1,0:T(8,128)(2,1)S(1)}, bf16[16,24,256]{2,1,0:T(8,128)(2,1)S(1)}, u32[]{:S(2)}, u32[]{:S(2)}) collective-permute-start(bf16[16,24,256]{2,1,0:T(8,128)(2,1)S(1)} %get-tuple-element.25), channel_id=1, source_target_pairs={{0,32},{16,48},{32,0},{48,16},{1,33},{17,49},{33,1},{49,17},{2,34}... | collective-permute-start | bytes 589832 | tf_op jit(solution)/shard_map/ppermute | solution.py:159
  67.4 3.1 %collective-permute-start.9 = (bf16[16,24,256]{2,1,0:T(8,128)(2,1)S(1)}, bf16[16,24,256]{2,1,0:T(8,128)(2,1)S(1)}, u32[]{:S(2)}, u32[]{:S(2)}) collective-permute-start(bf16[16,24,256]{2,1,0:T(8,128)(2,1)S(1)} %get-tuple-element.26), channel_id=1, source_target_pairs={{0,48},{16,32},{32,16},{48,0},{1,49},{17,33},{33,17},{49,1},{2,50}... | collective-permute-start | bytes 589832 | tf_op jit(solution)/shard_map/ppermute | solution.py:159
  71.3 2.3 %collective-permute-done.8.refs_2_ = bf16[16,24,256]{2,1,0:T(8,128)(2,1)S(1)} collective-permute-done((bf16[16,24,256]{2,1,0:T(8,128)(2,1)S(1)}, bf16[16,24,256]{2,1,0:T(8,128)(2,1)S(1)}, u32[]{:S(2)}, u32[]{:S(2)}) %collective-permute-start.8) | collective-permute-done | bytes 196640 | tf_op jit(solution)/shard_map/ppermute | solution.py:159
  73.6 4.3 %collective-permute-done.9.refs_3_ = bf16[16,24,256]{2,1,0:T(8,128)(2,1)S(1)} collective-permute-done((bf16[16,24,256]{2,1,0:T(8,128)(2,1)S(1)}, bf16[16,24,256]{2,1,0:T(8,128)(2,1)S(1)}, u32[]{:S(2)}, u32[]{:S(2)}) %collective-permute-start.9) | collective-permute-done | bytes 196640 | tf_op jit(solution)/shard_map/ppermute | solution.py:159
  78.6 13.2 %collective-permute-start.10 = (bf16[2,208,256]{2,1,0:T(8,128)(2,1)S(1)}, bf16[2,208,256]{2,1,0:T(8,128)(2,1)S(1)}, u32[]{:S(2)}, u32[]{:S(2)}) collective-permute-start(bf16[2,208,256]{2,1,0:T(8,128)(2,1)S(1)} %pack.1), channel_id=1, source_target_pairs={{0,4},{4,0},{1,5},{5,1},{2,6},{6,2},{3,7},{7,3},{8,12},{12,8},{9,1... | collective-permute-start | bytes 638984 | tf_op jit(solution)/shard_map/ppermute | solution.py:159
  91.8 13.0 %all-gather = bf16[8,208,256]{2,1,0:T(8,128)(2,1)S(1)} all-gather(bf16[2,208,256]{2,1,0:T(8,128)(2,1)S(1)} %pack.1), channel_id=2, replica_groups=mesh['zr'=4,'zb'=2,'y'=4,'c'=2,'h'=2,'x'=4] {'x'}, dimensions={0}, use_global_device_ids=true | all-gather | bytes 1064960 | tf_op jit(solution)/shard_map/all_gather | solution.py:274
  105.9 4.6 %all-to-all-start = ((bf16[4,2,208,256]{3,2,1,0:T(8,128)(2,1)}), bf16[4,2,208,256]{3,2,1,0:T(8,128)(2,1)S(1)}, u32[]{:S(2)}, u32[]{:S(2)}) async-start(bf16[4,2,208,256]{3,2,1,0:T(8,128)(2,1)} %spread.1), calls=%async_computation | async-start | bytes 1703936 | tf_op jit(solution)/shard_map/all_to_all | solution.py:285
  111.1 6.4 %collective-permute-start.11 = (bf16[4,2,208,256]{3,2,1,0:T(8,128)(2,1)S(1)}, bf16[4,2,208,256]{3,2,1,0:T(8,128)(2,1)S(1)}, u32[]{:S(2)}, u32[]{:S(2)}) collective-permute-start(bf16[4,2,208,256]{3,2,1,0:T(8,128)(2,1)S(1)} %bitcast.53), channel_id=1, source_target_pairs={{0,8},{8,0},{1,9},{9,1},{2,10},{10,2},{3,11},{11,3},{4,12},{12,4},... | collective-permute-start | bytes 2555912 | tf_op jit(solution)/shard_map/ppermute | solution.py:159
  119.1 7.5 %collective-permute-start.12 = (bf16[4,2,208,256]{3,2,1,0:T(8,128)(2,1)S(1)}, bf16[4,2,208,256]{3,2,1,0:T(8,128)(2,1)S(1)}, u32[]{:S(2)}, u32[]{:S(2)}) collective-permute-start(bf16[4,2,208,256]{3,2,1,0:T(8,128)(2,1)S(1)} %all-to-all-done.far_ref), channel_id=1, source_target_pairs={{0,8},{8,0},{1,9},{9,1},{2,10},{10,2},{3,11},{11,3},{4,12},{12,4},... | collective-permute-start | bytes 2555912 | tf_op jit(solution)/shard_map/ppermute | solution.py:159
  126.6 2.0 %collective-permute-done.12.far_swap_ref = bf16[4,2,208,256]{3,2,1,0:T(8,128)(2,1)S(1)} collective-permute-done((bf16[4,2,208,256]{3,2,1,0:T(8,128)(2,1)S(1)}, bf16[4,2,208,256]{3,2,1,0:T(8,128)(2,1)S(1)}, u32[]{:S(2)}, u32[]{:S(2)}) %collective-permute-start.12) | collective-permute-done | bytes 852000 | tf_op jit(solution)/shard_map/ppermute | solution.py:159
  130.5 5.7 %attention.1 = bf16[2,8,208,128]{3,2,1,0:T(8,128)(2,1)} custom-call(s32[16]{0:T(128)S(1)} %gather_fusion.1, bf16[4,2,208,256]{3,2,1,0:T(8,128)(2,1)S(1)} %bitcast.54, bf16[4,2,208,256]{3,2,1,0:T(8,128)(2,1)S(1)} %all-to-all-done.far_ref, bf16[4,2,208,256]{3,2,1,0:T(8,128)(2,1)S(1)} %collective-permute-done.11.own_swap_ref, ...), custom_call_target="tpu_custom_call" | custom-call | flops 1308622848 | bytes 8388608 | tf_op jit(solution)/shard_map/attention/pallas_call | solution.py:296
  136.2 3.8 %all-to-all-start.1 = ((bf16[16,208,128]{2,1,0:T(8,128)(2,1)}), bf16[16,208,128]{2,1,0:T(8,128)(2,1)S(1)}, u32[]{:S(2)}, u32[]{:S(2)}) async-start(bf16[16,208,128]{2,1,0:T(8,128)(2,1)} %bitcast.23), calls=%async_computation.1 | async-start | bytes 1703936 | tf_op jit(solution)/shard_map/all_to_all | solution.py:320
  140.0 18.2 %all-gather.9.cloned.1.call-done.own_ref = bf16[4096,128]{1,0:T(8,128)(2,1)} async-done(((bf16[1024,128]{1,0:T(8,128)(2,1)}), bf16[4096,128]{1,0:T(8,128)(2,1)}) %all-gather.9.cloned.1.call-update) | async-done | bytes 1048592 | tf_op jit(solution)/shard_map/all_gather | solution.py:241
  158.2 4.8 %collective-permute-start.13 = (bf16[4096,128]{1,0:T(8,128)(2,1)}, bf16[4096,128]{1,0:T(8,128)(2,1)S(1)}, u32[]{:S(2)}, u32[]{:S(2)}) collective-permute-start(bf16[4096,128]{1,0:T(8,128)(2,1)} %all-gather.9.cloned.1.call-done.own_ref), channel_id=1, source_target_pairs={{0,8},{8,0},{1,9},{9,1},{2,10},{10,2},{3,11},{11,3},{4,12},{12,4},... | collective-permute-start | bytes 3145736 | tf_op jit(solution)/shard_map/ppermute | solution.py:159
  163.1 2.4 %collective-permute-done.13.other_ref = bf16[4096,128]{1,0:T(8,128)(2,1)S(1)} collective-permute-done((bf16[4096,128]{1,0:T(8,128)(2,1)}, bf16[4096,128]{1,0:T(8,128)(2,1)S(1)}, u32[]{:S(2)}, u32[]{:S(2)}) %collective-permute-start.13) | collective-permute-done | bytes 1048608 | tf_op jit(solution)/shard_map/ppermute | solution.py:159
  (78 shorter events, 25.5 us)
Async XLA Ops:
  6.5 64.1 %copy-start = (s32[512]{0:T(512)S(1)}, s32[512]{0:T(512)}, u32[]{:S(2)}) copy-start(s32[512]{0:T(512)} %param.12) | copy-start | bytes 6148
  6.5 51.2 %all-gather.5.cloned.1.call-start = ((), (), s32[]{:S(2)}) async-start(), calls=%async_computation.2 | async-start | bytes 1769472 | tf_op jit(solution)/shard_map/all_gather | solution.py:222
  7.6 9.7 %collective-permute-start = (bf16[200,256]{1,0:T(8,128)(2,1)S(1)}, bf16[200,256]{1,0:T(8,128)(2,1)S(1)}, u32[]{:S(2)}, u32[]{:S(2)}) collective-permute-start(bf16[200,256]{1,0:T(8,128)(2,1)S(1)} %broadcast_select_fusion), channel_id=1, source_target_pairs={{0,8},{8,0},{1,9},{9,1},{2,10},{10,2},{3,11},{11,3},{4,12},{12,4},... | collective-permute-start | bytes 307208 | tf_op jit(solution)/shard_map/ppermute | solution.py:159
  19.1 100.0 %all-gather.7.cloned.1.call-start = ((), (), s32[]{:S(2)}) async-start(), calls=%async_computation.3 | async-start | bytes 3538944 | tf_op jit(solution)/shard_map/all_gather | solution.py:242
  20.5 2.6 %collective-permute-start.1 = (bf16[64,256]{1,0:T(8,128)(2,1)}, bf16[64,256]{1,0:T(8,128)(2,1)S(1)}, u32[]{:S(2)}, u32[]{:S(2)}) collective-permute-start(bf16[64,256]{1,0:T(8,128)(2,1)} %bitcast.70), channel_id=1, source_target_pairs={{0,0},{1,64},{2,128},{3,192},{4,256},{5,320},{6,384},{7,448},{8,8}... | collective-permute-start | bytes 98312 | tf_op jit(solution)/shard_map/ppermute | solution.py:227
  23.0 21.8 %copy-start.6 = (bf16[512]{0:T(512)(128)(2,1)S(1)}, bf16[512]{0:T(512)(128)(2,1)}, u32[]{:S(2)}) copy-start(bf16[512]{0:T(512)(128)(2,1)} %param.15) | copy-start | bytes 3076
  23.1 3.2 %collective-permute-start.2 = (bf16[72,512]{1,0:T(8,128)(2,1)S(1)}, bf16[72,512]{1,0:T(8,128)(2,1)S(1)}, u32[]{:S(2)}, u32[]{:S(2)}) collective-permute-start(bf16[72,512]{1,0:T(8,128)(2,1)S(1)} %select_bitcast_fusion.4), channel_id=1, source_target_pairs={{0,8},{8,0},{1,9},{9,1},{2,10},{10,2},{3,11},{11,3},{4,12},{12,4},... | collective-permute-start | bytes 221192 | tf_op jit(solution)/shard_map/ppermute | solution.py:159
  26.4 9.3 %collective-permute-start.3 = (bf16[2,72,512]{2,1,0:T(8,128)(2,1)S(1)}, bf16[2,72,512]{2,1,0:T(8,128)(2,1)S(1)}, u32[]{:S(2)}, u32[]{:S(2)}) collective-permute-start(bf16[2,72,512]{2,1,0:T(8,128)(2,1)S(1)} %get-tuple-element.42), channel_id=1, source_target_pairs={{0,16},{16,0},{32,48},{48,32},{1,17},{17,1},{33,49},{49,33},{2,18}... | collective-permute-start | bytes 442376 | tf_op jit(solution)/shard_map/ppermute | solution.py:159
  28.3 14.9 %collective-permute-start.4 = (bf16[2,72,512]{2,1,0:T(8,128)(2,1)S(1)}, bf16[2,72,512]{2,1,0:T(8,128)(2,1)S(1)}, u32[]{:S(2)}, u32[]{:S(2)}) collective-permute-start(bf16[2,72,512]{2,1,0:T(8,128)(2,1)S(1)} %get-tuple-element.42), channel_id=1, source_target_pairs={{0,32},{16,48},{32,0},{48,16},{1,33},{17,49},{33,1},{49,17},{2,34}... | collective-permute-start | bytes 442376 | tf_op jit(solution)/shard_map/ppermute | solution.py:159
  30.2 13.0 %collective-permute-start.5 = (bf16[2,72,512]{2,1,0:T(8,128)(2,1)S(1)}, bf16[2,72,512]{2,1,0:T(8,128)(2,1)S(1)}, u32[]{:S(2)}, u32[]{:S(2)}) collective-permute-start(bf16[2,72,512]{2,1,0:T(8,128)(2,1)S(1)} %get-tuple-element.42), channel_id=1, source_target_pairs={{0,48},{16,32},{32,16},{48,0},{1,49},{17,33},{33,17},{49,1},{2,50}... | collective-permute-start | bytes 442376 | tf_op jit(solution)/shard_map/ppermute | solution.py:159
  44.8 7.5 %collective-permute-start.6 = (bf16[512,128]{1,0:T(8,128)(2,1)S(1)}, bf16[512,128]{1,0:T(8,128)(2,1)S(1)}, u32[]{:S(2)}, u32[]{:S(2)}) collective-permute-start(bf16[512,128]{1,0:T(8,128)(2,1)S(1)} %slice.71), channel_id=1, source_target_pairs={{0,64},{64,0},{1,65},{65,1},{2,66},{66,2},{3,67},{67,3},{4,68},{68... | collective-permute-start | bytes 393224 | tf_op jit(solution)/shard_map/ppermute | solution.py:159
  59.7 68.9 %copy-start.4 = (f32[208,128]{1,0:T(8,128)S(1)}, f32[208,128]{1,0:T(8,128)}, u32[]{:S(2)}) copy-start(f32[208,128]{1,0:T(8,128)} %constant.84.clone.cos_ref) | copy-start | bytes 319492
  59.7 68.9 %copy-start.5 = (f32[208,128]{1,0:T(8,128)S(1)}, f32[208,128]{1,0:T(8,128)}, u32[]{:S(2)}) copy-start(f32[208,128]{1,0:T(8,128)} %constant.85.clone.sin_ref) | copy-start | bytes 319492
  59.7 11.6 %collective-permute-start.7 = (bf16[16,24,256]{2,1,0:T(8,128)(2,1)S(1)}, bf16[16,24,256]{2,1,0:T(8,128)(2,1)S(1)}, u32[]{:S(2)}, u32[]{:S(2)}) collective-permute-start(bf16[16,24,256]{2,1,0:T(8,128)(2,1)S(1)} %get-tuple-element.24), channel_id=1, source_target_pairs={{0,16},{16,0},{32,48},{48,32},{1,17},{17,1},{33,49},{49,33},{2,18}... | collective-permute-start | bytes 589832 | tf_op jit(solution)/shard_map/ppermute | solution.py:159
  64.2 9.4 %collective-permute-start.8 = (bf16[16,24,256]{2,1,0:T(8,128)(2,1)S(1)}, bf16[16,24,256]{2,1,0:T(8,128)(2,1)S(1)}, u32[]{:S(2)}, u32[]{:S(2)}) collective-permute-start(bf16[16,24,256]{2,1,0:T(8,128)(2,1)S(1)} %get-tuple-element.25), channel_id=1, source_target_pairs={{0,32},{16,48},{32,0},{48,16},{1,33},{17,49},{33,1},{49,17},{2,34}... | collective-permute-start | bytes 589832 | tf_op jit(solution)/shard_map/ppermute | solution.py:159
  67.4 10.5 %collective-permute-start.9 = (bf16[16,24,256]{2,1,0:T(8,128)(2,1)S(1)}, bf16[16,24,256]{2,1,0:T(8,128)(2,1)S(1)}, u32[]{:S(2)}, u32[]{:S(2)}) collective-permute-start(bf16[16,24,256]{2,1,0:T(8,128)(2,1)S(1)} %get-tuple-element.26), channel_id=1, source_target_pairs={{0,48},{16,32},{32,16},{48,0},{1,49},{17,33},{33,17},{49,1},{2,50}... | collective-permute-start | bytes 589832 | tf_op jit(solution)/shard_map/ppermute | solution.py:159
  78.6 26.2 %collective-permute-start.10 = (bf16[2,208,256]{2,1,0:T(8,128)(2,1)S(1)}, bf16[2,208,256]{2,1,0:T(8,128)(2,1)S(1)}, u32[]{:S(2)}, u32[]{:S(2)}) collective-permute-start(bf16[2,208,256]{2,1,0:T(8,128)(2,1)S(1)} %pack.1), channel_id=1, source_target_pairs={{0,4},{4,0},{1,5},{5,1},{2,6},{6,2},{3,7},{7,3},{8,12},{12,8},{9,1... | collective-permute-start | bytes 638984 | tf_op jit(solution)/shard_map/ppermute | solution.py:159
  105.9 13.3 %all-to-all-start = ((bf16[4,2,208,256]{3,2,1,0:T(8,128)(2,1)}), bf16[4,2,208,256]{3,2,1,0:T(8,128)(2,1)S(1)}, u32[]{:S(2)}, u32[]{:S(2)}) async-start(bf16[4,2,208,256]{3,2,1,0:T(8,128)(2,1)} %spread.1), calls=%async_computation | async-start | bytes 1703936 | tf_op jit(solution)/shard_map/all_to_all | solution.py:285
  110.4 47.7 %all-gather.9.cloned.1.call-start = ((), (), s32[]{:S(2)}) async-start(), calls=%async_computation.4 | async-start | bytes 1310720 | tf_op jit(solution)/shard_map/all_gather | solution.py:241
  111.1 15.5 %collective-permute-start.11 = (bf16[4,2,208,256]{3,2,1,0:T(8,128)(2,1)S(1)}, bf16[4,2,208,256]{3,2,1,0:T(8,128)(2,1)S(1)}, u32[]{:S(2)}, u32[]{:S(2)}) collective-permute-start(bf16[4,2,208,256]{3,2,1,0:T(8,128)(2,1)S(1)} %bitcast.53), channel_id=1, source_target_pairs={{0,8},{8,0},{1,9},{9,1},{2,10},{10,2},{3,11},{11,3},{4,12},{12,4},... | collective-permute-start | bytes 2555912 | tf_op jit(solution)/shard_map/ppermute | solution.py:159
  119.1 9.5 %collective-permute-start.12 = (bf16[4,2,208,256]{3,2,1,0:T(8,128)(2,1)S(1)}, bf16[4,2,208,256]{3,2,1,0:T(8,128)(2,1)S(1)}, u32[]{:S(2)}, u32[]{:S(2)}) collective-permute-start(bf16[4,2,208,256]{3,2,1,0:T(8,128)(2,1)S(1)} %all-to-all-done.far_ref), channel_id=1, source_target_pairs={{0,8},{8,0},{1,9},{9,1},{2,10},{10,2},{3,11},{11,3},{4,12},{12,4},... | collective-permute-start | bytes 2555912 | tf_op jit(solution)/shard_map/ppermute | solution.py:159
  128.6 1.9 %copy-start.1 = (bf16[4096,384]{1,0:T(8,128)(2,1)S(1)}, bf16[4096,384]{1,0:T(8,128)(2,1)}, u32[]{:S(2)}) copy-start(bf16[4096,384]{1,0:T(8,128)(2,1)} %all-gather.7.cloned.1.call-done.weight_ref) | copy-start | bytes 9437188
  136.2 29.3 %all-to-all-start.1 = ((bf16[16,208,128]{2,1,0:T(8,128)(2,1)}), bf16[16,208,128]{2,1,0:T(8,128)(2,1)S(1)}, u32[]{:S(2)}, u32[]{:S(2)}) async-start(bf16[16,208,128]{2,1,0:T(8,128)(2,1)} %bitcast.23), calls=%async_computation.1 | async-start | bytes 1703936 | tf_op jit(solution)/shard_map/all_to_all | solution.py:320
  158.2 7.3 %collective-permute-start.13 = (bf16[4096,128]{1,0:T(8,128)(2,1)}, bf16[4096,128]{1,0:T(8,128)(2,1)S(1)}, u32[]{:S(2)}, u32[]{:S(2)}) collective-permute-start(bf16[4096,128]{1,0:T(8,128)(2,1)} %all-gather.9.cloned.1.call-done.own_ref), channel_id=1, source_target_pairs={{0,8},{8,0},{1,9},{9,1},{2,10},{10,2},{3,11},{11,3},{4,12},{12,4},... | collective-permute-start | bytes 3145736 | tf_op jit(solution)/shard_map/ppermute | solution.py:159
  (2 other events, 2.6 us)
Sparse Core Ops, SparseCore 0:
  19.2 38.4 all-gather.4
  59.8 50.5 all-gather.6
  113.3 44.7 all-gather.8

commit v9 on v7

--- a/solution.py
+++ b/solution.py
@@ -55,7 +55,7 @@
 
 def attention_kernel(
     count_ref, own_ref, far_ref, own_swap_ref, far_swap_ref, weight_ref, cos_ref, sin_ref,
-    out_ref, normed_ref, *, query_len, passage_rows,
+    out_ref, own_out_ref, normed_ref, *, query_len, passage_rows,
 ):
     bf16, f32, i32 = jnp.bfloat16, jnp.float32, jnp.int32
     spread, groups, rows, part = own_ref.shape
@@ -87,8 +87,10 @@
                     chunk * inverse * gain
                 ).astype(bf16)
     projected = jnp.dot(
-        normed_ref[...], weight_ref[...], preferred_element_type=f32
-    )
+        normed_ref[...], weight_ref[:, : 3 * HEAD_DIM], preferred_element_type=f32
+    )
+
+    own_out_ref[...] = weight_ref[:, 3 * HEAD_DIM :]
 
     def rotate(inputs):
         return (
@@ -122,28 +124,37 @@
         exponent = jnp.exp(scores - jnp.max(scores, axis=-1, keepdims=True))
         weights = (exponent / jnp.sum(exponent, axis=-1, keepdims=True)).astype(bf16)
         attended = jnp.dot(weights, values, preferred_element_type=f32).astype(bf16)
-        for t in range(out_ref.shape[1]):
-            out_ref[group, t] = attended
+        out_ref[group] = attended
+
+
+def heads_kernel(own_ref, far_ref, spread_ref):
+    high = lax.axis_index("h")
+    groups = own_ref.shape[0]
+    spread = spread_ref.shape[0] // groups
+    for group in range(groups):
+        for x in range(spread):
+            spread_ref[group * spread + x, high] = own_ref[group]
+            spread_ref[group * spread + x, 1 - high] = far_ref[group]
 
 
 def output_kernel(heads_ref, own_ref, other_ref, near_ref, far_ref, out_ref, *, query_len, pairs, passage_rows):
     bf16, f32 = jnp.bfloat16, jnp.float32
     core = lax.axis_index("c")
     numbers = (((1,), (1,)), ((), ()))
-    tensors = heads_ref.shape[0] // 2
-    columns = own_ref.shape[0] // tensors
+    spread, highs = heads_ref.shape[0] // 2, heads_ref.shape[1]
+    columns = own_ref.shape[0] // (spread * highs)
     near, far = near_ref[...], far_ref[...]
     first = core == 0
     final = jnp.concatenate(
         [jnp.where(first, near, far), jnp.where(first, far, near)], axis=1
     ).astype(f32)
     summed = jnp.zeros(final.shape, f32)
-    for t in range(tensors):
-        block = slice(t * columns, (t + 1) * columns)
+    for t in range(spread * highs):
+        block, high, x = slice(t * columns, (t + 1) * columns), t // spread, t % spread
         partial_value = lax.dot_general(
-            heads_ref[core * tensors + t], own_ref[block], numbers, preferred_element_type=f32
+            heads_ref[core * spread + x, high], own_ref[block], numbers, preferred_element_type=f32
         ) + lax.dot_general(
-            heads_ref[(1 - core) * tensors + t], other_ref[block], numbers, preferred_element_type=f32
+            heads_ref[(1 - core) * spread + x, high], other_ref[block], numbers, preferred_element_type=f32
         )
         summed = summed + partial_value.astype(bf16).astype(f32)
     final = final + summed
@@ -234,8 +245,7 @@
     weight = gather_plane(weight)
     asked = weight[:, :, depth, : 2 * pairs].astype(i32)
     weight = weight[:, :, :depth].reshape(plane * depth, 4 * HEAD_DIM)
-    own_out = lax.all_gather(weight[:, 3 * HEAD_DIM :], "z", axis=0, tiled=True)
-    weight = lax.all_gather(weight[:, : 3 * HEAD_DIM], "z", axis=0, tiled=True)
+    weight = lax.all_gather(weight, "z", axis=0, tiled=True)
 
     owner, place = asked[:, :, :pairs], asked[:, :, pairs:]
     owner_z, owner_y, owner_c = owner // plane, owner // cores % lines, owner % cores
@@ -267,7 +277,8 @@
     )(source.reshape(-1), counts, *arrived, queries, gain)
 
     far = partner(packed, "h", 1)
-    own_full = on_every(packed, "x")
+    own_full = lax.all_gather(packed, "x", axis=0)
+    far, own_full = lax.optimization_barrier((far, own_full))
     far = pl.pallas_call(
         spread_kernel,
         out_shape=jax.ShapeDtypeStruct((SIZE["x"],) + packed.shape, bf16),
@@ -279,7 +290,6 @@
     )(far)
     far_full = lax.all_to_all(far, "x", split_axis=0, concat_axis=0, tiled=True)
     own_swap = partner(own_full, "c", 1)
-    far_full, weight = lax.optimization_barrier((far_full, weight))
     far_swap = partner(far_full, "c", 1)
 
     row = np.arange(rows)
@@ -288,11 +298,14 @@
     frequency = np.power(10000.0, -2.0 * np.arange(half) / HEAD_DIM).astype(np.float32)
     angles = slot.astype(np.float32)[:, None] * frequency[None, :]
     cosine, sine = np.cos(angles), np.sin(angles)
-    attended = pl.pallas_call(
+    attended, own_out = pl.pallas_call(
         functools.partial(attention_kernel, query_len=query_len, passage_rows=passage_rows),
-        out_shape=jax.ShapeDtypeStruct((cores, tensors, rows, HEAD_DIM), bf16),
+        out_shape=[
+            jax.ShapeDtypeStruct((cores, rows, HEAD_DIM), bf16),
+            jax.ShapeDtypeStruct((weight.shape[0], HEAD_DIM), bf16),
+        ],
         in_specs=[SMEM] + [VMEM] * 7,
-        out_specs=VMEM,
+        out_specs=[VMEM] * 2,
         scratch_shapes=[pltpu.VMEM((cores * rows, tensors * features), bf16)],
         compiler_params=pltpu.CompilerParams(vmem_limit_bytes=18 * MIB),
         cost_estimate=pl.CostEstimate(
@@ -312,14 +325,15 @@
         jnp.asarray(np.concatenate([-sine, sine], axis=1), f32),
     )
 
-    heads = lax.all_to_all(
-        attended.reshape(-1, rows, HEAD_DIM),
-        ("c",) + TENSOR,
-        split_axis=0,
-        concat_axis=0,
-        tiled=True,
-    )
-    own_out, _ = lax.optimization_barrier((own_out, attended))
+    heads = pl.pallas_call(
+        heads_kernel,
+        out_shape=jax.ShapeDtypeStruct((cores * SIZE["x"], SIZE["h"], rows, HEAD_DIM), bf16),
+        in_specs=[VMEM] * 2,
+        out_specs=VMEM,
+        compiler_params=options,
+        name="heads",
+    )(attended, partner(attended, "h", 1))
+    heads = lax.all_to_all(heads, ("c", "x"), split_axis=0, concat_axis=0, tiled=True)
     core = lax.axis_index("c")
     near_rows = lax.dynamic_index_in_dim(packed, core, axis=0, keepdims=False)
     far_rows = lax.dynamic_slice(

time: 173 us -> 180 us (1.040)
  the two profiles are of different devices: /device:TPU:1 before, /device:TPU:65 now
where the time goes in v9:
time: 180 us; the launch traced here: 179 us
  starting transfers between devices  73.6 us (41%)
  waiting for transfers between devices  53.6 us (30%)
  between operations  13.7 us (8%)
  Pallas kernels  12.4 us (7%)
  blocking collectives  11.2 us (6%)
  local copies, waits for them, and re-layouts  9.77 us (5%)
  other arithmetic  4.53 us (3%)
    ppermute x13, starting transfers between devices, partner(): return lax.ppermute(value, axis, [(i, i ^ bit) for i in range(SIZE[axis])])  61.3 us
    ppermute x13, waiting for transfers between devices, partner(): return lax.ppermute(value, axis, [(i, i ^ bit) for i in range(SIZE[axis])])  25.4 us
    all_gather x1, waiting for transfers between devices, on_device(): library = lax.all_gather(held, 'z', axis=0, tiled=True)  12.9 us
    all_to_all x1, waiting for transfers between devices, on_device(): lax.all_to_all(heads, ('c', 'x'), split_axis=0, concat_axis=0, tiled=True)  12.8 us
    all_gather x1, blocking collectives, on_device(): own_full = lax.all_gather(packed, 'x', axis=0)  11.2 us
    all_to_all x1, starting transfers between devices, on_device(): lax.all_to_all(heads, ('c', 'x'), split_axis=0, concat_axis=0, tiled=True)  6.54 us
    pallas_call x1, Pallas kernels, on_device(): pl.pallas_call(functools.partial(attention_kernel, query_len=query_len, p...  5.77 us
    unnamed x16, local copies, waits for them, and re-layouts  5.71 us
  transfers between devices with their start and end apart: 18, of which 12 were waited for; matrix products, arithmetic and copies ran while one was open for 3% of the time, Pallas kernels for 2%

profile of v9, /device:TPU:65, one launch (start us, length us, event | category | flops | bytes accessed | tf_op | source)
XLA Modules:
  0.0 178.8 jit_solution(2542748651388833382)
XLA Ops:
  7.6 2.6 %collective-permute-start = (bf16[200,256]{1,0:T(8,128)(2,1)S(1)}, bf16[200,256]{1,0:T(8,128)(2,1)S(1)}, u32[]{:S(2)}, u32[]{:S(2)}) collective-permute-start(bf16[200,256]{1,0:T(8,128)(2,1)S(1)} %broadcast_select_fusion), channel_id=1, source_target_pairs={{0,8},{8,0},{1,9},{9,1},{2,10},{10,2},{3,11},{11,3},{4,12},{12,4},... | collective-permute-start | bytes 307208 | tf_op jit(solution)/shard_map/ppermute | solution.py:169
  17.7 2.4 %collective-permute-done.1 = bf16[64,256]{1,0:T(8,128)(2,1)S(1)} collective-permute-done((bf16[64,256]{1,0:T(8,128)(2,1)}, bf16[64,256]{1,0:T(8,128)(2,1)S(1)}, u32[]{:S(2)}, u32[]{:S(2)}) %collective-permute-start.1) | collective-permute-done | bytes 32800 | tf_op jit(solution)/shard_map/ppermute | solution.py:237
  20.1 3.4 %collective-permute-start.2 = (bf16[72,512]{1,0:T(8,128)(2,1)S(1)}, bf16[72,512]{1,0:T(8,128)(2,1)S(1)}, u32[]{:S(2)}, u32[]{:S(2)}) collective-permute-start(bf16[72,512]{1,0:T(8,128)(2,1)S(1)} %select_bitcast_fusion.2), channel_id=1, source_target_pairs={{0,8},{8,0},{1,9},{9,1},{2,10},{10,2},{3,11},{11,3},{4,12},{12,4},... | collective-permute-start | bytes 221192 | tf_op jit(solution)/shard_map/ppermute | solution.py:169
  24.5 4.2 %collective-permute-start.4 = (bf16[2,72,512]{2,1,0:T(8,128)(2,1)S(1)}, bf16[2,72,512]{2,1,0:T(8,128)(2,1)S(1)}, u32[]{:S(2)}, u32[]{:S(2)}) collective-permute-start(bf16[2,72,512]{2,1,0:T(8,128)(2,1)S(1)} %get-tuple-element.34), channel_id=1, source_target_pairs={{0,32},{16,48},{32,0},{48,16},{1,33},{17,49},{33,1},{49,17},{2,34}... | collective-permute-start | bytes 442376 | tf_op jit(solution)/shard_map/ppermute | solution.py:169
  28.7 3.2 %collective-permute-start.3 = (bf16[2,72,512]{2,1,0:T(8,128)(2,1)S(1)}, bf16[2,72,512]{2,1,0:T(8,128)(2,1)S(1)}, u32[]{:S(2)}, u32[]{:S(2)}) collective-permute-start(bf16[2,72,512]{2,1,0:T(8,128)(2,1)S(1)} %get-tuple-element.34), channel_id=1, source_target_pairs={{0,16},{16,0},{32,48},{48,32},{1,17},{17,1},{33,49},{49,33},{2,18}... | collective-permute-start | bytes 442376 | tf_op jit(solution)/shard_map/ppermute | solution.py:169
  33.8 2.3 %collective-permute-done.4 = bf16[2,72,512]{2,1,0:T(8,128)(2,1)S(1)} collective-permute-done((bf16[2,72,512]{2,1,0:T(8,128)(2,1)S(1)}, bf16[2,72,512]{2,1,0:T(8,128)(2,1)S(1)}, u32[]{:S(2)}, u32[]{:S(2)}) %collective-permute-start.4) | collective-permute-done | bytes 147488 | tf_op jit(solution)/shard_map/ppermute | solution.py:169
  37.3 2.8 %collective-permute-done.5 = bf16[2,72,512]{2,1,0:T(8,128)(2,1)S(1)} collective-permute-done((bf16[2,72,512]{2,1,0:T(8,128)(2,1)S(1)}, bf16[2,72,512]{2,1,0:T(8,128)(2,1)S(1)}, u32[]{:S(2)}, u32[]{:S(2)}) %collective-permute-start.5) | collective-permute-done | bytes 147488 | tf_op jit(solution)/shard_map/ppermute | solution.py:169
  42.6 12.9 %all-gather.4.cloned.1.call-done.library_ref = bf16[128,24,256]{2,1,0:T(8,128)(2,1)} async-done(((bf16[16,24,256]{2,1,0:T(8,128)(2,1)}), bf16[128,24,256]{2,1,0:T(8,128)(2,1)}) %all-gather.4.cloned.1.call-update) | async-done | bytes 1572880 | tf_op jit(solution)/shard_map/all_gather | solution.py:232
  57.6 2.9 %collective-permute-start.6 = (bf16[16,24,256]{2,1,0:T(8,128)(2,1)S(1)}, bf16[16,24,256]{2,1,0:T(8,128)(2,1)S(1)}, u32[]{:S(2)}, u32[]{:S(2)}) collective-permute-start(bf16[16,24,256]{2,1,0:T(8,128)(2,1)S(1)} %get-tuple-element.20), channel_id=1, source_target_pairs={{0,16},{16,0},{32,48},{48,32},{1,17},{17,1},{33,49},{49,33},{2,18}... | collective-permute-start | bytes 589832 | tf_op jit(solution)/shard_map/ppermute | solution.py:169
  60.5 4.0 %collective-permute-start.7 = (bf16[16,24,256]{2,1,0:T(8,128)(2,1)S(1)}, bf16[16,24,256]{2,1,0:T(8,128)(2,1)S(1)}, u32[]{:S(2)}, u32[]{:S(2)}) collective-permute-start(bf16[16,24,256]{2,1,0:T(8,128)(2,1)S(1)} %get-tuple-element.21), channel_id=1, source_target_pairs={{0,32},{16,48},{32,0},{48,16},{1,33},{17,49},{33,1},{49,17},{2,34}... | collective-permute-start | bytes 589832 | tf_op jit(solution)/shard_map/ppermute | solution.py:169
  64.5 2.3 %collective-permute-start.8 = (bf16[16,24,256]{2,1,0:T(8,128)(2,1)S(1)}, bf16[16,24,256]{2,1,0:T(8,128)(2,1)S(1)}, u32[]{:S(2)}, u32[]{:S(2)}) collective-permute-start(bf16[16,24,256]{2,1,0:T(8,128)(2,1)S(1)} %get-tuple-element.22), channel_id=1, source_target_pairs={{0,48},{16,32},{32,16},{48,0},{1,49},{17,33},{33,17},{49,1},{2,50}... | collective-permute-start | bytes 589832 | tf_op jit(solution)/shard_map/ppermute | solution.py:169
  67.6 2.4 %collective-permute-done.7.refs_2_ = bf16[16,24,256]{2,1,0:T(8,128)(2,1)S(1)} collective-permute-done((bf16[16,24,256]{2,1,0:T(8,128)(2,1)S(1)}, bf16[16,24,256]{2,1,0:T(8,128)(2,1)S(1)}, u32[]{:S(2)}, u32[]{:S(2)}) %collective-permute-start.7) | collective-permute-done | bytes 196640 | tf_op jit(solution)/shard_map/ppermute | solution.py:169
  70.0 4.6 %collective-permute-done.8.refs_3_ = bf16[16,24,256]{2,1,0:T(8,128)(2,1)S(1)} collective-permute-done((bf16[16,24,256]{2,1,0:T(8,128)(2,1)S(1)}, bf16[16,24,256]{2,1,0:T(8,128)(2,1)S(1)}, u32[]{:S(2)}, u32[]{:S(2)}) %collective-permute-start.8) | collective-permute-done | bytes 196640 | tf_op jit(solution)/shard_map/ppermute | solution.py:169
  75.3 5.4 %collective-permute-start.9 = (bf16[2,208,256]{2,1,0:T(8,128)(2,1)S(1)}, bf16[2,208,256]{2,1,0:T(8,128)(2,1)S(1)}, u32[]{:S(2)}, u32[]{:S(2)}) collective-permute-start(bf16[2,208,256]{2,1,0:T(8,128)(2,1)S(1)} %pack.1), channel_id=1, source_target_pairs={{0,4},{4,0},{1,5},{5,1},{2,6},{6,2},{3,7},{7,3},{8,12},{12,8},{9,1... | collective-permute-start | bytes 638984 | tf_op jit(solution)/shard_map/ppermute | solution.py:169
  80.7 11.2 %all-gather = bf16[8,208,256]{2,1,0:T(8,128)(2,1)S(1)} all-gather(bf16[2,208,256]{2,1,0:T(8,128)(2,1)S(1)} %pack.1), channel_id=2, replica_groups=mesh['z'=8,'y'=4,'c'=2,'h'=2,'x'=4] {'x'}, dimensions={0}, use_global_device_ids=true | all-gather | bytes 1064960 | tf_op jit(solution)/shard_map/all_gather | solution.py:280
  92.8 3.5 %all-to-all-start = ((bf16[4,2,208,256]{3,2,1,0:T(8,128)(2,1)}), bf16[4,2,208,256]{3,2,1,0:T(8,128)(2,1)S(1)}, u32[]{:S(2)}, u32[]{:S(2)}) async-start(bf16[4,2,208,256]{3,2,1,0:T(8,128)(2,1)} %spread.1), calls=%async_computation | async-start | bytes 1703936 | tf_op jit(solution)/shard_map/all_to_all | solution.py:291
  96.3 17.3 %collective-permute-start.10 = (bf16[4,2,208,256]{3,2,1,0:T(8,128)(2,1)S(1)}, bf16[4,2,208,256]{3,2,1,0:T(8,128)(2,1)S(1)}, u32[]{:S(2)}, u32[]{:S(2)}) collective-permute-start(bf16[4,2,208,256]{3,2,1,0:T(8,128)(2,1)S(1)} %bitcast.47), channel_id=1, source_target_pairs={{0,8},{8,0},{1,9},{9,1},{2,10},{10,2},{3,11},{11,3},{4,12},{12,4},... | collective-permute-start | bytes 2555912 | tf_op jit(solution)/shard_map/ppermute | solution.py:169
  113.6 9.8 %collective-permute-start.11 = (bf16[4,2,208,256]{3,2,1,0:T(8,128)(2,1)S(1)}, bf16[4,2,208,256]{3,2,1,0:T(8,128)(2,1)S(1)}, u32[]{:S(2)}, u32[]{:S(2)}) collective-permute-start(bf16[4,2,208,256]{3,2,1,0:T(8,128)(2,1)S(1)} %all-to-all-done.far_ref), channel_id=1, source_target_pairs={{0,8},{8,0},{1,9},{9,1},{2,10},{10,2},{3,11},{11,3},{4,12},{12,4},... | collective-permute-start | bytes 2555912 | tf_op jit(solution)/shard_map/ppermute | solution.py:169
  129.7 5.8 %attention.1 = (bf16[2,208,128]{2,1,0:T(8,128)(2,1)S(1)}, bf16[4096,128]{1,0:T(8,128)(2,1)}) custom-call(s32[16]{0:T(128)S(1)} %gather_fusion.1, bf16[4,2,208,256]{3,2,1,0:T(8,128)(2,1)S(1)} %bitcast.48, bf16[4,2,208,256]{3,2,1,0:T(8,128)(2,1)S(1)} %all-to-all-done.far_ref, bf16[4,2,208,256]{3,2,1,0:T(8,128)(2,1)S(1)} %collective-permute-done.10.own_swap_ref, ...), custom_call_target="tpu_custom_call" | custom-call | flops 1308622848 | bytes 8388608 | tf_op jit(solution)/shard_map/attention/pallas_call | solution.py:301
  135.5 2.3 %collective-permute-start.13 = (bf16[4096,128]{1,0:T(8,128)(2,1)}, bf16[4096,128]{1,0:T(8,128)(2,1)}, u32[]{:S(2)}, u32[]{:S(2)}) collective-permute-start(bf16[4096,128]{1,0:T(8,128)(2,1)} %get-tuple-element.26.own_ref), channel_id=1, source_target_pairs={{0,8},{8,0},{1,9},{9,1},{2,10},{10,2},{3,11},{11,3},{4,12},{12,4},... | collective-permute-start | bytes 3145736 | tf_op jit(solution)/shard_map/ppermute | solution.py:169
  139.7 8.5 %collective-permute-done.12.far_ref = bf16[2,208,128]{2,1,0:T(8,128)(2,1)S(1)} collective-permute-done((bf16[2,208,128]{2,1,0:T(8,128)(2,1)S(1)}, bf16[2,208,128]{2,1,0:T(8,128)(2,1)S(1)}, u32[]{:S(2)}, u32[]{:S(2)}) %collective-permute-start.12) | collective-permute-done | bytes 106528 | tf_op jit(solution)/shard_map/ppermute | solution.py:169
  149.2 6.5 %all-to-all-start.1 = ((bf16[8,2,208,128]{3,2,1,0:T(8,128)(2,1)}), bf16[8,2,208,128]{3,2,1,0:T(8,128)(2,1)S(1)}, u32[]{:S(2)}, u32[]{:S(2)}) async-start(bf16[8,2,208,128]{3,2,1,0:T(8,128)(2,1)} %heads.1), calls=%async_computation.1 | async-start | bytes 1703936 | tf_op jit(solution)/shard_map/all_to_all | solution.py:336
  155.8 12.8 %all-to-all-done.1.heads_ref = bf16[8,2,208,128]{3,2,1,0:T(8,128)(2,1)S(1)} async-done(((bf16[8,2,208,128]{3,2,1,0:T(8,128)(2,1)}), bf16[8,2,208,128]{3,2,1,0:T(8,128)(2,1)S(1)}, u32[]{:S(2)}, u32[]{:S(2)}) %all-to-all-start.1) | async-done | bytes 852000 | tf_op jit(solution)/shard_map/all_to_all | solution.py:336
  168.6 3.3 %output.1 = bf16[256,512]{1,0:T(8,128)(2,1)} custom-call(bf16[8,2,208,128]{3,2,1,0:T(8,128)(2,1)S(1)} %all-to-all-done.1.heads_ref, bf16[4096,128]{1,0:T(8,128)(2,1)} %get-tuple-element.26.own_ref, bf16[4096,128]{1,0:T(8,128)(2,1)} %collective-permute-done.13.other_ref, bf16[208,256]{1,0:T(8,128)(2,1)S(1)} %dynamic-slice_bitcast_fusion.1.near_ref, ...), custom_call_target="tpu_custom_call" | custom-call | flops 436207616 | bytes 3145728 | tf_op jit(solution)/shard_map/output/pallas_call | solution.py:343
  (74 shorter events, 28.7 us)
Async XLA Ops:
  6.5 60.4 %copy-start = (s32[512]{0:T(512)S(1)}, s32[512]{0:T(512)}, u32[]{:S(2)}) copy-start(s32[512]{0:T(512)} %param.12) | copy-start | bytes 6148
  6.5 35.2 %copy-start.7 = (bf16[512]{0:T(512)(128)(2,1)S(1)}, bf16[512]{0:T(512)(128)(2,1)}, u32[]{:S(2)}) copy-start(bf16[512]{0:T(512)(128)(2,1)} %param.15) | copy-start | bytes 3076
  6.5 49.0 %all-gather.4.cloned.1.call-start = ((), (), s32[]{:S(2)}) async-start(), calls=%async_computation.2 | async-start | bytes 1769472 | tf_op jit(solution)/shard_map/all_gather | solution.py:232
  7.6 3.5 %collective-permute-start = (bf16[200,256]{1,0:T(8,128)(2,1)S(1)}, bf16[200,256]{1,0:T(8,128)(2,1)S(1)}, u32[]{:S(2)}, u32[]{:S(2)}) collective-permute-start(bf16[200,256]{1,0:T(8,128)(2,1)S(1)} %broadcast_select_fusion), channel_id=1, source_target_pairs={{0,8},{8,0},{1,9},{9,1},{2,10},{10,2},{3,11},{11,3},{4,12},{12,4},... | collective-permute-start | bytes 307208 | tf_op jit(solution)/shard_map/ppermute | solution.py:169
  12.9 113.4 %all-gather.6.cloned.1.call-start = ((), (), s32[]{:S(2)}) async-start(), calls=%async_computation.3 | async-start | bytes 4718592 | tf_op jit(solution)/shard_map/all_gather | solution.py:248
  14.3 5.8 %collective-permute-start.1 = (bf16[64,256]{1,0:T(8,128)(2,1)}, bf16[64,256]{1,0:T(8,128)(2,1)S(1)}, u32[]{:S(2)}, u32[]{:S(2)}) collective-permute-start(bf16[64,256]{1,0:T(8,128)(2,1)} %bitcast.61), channel_id=1, source_target_pairs={{0,0},{1,64},{2,128},{3,192},{4,256},{5,320},{6,384},{7,448},{8,8}... | collective-permute-start | bytes 98312 | tf_op jit(solution)/shard_map/ppermute | solution.py:237
  20.1 4.3 %collective-permute-start.2 = (bf16[72,512]{1,0:T(8,128)(2,1)S(1)}, bf16[72,512]{1,0:T(8,128)(2,1)S(1)}, u32[]{:S(2)}, u32[]{:S(2)}) collective-permute-start(bf16[72,512]{1,0:T(8,128)(2,1)S(1)} %select_bitcast_fusion.2), channel_id=1, source_target_pairs={{0,8},{8,0},{1,9},{9,1},{2,10},{10,2},{3,11},{11,3},{4,12},{12,4},... | collective-permute-start | bytes 221192 | tf_op jit(solution)/shard_map/ppermute | solution.py:169
  24.5 11.7 %collective-permute-start.4 = (bf16[2,72,512]{2,1,0:T(8,128)(2,1)S(1)}, bf16[2,72,512]{2,1,0:T(8,128)(2,1)S(1)}, u32[]{:S(2)}, u32[]{:S(2)}) collective-permute-start(bf16[2,72,512]{2,1,0:T(8,128)(2,1)S(1)} %get-tuple-element.34), channel_id=1, source_target_pairs={{0,32},{16,48},{32,0},{48,16},{1,33},{17,49},{33,1},{49,17},{2,34}... | collective-permute-start | bytes 442376 | tf_op jit(solution)/shard_map/ppermute | solution.py:169
  28.7 8.6 %collective-permute-start.3 = (bf16[2,72,512]{2,1,0:T(8,128)(2,1)S(1)}, bf16[2,72,512]{2,1,0:T(8,128)(2,1)S(1)}, u32[]{:S(2)}, u32[]{:S(2)}) collective-permute-start(bf16[2,72,512]{2,1,0:T(8,128)(2,1)S(1)} %get-tuple-element.34), channel_id=1, source_target_pairs={{0,16},{16,0},{32,48},{48,32},{1,17},{17,1},{33,49},{49,33},{2,18}... | collective-permute-start | bytes 442376 | tf_op jit(solution)/shard_map/ppermute | solution.py:169
  31.9 8.2 %collective-permute-start.5 = (bf16[2,72,512]{2,1,0:T(8,128)(2,1)S(1)}, bf16[2,72,512]{2,1,0:T(8,128)(2,1)S(1)}, u32[]{:S(2)}, u32[]{:S(2)}) collective-permute-start(bf16[2,72,512]{2,1,0:T(8,128)(2,1)S(1)} %get-tuple-element.34), channel_id=1, source_target_pairs={{0,48},{16,32},{32,16},{48,0},{1,49},{17,33},{33,17},{49,1},{2,50}... | collective-permute-start | bytes 442376 | tf_op jit(solution)/shard_map/ppermute | solution.py:169
  40.8 85.6 %copy-start.5 = (f32[208,128]{1,0:T(8,128)S(1)}, f32[208,128]{1,0:T(8,128)}, u32[]{:S(2)}) copy-start(f32[208,128]{1,0:T(8,128)} %constant.81.clone.sin_ref) | copy-start | bytes 319492
  40.8 85.6 %copy-start.6 = (f32[208,128]{1,0:T(8,128)S(1)}, f32[208,128]{1,0:T(8,128)}, u32[]{:S(2)}) copy-start(f32[208,128]{1,0:T(8,128)} %constant.80.clone.cos_ref) | copy-start | bytes 319492
  55.5 1.4 copy-start.2
  57.6 10.1 %collective-permute-start.6 = (bf16[16,24,256]{2,1,0:T(8,128)(2,1)S(1)}, bf16[16,24,256]{2,1,0:T(8,128)(2,1)S(1)}, u32[]{:S(2)}, u32[]{:S(2)}) collective-permute-start(bf16[16,24,256]{2,1,0:T(8,128)(2,1)S(1)} %get-tuple-element.20), channel_id=1, source_target_pairs={{0,16},{16,0},{32,48},{48,32},{1,17},{17,1},{33,49},{49,33},{2,18}... | collective-permute-start | bytes 589832 | tf_op jit(solution)/shard_map/ppermute | solution.py:169
  60.5 9.5 %collective-permute-start.7 = (bf16[16,24,256]{2,1,0:T(8,128)(2,1)S(1)}, bf16[16,24,256]{2,1,0:T(8,128)(2,1)S(1)}, u32[]{:S(2)}, u32[]{:S(2)}) collective-permute-start(bf16[16,24,256]{2,1,0:T(8,128)(2,1)S(1)} %get-tuple-element.21), channel_id=1, source_target_pairs={{0,32},{16,48},{32,0},{48,16},{1,33},{17,49},{33,1},{49,17},{2,34}... | collective-permute-start | bytes 589832 | tf_op jit(solution)/shard_map/ppermute | solution.py:169
  64.5 10.1 %collective-permute-start.8 = (bf16[16,24,256]{2,1,0:T(8,128)(2,1)S(1)}, bf16[16,24,256]{2,1,0:T(8,128)(2,1)S(1)}, u32[]{:S(2)}, u32[]{:S(2)}) collective-permute-start(bf16[16,24,256]{2,1,0:T(8,128)(2,1)S(1)} %get-tuple-element.22), channel_id=1, source_target_pairs={{0,48},{16,32},{32,16},{48,0},{1,49},{17,33},{33,17},{49,1},{2,50}... | collective-permute-start | bytes 589832 | tf_op jit(solution)/shard_map/ppermute | solution.py:169
  75.3 16.6 %collective-permute-start.9 = (bf16[2,208,256]{2,1,0:T(8,128)(2,1)S(1)}, bf16[2,208,256]{2,1,0:T(8,128)(2,1)S(1)}, u32[]{:S(2)}, u32[]{:S(2)}) collective-permute-start(bf16[2,208,256]{2,1,0:T(8,128)(2,1)S(1)} %pack.1), channel_id=1, source_target_pairs={{0,4},{4,0},{1,5},{5,1},{2,6},{6,2},{3,7},{7,3},{8,12},{12,8},{9,1... | collective-permute-start | bytes 638984 | tf_op jit(solution)/shard_map/ppermute | solution.py:169
  92.8 20.8 %all-to-all-start = ((bf16[4,2,208,256]{3,2,1,0:T(8,128)(2,1)}), bf16[4,2,208,256]{3,2,1,0:T(8,128)(2,1)S(1)}, u32[]{:S(2)}, u32[]{:S(2)}) async-start(bf16[4,2,208,256]{3,2,1,0:T(8,128)(2,1)} %spread.1), calls=%async_computation | async-start | bytes 1703936 | tf_op jit(solution)/shard_map/all_to_all | solution.py:291
  96.3 27.1 %collective-permute-start.10 = (bf16[4,2,208,256]{3,2,1,0:T(8,128)(2,1)S(1)}, bf16[4,2,208,256]{3,2,1,0:T(8,128)(2,1)S(1)}, u32[]{:S(2)}, u32[]{:S(2)}) collective-permute-start(bf16[4,2,208,256]{3,2,1,0:T(8,128)(2,1)S(1)} %bitcast.47), channel_id=1, source_target_pairs={{0,8},{8,0},{1,9},{9,1},{2,10},{10,2},{3,11},{11,3},{4,12},{12,4},... | collective-permute-start | bytes 2555912 | tf_op jit(solution)/shard_map/ppermute | solution.py:169
  113.6 11.8 %collective-permute-start.11 = (bf16[4,2,208,256]{3,2,1,0:T(8,128)(2,1)S(1)}, bf16[4,2,208,256]{3,2,1,0:T(8,128)(2,1)S(1)}, u32[]{:S(2)}, u32[]{:S(2)}) collective-permute-start(bf16[4,2,208,256]{3,2,1,0:T(8,128)(2,1)S(1)} %all-to-all-done.far_ref), channel_id=1, source_target_pairs={{0,8},{8,0},{1,9},{9,1},{2,10},{10,2},{3,11},{11,3},{4,12},{12,4},... | collective-permute-start | bytes 2555912 | tf_op jit(solution)/shard_map/ppermute | solution.py:169
  126.4 2.2 %copy-start.1 = (bf16[4096,512]{1,0:T(8,128)(2,1)S(1)}, bf16[4096,512]{1,0:T(8,128)(2,1)}, u32[]{:S(2)}) copy-start(bf16[4096,512]{1,0:T(8,128)(2,1)} %all-gather.6.cloned.1.call-done.weight_ref) | copy-start | bytes 12582916
  135.5 33.1 %collective-permute-start.13 = (bf16[4096,128]{1,0:T(8,128)(2,1)}, bf16[4096,128]{1,0:T(8,128)(2,1)}, u32[]{:S(2)}, u32[]{:S(2)}) collective-permute-start(bf16[4096,128]{1,0:T(8,128)(2,1)} %get-tuple-element.26.own_ref), channel_id=1, source_target_pairs={{0,8},{8,0},{1,9},{9,1},{2,10},{10,2},{3,11},{11,3},{4,12},{12,4},... | collective-permute-start | bytes 3145736 | tf_op jit(solution)/shard_map/ppermute | solution.py:169
  137.8 10.4 %collective-permute-start.12 = (bf16[2,208,128]{2,1,0:T(8,128)(2,1)S(1)}, bf16[2,208,128]{2,1,0:T(8,128)(2,1)S(1)}, u32[]{:S(2)}, u32[]{:S(2)}) collective-permute-start(bf16[2,208,128]{2,1,0:T(8,128)(2,1)S(1)} %get-tuple-element.25.own_ref), channel_id=1, source_target_pairs={{0,4},{4,0},{1,5},{5,1},{2,6},{6,2},{3,7},{7,3},{8,12},{12,8},{9,1... | collective-permute-start | bytes 319496 | tf_op jit(solution)/shard_map/ppermute | solution.py:169
  149.2 19.4 %all-to-all-start.1 = ((bf16[8,2,208,128]{3,2,1,0:T(8,128)(2,1)}), bf16[8,2,208,128]{3,2,1,0:T(8,128)(2,1)S(1)}, u32[]{:S(2)}, u32[]{:S(2)}) async-start(bf16[8,2,208,128]{3,2,1,0:T(8,128)(2,1)} %heads.1), calls=%async_computation.1 | async-start | bytes 1703936 | tf_op jit(solution)/shard_map/all_to_all | solution.py:336
  (2 other events, 2.1 us)
Sparse Core Ops, SparseCore 0:
  13.0 42.4 all-gather.3
  57.6 58.6 all-gather.5
